TPU v7x, 32 devices: a whole 2x2x4 slice. The times are simulated.
32 devices in a mesh: group: 1, wide: 16 (over z, y, x), narrow: 2 (over core).
Axes of the slice: x: 2, y: 2, z: 4, core: 2. Of those that a mesh axis runs over, the one named last changes fastest.
Arguments:
- tokens: bfloat16 [256, 7168], P(('group', 'wide', 'narrow')), may hold values from -6 to 6
- expert_ids: int32 [256, 8], P(('group', 'wide', 'narrow')), may hold values from 0 to 15, all different within a row; in each aligned block of 8 rows (0 to 7, 8 to 15, ...) at most 8 rows name the same one
- gate_weights: float32 [256, 8], P(('group', 'wide', 'narrow')), may hold values from 0.05 to 0.3
- w_gate: bfloat16 [32, 7168, 512], P(('wide', 'narrow')), may hold values from -0.0625 to 0.0625
- w_up: bfloat16 [32, 7168, 512], P(('wide', 'narrow')), may hold values from -0.0625 to 0.0625
- w_down: bfloat16 [32, 512, 7168], P(('wide', 'narrow')), may hold values from -0.1875 to 0.1875
Outputs:
- mixed: bfloat16 [256, 7168], P(('group', 'wide', 'narrow'))
Inputs may be any that keep to these rules, and one draw needn't show every extreme that they name: `expert_ids`: each token names 8 different experts. Among the 8 tokens of one device no expert is named by more than 8 tokens, and in every draw some expert is named by exactly 8 tokens of some device.
All inputs are finite; a program needn't handle non-finite values.
Results may differ from a plain program's by a relative error of at most 0.0058.
Values may be sent and summed in bfloat16 or wider, within the bound.
No kernel may reach another device: no remote copies, remote signals or barrier semaphores. Data moves between devices by JAX's collectives and lax.ppermute only.
A program may use at most 128 MiB of HBM per device.

v0:
```python
import jax
import jax.numpy as jnp
from jax import lax
from jax.sharding import PartitionSpec as P

FF = 1024


def run_slice(rows, gate_mat, up_mat, down_mat):
    gate = jnp.dot(rows, gate_mat, preferred_element_type=jnp.float32)
    up = jnp.dot(rows, up_mat, preferred_element_type=jnp.float32)
    hidden = (jax.nn.silu(gate) * up).astype(jnp.bfloat16)
    return jnp.dot(hidden, down_mat, preferred_element_type=jnp.float32).astype(jnp.bfloat16)


def body(tokens, expert_ids, gate_weights, w_gate, w_up, w_down):
    n_wide = lax.axis_size("wide")
    n_narrow = lax.axis_size("narrow")
    n_devices = n_wide * n_narrow
    slices = FF // w_gate.shape[2]
    experts = n_devices // slices
    tok_rows, width = tokens.shape
    chosen = expert_ids.shape[1]
    capacity = min(tok_rows, max(2, 2 * tok_rows * chosen // experts))
    routed = tok_rows * chosen
    flat_ids = expert_ids.reshape(routed)
    onehot = (flat_ids[:, None] == jnp.arange(experts, dtype=jnp.int32)[None, :]).astype(jnp.int32)
    ranks = jnp.sum(jnp.cumsum(onehot, 0) * onehot, 1) - 1
    slots = flat_ids * capacity + ranks
    copies = jnp.broadcast_to(tokens[:, None, :], (tok_rows, chosen, width)).reshape(routed, width)
    expert_rows = jnp.zeros((experts * capacity, width), tokens.dtype).at[slots].set(copies)
    expert_rows = expert_rows.reshape(experts, capacity, width)
    outgoing = jnp.repeat(expert_rows, slices, axis=0)
    arrived = lax.all_to_all(outgoing, ("wide", "narrow"), split_axis=0, concat_axis=0, tiled=True)
    results = run_slice(arrived.reshape(n_devices * capacity, width), w_gate[0], w_up[0], w_down[0])
    returned = lax.all_to_all(
        results.reshape(n_devices, capacity, width),
        ("wide", "narrow"),
        split_axis=0,
        concat_axis=0,
        tiled=True,
    )
    pieces = returned.reshape(experts, slices, capacity, width).astype(jnp.float32)
    summed = jnp.sum(pieces, 1).reshape(experts * capacity, width)
    picked = summed[slots].reshape(tok_rows, chosen, width)
    mixed = jnp.sum(picked * gate_weights[:, :, None], 1)
    return mixed.astype(jnp.bfloat16)


def solution(mesh):
    in_specs = (
        P(("group", "wide", "narrow"), None),
        P(("group", "wide", "narrow"), None),
        P(("group", "wide", "narrow"), None),
        P(("wide", "narrow"), None, None),
        P(("wide", "narrow"), None, None),
        P(("wide", "narrow"), None, None),
    )
    out_specs = P(("group", "wide", "narrow"), None)
    return jax.shard_map(body, mesh=mesh, in_specs=in_specs, out_specs=out_specs, check_vma=False)
```

profile of v0, /device:TPU:0, one launch (start us, length us, event | category | flops | bytes accessed | tf_op | source)
XLA Modules:
  0.0 210.5 jit_solution(8561175023350929752)
XLA Ops:
  0.0 0.0 copy-start
  0.0 0.8 eq.15
  0.8 0.7 broadcast_multiply_fusion
  1.5 0.1 fusion.33
  1.6 0.1 reduce_window_sum.11
  1.7 0.2 select_reduce_fusion
  1.8 0.1 mul.36
  1.9 0.0 copy-done
  1.9 2.4 %scatter_custom_fusion = bf16[128,7168]{1,0:T(8,128)(2,1)S(1)} fusion(s32[64]{0:T(128)S(1)} %fusion.34, bf16[]{:T(256)} %constant.7.clone.1, bf16[8,7168]{1,0:T(8,128)(2,1)S(1)} %copy-done), kind=kCustom, calls=%fused_computation.16 | custom fusion | bytes 1949698 | tf_op jit(solution)/shard_map/scatter | solution.py:31
  4.4 0.4 broadcast_in_dim.8
  4.8 90.1 %all_to_all.10 = bf16[32,8,7168]{2,1,0:T(8,128)(2,1)S(1)} all-to-all(bf16[32,8,7168]{2,1,0:T(8,128)(2,1)S(1)} %bitcast.48), channel_id=1, replica_groups=mesh['group'=1,'wide'=16,'narrow'=2] {'wide','narrow'}, dimensions={0} | all-to-all | bytes 7340032 | tf_op jit(solution)/shard_map/all_to_all | solution.py:34
  94.9 0.0 copy-start.1
  94.9 1.8 copy-done.1
  96.7 5.2 %fusion.4 = f32[256,512]{1,0:T(8,128)S(1)} fusion(bf16[1,7168,512]{2,1,0:T(8,128)(2,1)} %param.9, bf16[32,8,7168]{2,1,0:T(8,128)(2,1)S(1)} %all_to_all.10), kind=kOutput, calls=%fused_computation.8 | convolution fusion | flops 1879048192 | bytes 11534336 | tf_op jit(solution)/shard_map/dot_general | solution.py:10
  101.9 12.1 %fusion = bf16[32,8,7168]{2,1,0:T(8,128)(2,1)} fusion(bf16[1,512,7168]{2,1,0:T(8,128)(2,1)} %param.11, bf16[1,7168,512]{2,1,0:T(8,128)(2,1)} %param.10, bf16[32,8,7168]{2,1,0:T(8,128)(2,1)} %copy-done.1, f32[256,512]{1,0:T(8,128)S(1)} %fusion.4), kind=kOutput, calls=%fused_computation.3 | convolution fusion | flops 3760717824 | bytes 22544384 | tf_op jit(solution)/shard_map/dot_general | solution.py:13
  114.0 3.5 %all-to-all-start.1 = ((bf16[32,8,7168]{2,1,0:T(8,128)(2,1)}), bf16[32,8,7168]{2,1,0:T(8,128)(2,1)}, u32[]{:S(2)}, u32[]{:S(2)}) async-start(bf16[32,8,7168]{2,1,0:T(8,128)(2,1)} %fusion), calls=%async_computation.1 | async-start | bytes 7340032 | tf_op jit(solution)/shard_map/all_to_all | solution.py:36
  117.6 82.7 %all-to-all-done.1 = bf16[32,8,7168]{2,1,0:T(8,128)(2,1)} async-done(((bf16[32,8,7168]{2,1,0:T(8,128)(2,1)}), bf16[32,8,7168]{2,1,0:T(8,128)(2,1)}, u32[]{:S(2)}, u32[]{:S(2)}) %all-to-all-start.1) | async-done | bytes 3670048 | tf_op jit(solution)/shard_map/all_to_all | solution.py:36
  200.3 4.9 %convert_reduce_fusion = f32[16,8,7168]{2,1,0:T(8,128)} fusion(bf16[32,8,7168]{2,1,0:T(8,128)(2,1)} %all-to-all-done.1), kind=kLoop, calls=%fused_computation.4 | loop fusion | flops 2752512 | bytes 7340032 | tf_op jit(solution)/shard_map/reduce_sum | solution.py:44
  205.2 0.0 copy-start.2
  205.2 4.0 %gather_fusion = f32[64,7168]{1,0:T(8,128)S(1)} fusion(f32[128,7168]{1,0:T(8,128)} %bitcast.47, s32[1024]{0:T(1024)S(1)} %pad_clamp_fusion), kind=kCustom, calls=%fused_computation | custom fusion | bytes 3670272 | tf_op jit(solution)/shard_map/gather | solution.py:45
  209.3 0.0 copy-done.2
  209.3 1.2 fusion.8
  (2 shorter events, 0.0 us)
Async XLA Ops:
  0.0 1.9 copy-start
  94.9 1.8 copy-start.1
  114.0 86.3 %all-to-all-start.1 = ((bf16[32,8,7168]{2,1,0:T(8,128)(2,1)}), bf16[32,8,7168]{2,1,0:T(8,128)(2,1)}, u32[]{:S(2)}, u32[]{:S(2)}) async-start(bf16[32,8,7168]{2,1,0:T(8,128)(2,1)} %fusion), calls=%async_computation.1 | async-start | bytes 7340032 | tf_op jit(solution)/shard_map/all_to_all | solution.py:36
  205.2 4.0 %copy-start.2 = (f32[8,8]{1,0:T(8,128)S(1)}, f32[8,8]{1,0:T(8,128)}, u32[]{:S(2)}) copy-start(f32[8,8]{1,0:T(8,128)} %param.8) | copy-start | bytes 772
where the time goes:
time: 211 us
  blocking collectives  90.1 us (43%)
  waiting for transfers between devices  82.7 us (39%)
  matrix products  17.4 us (8%)
  local copies, waits for them, and re-layouts  9.56 us (5%)
  other arithmetic  7.19 us (3%)
  starting transfers between devices  3.54 us (2%)
    all_to_all x1, blocking collectives, body(): lax.all_to_all(outgoing, ('wide', 'narrow'), split_axis=0, concat_axis=0,...  90.1 us
    all_to_all x1, waiting for transfers between devices, body(): lax.all_to_all(results.reshape(n_devices, capacity, width), ('wide', 'nar...  82.7 us
    dot_general x1, matrix products, run_slice(): jnp.dot(hidden, down_mat, preferred_element_type=jnp.float32)  12.1 us
    dot_general x1, matrix products, run_slice(): gate = jnp.dot(rows, gate_mat, preferred_element_type=jnp.float32)  5.22 us
    reduce_sum x1, other arithmetic, body(): summed = jnp.sum(pieces, 1).reshape(experts * capacity, width)  4.9 us
  transfers between devices with their start and end apart: 1, of which 1 were waited for; matrix products, arithmetic and copies ran while one was open for 0% of the time, Pallas kernels for 0%

commit v1 on v0

v1 whole, which is shorter than its diff:
```python
import jax
import jax.numpy as jnp
from jax import lax
from jax.sharding import PartitionSpec as P

FF = 1024
AXES = ("wide", "narrow")
LANES = 128
F32 = jnp.float32
BF16 = jnp.bfloat16


def exchanges(n_wide, n_narrow):
    n = n_wide * n_narrow
    inner = min(4, n_wide)
    steps = []
    stride = inner * n_narrow
    rest = n_wide // inner
    while rest > 1:
        radix = min(4, rest)
        steps.append([[(i, i ^ (k * stride)) for i in range(n)] for k in range(1, radix)])
        stride *= radix
        rest //= radix
    if inner == 4:
        a, b = n_narrow, 2 * n_narrow
        steps.append([[(i, i ^ (a if i % n_narrow == 0 else b)) for i in range(n)]])
        steps.append([[(i, i ^ (b if i % n_narrow == 0 else a)) for i in range(n)]])
    elif inner == 2:
        steps.append([[(i, i ^ n_narrow) for i in range(n)]])
    if n_narrow == 2:
        steps.append([[(i, i ^ 1) for i in range(n)]])
    return steps


def gather(block, steps):
    for step in steps:
        block = jnp.concatenate([block] + [lax.ppermute(block, AXES, p) for p in step], 0)
    return block


def scatter_sum(share, steps):
    for step in reversed(steps):
        rows = share.shape[0] // (len(step) + 1)
        got = [lax.ppermute(share[(k + 1) * rows:(k + 2) * rows].astype(BF16), AXES, p) for k, p in enumerate(step)]
        share = share[:rows]
        for g in got:
            share = share + g.astype(F32)
    return share


def split3(v):
    high = lax.reduce_precision(v, 8, 7)
    mid = lax.reduce_precision(v - high, 8, 7)
    low = lax.reduce_precision(v - high - mid, 8, 7)
    return [high, mid, low]


def body(tokens, expert_ids, gate_weights, w_gate, w_up, w_down):
    n_wide = lax.axis_size("wide")
    n_narrow = lax.axis_size("narrow")
    slices = FF // w_gate.shape[2]
    experts = n_wide * n_narrow // slices
    expert = lax.axis_index(AXES) // slices
    rows, width = tokens.shape
    steps = exchanges(n_wide, n_narrow)

    named = expert_ids[:, :, None] == jnp.arange(experts, dtype=jnp.int32)[None, None, :]
    table = jnp.sum(jnp.where(named, gate_weights[:, :, None], 0.0), 1)
    extra = jnp.concatenate(split3(table) + [jnp.zeros((rows, LANES - 3 * experts), F32)], 1).astype(BF16)
    sent = jnp.concatenate([tokens, extra], 1)

    cut = width // 2 // LANES * LANES
    first = gather(sent[:, :cut], steps)
    second = gather(sent[:, cut:], steps)
    lane = jnp.arange(LANES, dtype=jnp.int32)
    mine = (lane % experts == expert) & (lane < 3 * experts)
    scale = jnp.sum(jnp.where(mine[None, :], second[:, width - cut:].astype(F32), 0.0), 1, keepdims=True)
    second = second[:, :width - cut]

    def dot(a, b):
        return jnp.dot(a, b, preferred_element_type=F32)

    gate = dot(first, w_gate[0, :cut]) + dot(second, w_gate[0, cut:])
    up = dot(first, w_up[0, :cut]) + dot(second, w_up[0, cut:])
    hidden = (jax.nn.silu(gate) * up).astype(BF16)
    outs = []
    for a, b in ((0, cut), (cut, width)):
        share = dot(hidden, w_down[0, :, a:b]) * scale
        outs.append(scatter_sum(share, steps).astype(BF16))
    return jnp.concatenate(outs, 1)


def solution(mesh):
    in_specs = (
        P(("group", "wide", "narrow"), None),
        P(("group", "wide", "narrow"), None),
        P(("group", "wide", "narrow"), None),
        P(("wide", "narrow"), None, None),
        P(("wide", "narrow"), None, None),
        P(("wide", "narrow"), None, None),
    )
    out_specs = P(("group", "wide", "narrow"), None)
    return jax.shard_map(body, mesh=mesh, in_specs=in_specs, out_specs=out_specs, check_vma=False)
```

time: 211 us -> 89.5 us (0.42)
  blocking collectives: 90.1 us -> 0 us
  waiting for transfers between devices: 82.7 us -> 31 us
  starting transfers between devices: 3.54 us -> 30.6 us
  matrix products: 17.4 us -> 12.3 us
  other arithmetic: 7.19 us -> 3.77 us
    all_to_all x1 -> x0, blocking collectives: 90.1 us -> none  [body(): lax.all_to_all(outgoing, ('wide', 'narrow'), split_axis=0, concat_axis=0,...]
    all_to_all x1 -> x0, waiting for transfers between devices: 82.7 us -> none  [body(): lax.all_to_all(results.reshape(n_devices, capacity, width), ('wide', 'nar...]
    ppermute x0 -> x24, waiting for transfers between devices: none -> 31 us  [the longest x12 18.1 us: scatter_sum(): lax.ppermute(share[(k + 1) * rows:(k + 2) * rows].astype(BF16), AXES, p)]
    ppermute x0 -> x24, starting transfers between devices: none -> 30.6 us  [the longest x12 16.8 us: gather(): lax.ppermute(block, AXES, p)]
    dot_general x2 -> x6, matrix products: 17.4 us -> 12.3 us  [dot(): return jnp.dot(a, b, preferred_element_type=F32)]
    unnamed x6 -> x28, local copies, waits for them, and re-layouts: 1.8 us -> 6.78 us
    concatenate x0 -> x5, local copies, waits for them, and re-layouts: none -> 4.1 us  [the longest x4 3.11 us: gather(): jnp.concatenate([block] + [lax.ppermute(block, AXES, p) for p in step], 0)]
    gather x1 -> x0, local copies, waits for them, and re-layouts: 4.03 us -> none  [body(): picked = summed[slots].reshape(tok_rows, chosen, width)]
  transfers between devices with their start and end apart: 1 -> 24, of which waited for: 1 -> 12; matrix products, arithmetic and copies ran while one was open for 0% -> 10% of each run, Pallas kernels for 0% -> 0%
where the time goes in v1:
time: 89.5 us; the launch traced here: 89.2 us
  waiting for transfers between devices  31 us (35%)
  starting transfers between devices  30.6 us (34%)
  matrix products  12.3 us (14%)
  local copies, waits for them, and re-layouts  11.2 us (13%)
  other arithmetic  3.77 us (4%)
    ppermute x12, waiting for transfers between devices, scatter_sum(): lax.ppermute(share[(k + 1) * rows:(k + 2) * rows].astype(BF16), AXES, p)  18.1 us
    ppermute x12, starting transfers between devices, gather(): lax.ppermute(block, AXES, p)  16.8 us
    ppermute x12, starting transfers between devices, scatter_sum(): lax.ppermute(share[(k + 1) * rows:(k + 2) * rows].astype(BF16), AXES, p)  13.8 us
    ppermute x12, waiting for transfers between devices, gather(): lax.ppermute(block, AXES, p)  12.8 us
    dot_general x6, matrix products, dot(): return jnp.dot(a, b, preferred_element_type=F32)  12.3 us
    unnamed x28, local copies, waits for them, and re-layouts  6.78 us
    concatenate x4, local copies, waits for them, and re-layouts, gather(): jnp.concatenate([block] + [lax.ppermute(block, AXES, p) for p in step], 0)  3.11 us
  transfers between devices with their start and end apart: 24, of which 12 were waited for; matrix products, arithmetic and copies ran while one was open for 10% of the time, Pallas kernels for 0%

profile of v1, /device:TPU:0, one launch (start us, length us, event | category | flops | bytes accessed | tf_op | source)
XLA Modules:
  0.0 89.2 jit_solution(7852066437494204599)
XLA Ops:
  0.0 1.5 %constant_dynamic-update-slice_fusion.10 = (bf16[128,3584]{1,0:T(8,128)(2,1)}, bf16[64,3584]{1,0:T(8,128)(2,1)S(1)}, bf16[256,3584]{1,0:T(8,128)(2,1)}, bf16[8,3584]{1,0:T(8,128)(2,1)S(1)}) fusion(bf16[8,7168]{1,0:T(8,128)(2,1)} %param.6), kind=kLoop, calls=%fused_computation.57 | loop fusion | bytes 286720
  1.5 5.0 %collective-permute-start.2 = (bf16[8,3584]{1,0:T(8,128)(2,1)S(1)}, bf16[8,3584]{1,0:T(8,128)(2,1)S(1)}, u32[]{:S(2)}, u32[]{:S(2)}) collective-permute-start(bf16[8,3584]{1,0:T(8,128)(2,1)S(1)} %get-tuple-element.32), channel_id=1, source_target_pairs={{0,24},{1,25},{2,26},{3,27},{4,28},{5,29},{6,30},{7,31},{8,16},{9,... | collective-permute-start | bytes 172040 | tf_op jit(solution)/shard_map/ppermute | solution.py:37
  8.9 3.9 %collective-permute-start.8 = (bf16[8,3712]{1,0:T(8,128)(2,1)S(1)}, bf16[8,3712]{1,0:T(8,128)(2,1)S(1)}, u32[]{:S(2)}, u32[]{:S(2)}) collective-permute-start(bf16[8,3712]{1,0:T(8,128)(2,1)S(1)} %get-tuple-element.28), channel_id=1, source_target_pairs={{0,24},{1,25},{2,26},{3,27},{4,28},{5,29},{6,30},{7,31},{8,16},{9,... | collective-permute-start | bytes 178184 | tf_op jit(solution)/shard_map/ppermute | solution.py:37
  13.5 1.7 %collective-permute-start.3 = (bf16[32,3584]{1,0:T(8,128)(2,1)S(1)}, bf16[32,3584]{1,0:T(8,128)(2,1)S(1)}, u32[]{:S(2)}, u32[]{:S(2)}) collective-permute-start(bf16[32,3584]{1,0:T(8,128)(2,1)S(1)} %pad_maximum_fusion.1), channel_id=1, source_target_pairs={{0,2},{1,5},{2,0},{3,7},{4,6},{5,1},{6,4},{7,3},{8,10},{9,13},{10,... | collective-permute-start | bytes 688136 | tf_op jit(solution)/shard_map/ppermute | solution.py:37
  17.9 1.6 %collective-permute-start.9 = (bf16[32,3712]{1,0:T(8,128)(2,1)S(1)}, bf16[32,3712]{1,0:T(8,128)(2,1)S(1)}, u32[]{:S(2)}, u32[]{:S(2)}) collective-permute-start(bf16[32,3712]{1,0:T(8,128)(2,1)S(1)} %pad_maximum_fusion), channel_id=1, source_target_pairs={{0,2},{1,5},{2,0},{3,7},{4,6},{5,1},{6,4},{7,3},{8,10},{9,13},{10,... | collective-permute-start | bytes 712712 | tf_op jit(solution)/shard_map/ppermute | solution.py:37
  20.5 1.6 %collective-permute-start.4 = (bf16[64,3584]{1,0:T(8,128)(2,1)S(1)}, bf16[64,3584]{1,0:T(8,128)(2,1)S(1)}, u32[]{:S(2)}, u32[]{:S(2)}) collective-permute-start(bf16[64,3584]{1,0:T(8,128)(2,1)S(1)} %get-tuple-element.24), channel_id=1, source_target_pairs={{0,4},{1,3},{2,6},{3,1},{4,0},{5,7},{6,2},{7,5},{8,12},{9,11},{10,... | collective-permute-start | bytes 1376264 | tf_op jit(solution)/shard_map/ppermute | solution.py:37
  22.1 4.6 %collective-permute-done.9 = bf16[32,3712]{1,0:T(8,128)(2,1)S(1)} collective-permute-done((bf16[32,3712]{1,0:T(8,128)(2,1)S(1)}, bf16[32,3712]{1,0:T(8,128)(2,1)S(1)}, u32[]{:S(2)}, u32[]{:S(2)}) %collective-permute-start.9) | collective-permute-done | bytes 237600 | tf_op jit(solution)/shard_map/ppermute | solution.py:37
  26.7 1.6 %collective-permute-start.10 = (bf16[64,3712]{1,0:T(8,128)(2,1)S(1)}, bf16[64,3712]{1,0:T(8,128)(2,1)S(1)}, u32[]{:S(2)}, u32[]{:S(2)}) collective-permute-start(bf16[64,3712]{1,0:T(8,128)(2,1)S(1)} %get-tuple-element.15), channel_id=1, source_target_pairs={{0,4},{1,3},{2,6},{3,1},{4,0},{5,7},{6,2},{7,5},{8,12},{9,11},{10,... | collective-permute-start | bytes 1425416 | tf_op jit(solution)/shard_map/ppermute | solution.py:37
  28.9 1.0 %constant_dynamic-update-slice_fusion.5 = (bf16[128,3584]{1,0:T(8,128)(2,1)}, bf16[256,3584]{1,0:T(8,128)(2,1)}) fusion(bf16[128,3584]{1,0:T(8,128)(2,1)} %get-tuple-element.22, bf16[64,3584]{1,0:T(8,128)(2,1)S(1)} %collective-permute-done.4, bf16[256,3584]{1,0:T(8,128)(2,1)} %get-tuple-element.23), kind=kLoop, calls=%fused_computation.52 | loop fusion | bytes 1376256 | tf_op jit(solution)/shard_map/concatenate | solution.py:37
  30.1 5.4 %collective-permute-done.10 = bf16[64,3712]{1,0:T(8,128)(2,1)S(1)} collective-permute-done((bf16[64,3712]{1,0:T(8,128)(2,1)S(1)}, bf16[64,3712]{1,0:T(8,128)(2,1)S(1)}, u32[]{:S(2)}, u32[]{:S(2)}) %collective-permute-start.10) | collective-permute-done | bytes 475168 | tf_op jit(solution)/shard_map/ppermute | solution.py:37
  35.6 1.3 %copy-done = bf16[256,3712]{1,0:T(8,128)(2,1)} copy-done((bf16[256,3712]{1,0:T(8,128)(2,1)}, bf16[256,3712]{1,0:T(8,128)(2,1)S(1)}, u32[]{:S(2)}) %copy-start) | copy-done | bytes 1900568
  36.9 1.0 %constant_dynamic-update-slice_fusion.11 = bf16[256,3584]{1,0:T(8,128)(2,1)} fusion(bf16[256,3584]{1,0:T(8,128)(2,1)} %get-tuple-element.12, bf16[128,3584]{1,0:T(8,128)(2,1)S(1)} %collective-permute-done.5), kind=kLoop, calls=%fused_computation.58 | loop fusion | bytes 1835008 | tf_op jit(solution)/shard_map/concatenate | solution.py:37
  37.9 1.5 %collective-permute-done.11 = bf16[128,3712]{1,0:T(8,128)(2,1)S(1)} collective-permute-done((bf16[128,3712]{1,0:T(8,128)(2,1)S(1)}, bf16[128,3712]{1,0:T(8,128)(2,1)S(1)}, u32[]{:S(2)}, u32[]{:S(2)}) %collective-permute-start.11) | collective-permute-done | bytes 950304 | tf_op jit(solution)/shard_map/ppermute | solution.py:37
  39.4 1.0 %constant_dynamic-update-slice_fusion.29 = bf16[256,3712]{1,0:T(8,128)(2,1)} fusion(bf16[256,3712]{1,0:T(8,128)(2,1)} %copy-done, bf16[128,3712]{1,0:T(8,128)(2,1)S(1)} %collective-permute-done.11), kind=kLoop, calls=%fused_computation.76 | loop fusion | bytes 1900544 | tf_op jit(solution)/shard_map/concatenate | solution.py:37
  40.4 1.5 %select_reduce_fusion = f32[256]{0:T(256)S(1)} fusion(bf16[256,3712]{1,0:T(8,128)(2,1)} %constant_dynamic-update-slice_fusion.29, pred[128]{0:T(512)(128)(4,1)S(1)} %compare_and_fusion), kind=kLoop, calls=%fused_computation.37 | loop fusion | flops 98048 | bytes 66688 | tf_op jit(solution)/shard_map/reduce_sum | solution.py:77
  42.0 3.8 %fusion.2 = f32[256,512]{1,0:T(8,128)S(1)} fusion(bf16[1,7168,512]{2,1,0:T(8,128)(2,1)} %param.10, bf16[256,3712]{1,0:T(8,128)(2,1)} %constant_dynamic-update-slice_fusion.29), kind=kOutput, calls=%fused_computation.4 | convolution fusion | flops 939524096 | bytes 6029312 | tf_op jit(solution)/shard_map/dot_general | solution.py:81
  45.9 3.9 %fusion.6 = f32[256,512]{1,0:T(8,128)S(1)} fusion(bf16[1,7168,512]{2,1,0:T(8,128)(2,1)} %param.9, bf16[256,3712]{1,0:T(8,128)(2,1)S(1)} %copy-done.1), kind=kOutput, calls=%fused_computation.8 | convolution fusion | flops 939524096 | bytes 6029312 | tf_op jit(solution)/shard_map/dot_general | solution.py:81
  49.8 1.1 %fusion.18 = f32[256,512]{1,0:T(8,128)S(1)} fusion(f32[256,512]{1,0:T(8,128)S(1)} %fusion.6, bf16[256,3584]{1,0:T(8,128)(2,1)S(1)} %copy-done.2, bf16[1,7168,512]{2,1,0:T(8,128)(2,1)S(1)} %bitcast.31), kind=kOutput, calls=%fused_computation.24 | convolution fusion | flops 939655168 | bytes 6553600 | tf_op jit(solution)/shard_map/dot_general | solution.py:81
  50.9 1.2 %multiply_convert_fusion = bf16[256,512]{1,0:T(8,128)(2,1)S(1)} fusion(f32[256,512]{1,0:T(8,128)S(1)} %fusion.18, f32[256,512]{1,0:T(8,128)S(1)} %fusion.2, bf16[256,3584]{1,0:T(8,128)(2,1)S(1)} %copy-done.2, bf16[1,7168,512]{2,1,0:T(8,128)(2,1)S(1)} %bitcast.33), kind=kOutput, calls=%fused_computation.30 | convolution fusion | flops 940441600 | bytes 6815744 | tf_op jit(solution)/shard_map/dot_general | solution.py:81
  52.1 1.0 %slice-done.1 = s8[3145728]{0:T(1024)(128)(4,1)S(1)} async-done(((s8[7340032]{0:T(1024)(128)(4,1)}), s8[3145728]{0:T(1024)(128)(4,1)S(1)}, s32[]{:S(2)}) %slice-start.1) | async-done | bytes 3145752
  53.1 1.2 %convolution_multiply_fusion = f32[256,3584]{1,0:T(8,128)S(1)} fusion(bf16[256,512]{1,0:T(8,128)(2,1)S(1)} %multiply_convert_fusion, bf16[1,512,7168]{2,1,0:T(8,128)(2,1)S(1)} %bitcast.29, f32[256]{0:T(256)S(1)} %select_reduce_fusion), kind=kOutput, calls=%fused_computation | convolution fusion | flops 940441600 | bytes 7603200 | tf_op jit(solution)/shard_map/dot_general | solution.py:81
  54.6 1.2 %convolution_multiply_fusion.1 = f32[256,3584]{1,0:T(8,128)S(1)} fusion(bf16[256,512]{1,0:T(8,128)(2,1)S(1)} %multiply_convert_fusion, bf16[1,512,7168]{2,1,0:T(8,128)(2,1)S(1)} %bitcast.29, f32[256]{0:T(256)S(1)} %select_reduce_fusion), kind=kOutput, calls=%fused_computation.1 | convolution fusion | flops 940441600 | bytes 7603200 | tf_op jit(solution)/shard_map/dot_general | solution.py:81
  57.1 1.6 %collective-permute-start.19 = (bf16[64,3584]{1,0:T(8,128)(2,1)S(1)}, bf16[64,3584]{1,0:T(8,128)(2,1)S(1)}, u32[]{:S(2)}, u32[]{:S(2)}) collective-permute-start(bf16[64,3584]{1,0:T(8,128)(2,1)S(1)} %slice.222), channel_id=1, source_target_pairs={{0,4},{1,3},{2,6},{3,1},{4,0},{5,7},{6,2},{7,5},{8,12},{9,11},{10,... | collective-permute-start | bytes 1376264 | tf_op jit(solution)/shard_map/ppermute | solution.py:44
  59.0 1.2 %collective-permute-start.13 = (bf16[64,3584]{1,0:T(8,128)(2,1)S(1)}, bf16[64,3584]{1,0:T(8,128)(2,1)S(1)}, u32[]{:S(2)}, u32[]{:S(2)}) collective-permute-start(bf16[64,3584]{1,0:T(8,128)(2,1)S(1)} %slice.223), channel_id=1, source_target_pairs={{0,4},{1,3},{2,6},{3,1},{4,0},{5,7},{6,2},{7,5},{8,12},{9,11},{10,... | collective-permute-start | bytes 1376264 | tf_op jit(solution)/shard_map/ppermute | solution.py:44
  60.3 5.4 %collective-permute-done.19 = bf16[64,3584]{1,0:T(8,128)(2,1)S(1)} collective-permute-done((bf16[64,3584]{1,0:T(8,128)(2,1)S(1)}, bf16[64,3584]{1,0:T(8,128)(2,1)S(1)}, u32[]{:S(2)}, u32[]{:S(2)}) %collective-permute-start.19) | collective-permute-done | bytes 458784 | tf_op jit(solution)/shard_map/ppermute | solution.py:44
  65.8 1.6 %collective-permute-start.20 = (bf16[32,3584]{1,0:T(8,128)(2,1)S(1)}, bf16[32,3584]{1,0:T(8,128)(2,1)S(1)}, u32[]{:S(2)}, u32[]{:S(2)}) collective-permute-start(bf16[32,3584]{1,0:T(8,128)(2,1)S(1)} %slice.224), channel_id=1, source_target_pairs={{0,2},{1,5},{2,0},{3,7},{4,6},{5,1},{6,4},{7,3},{8,10},{9,13},{10,... | collective-permute-start | bytes 688136 | tf_op jit(solution)/shard_map/ppermute | solution.py:44
  67.4 5.7 %collective-permute-done.13 = bf16[64,3584]{1,0:T(8,128)(2,1)S(1)} collective-permute-done((bf16[64,3584]{1,0:T(8,128)(2,1)S(1)}, bf16[64,3584]{1,0:T(8,128)(2,1)S(1)}, u32[]{:S(2)}, u32[]{:S(2)}) %collective-permute-start.13) | collective-permute-done | bytes 458784 | tf_op jit(solution)/shard_map/ppermute | solution.py:44
  73.3 1.6 %collective-permute-start.14 = (bf16[32,3584]{1,0:T(8,128)(2,1)S(1)}, bf16[32,3584]{1,0:T(8,128)(2,1)S(1)}, u32[]{:S(2)}, u32[]{:S(2)}) collective-permute-start(bf16[32,3584]{1,0:T(8,128)(2,1)S(1)} %slice.225), channel_id=1, source_target_pairs={{0,2},{1,5},{2,0},{3,7},{4,6},{5,1},{6,4},{7,3},{8,10},{9,13},{10,... | collective-permute-start | bytes 688136 | tf_op jit(solution)/shard_map/ppermute | solution.py:44
  75.4 3.0 %collective-permute-start.23 = (bf16[8,3584]{1,0:T(8,128)(2,1)S(1)}, bf16[8,3584]{1,0:T(8,128)(2,1)S(1)}, u32[]{:S(2)}, u32[]{:S(2)}) collective-permute-start(bf16[8,3584]{1,0:T(8,128)(2,1)S(1)} %get-tuple-element.20), channel_id=1, source_target_pairs={{0,24},{1,25},{2,26},{3,27},{4,28},{5,29},{6,30},{7,31},{8,16},{9,... | collective-permute-start | bytes 172040 | tf_op jit(solution)/shard_map/ppermute | solution.py:44
  80.0 3.0 %collective-permute-start.17 = (bf16[8,3584]{1,0:T(8,128)(2,1)S(1)}, bf16[8,3584]{1,0:T(8,128)(2,1)S(1)}, u32[]{:S(2)}, u32[]{:S(2)}) collective-permute-start(bf16[8,3584]{1,0:T(8,128)(2,1)S(1)} %get-tuple-element.17), channel_id=1, source_target_pairs={{0,24},{1,25},{2,26},{3,27},{4,28},{5,29},{6,30},{7,31},{8,16},{9,... | collective-permute-start | bytes 172040 | tf_op jit(solution)/shard_map/ppermute | solution.py:44
  83.0 2.2 %collective-permute-done.22 = bf16[8,3584]{1,0:T(8,128)(2,1)S(1)} collective-permute-done((bf16[8,3584]{1,0:T(8,128)(2,1)S(1)}, bf16[8,3584]{1,0:T(8,128)(2,1)S(1)}, u32[]{:S(2)}, u32[]{:S(2)}) %collective-permute-start.22) | collective-permute-done | bytes 57376 | tf_op jit(solution)/shard_map/ppermute | solution.py:44
  86.1 2.5 %collective-permute-done.16 = bf16[8,3584]{1,0:T(8,128)(2,1)S(1)} collective-permute-done((bf16[8,3584]{1,0:T(8,128)(2,1)S(1)}, bf16[8,3584]{1,0:T(8,128)(2,1)S(1)}, u32[]{:S(2)}, u32[]{:S(2)}) %collective-permute-start.16) | collective-permute-done | bytes 57376 | tf_op jit(solution)/shard_map/ppermute | solution.py:44
  (82 shorter events, 13.5 us)
Async XLA Ops:
  1.5 11.3 %collective-permute-start.2 = (bf16[8,3584]{1,0:T(8,128)(2,1)S(1)}, bf16[8,3584]{1,0:T(8,128)(2,1)S(1)}, u32[]{:S(2)}, u32[]{:S(2)}) collective-permute-start(bf16[8,3584]{1,0:T(8,128)(2,1)S(1)} %get-tuple-element.32), channel_id=1, source_target_pairs={{0,24},{1,25},{2,26},{3,27},{4,28},{5,29},{6,30},{7,31},{8,16},{9,... | collective-permute-start | bytes 172040 | tf_op jit(solution)/shard_map/ppermute | solution.py:37
  6.5 6.9 %collective-permute-start.1 = (bf16[8,3584]{1,0:T(8,128)(2,1)S(1)}, bf16[8,3584]{1,0:T(8,128)(2,1)S(1)}, u32[]{:S(2)}, u32[]{:S(2)}) collective-permute-start(bf16[8,3584]{1,0:T(8,128)(2,1)S(1)} %get-tuple-element.32), channel_id=1, source_target_pairs={{0,16},{1,17},{2,18},{3,19},{4,20},{5,21},{6,22},{7,23},{8,24},{9,... | collective-permute-start | bytes 172040 | tf_op jit(solution)/shard_map/ppermute | solution.py:37
  6.5 6.9 %collective-permute-start = (bf16[8,3584]{1,0:T(8,128)(2,1)S(1)}, bf16[8,3584]{1,0:T(8,128)(2,1)S(1)}, u32[]{:S(2)}, u32[]{:S(2)}) collective-permute-start(bf16[8,3584]{1,0:T(8,128)(2,1)S(1)} %get-tuple-element.32), channel_id=1, source_target_pairs={{0,8},{1,9},{2,10},{3,11},{4,12},{5,13},{6,14},{7,15},{8,0},{9,1},... | collective-permute-start | bytes 172040 | tf_op jit(solution)/shard_map/ppermute | solution.py:37
  8.9 8.2 %collective-permute-start.8 = (bf16[8,3712]{1,0:T(8,128)(2,1)S(1)}, bf16[8,3712]{1,0:T(8,128)(2,1)S(1)}, u32[]{:S(2)}, u32[]{:S(2)}) collective-permute-start(bf16[8,3712]{1,0:T(8,128)(2,1)S(1)} %get-tuple-element.28), channel_id=1, source_target_pairs={{0,24},{1,25},{2,26},{3,27},{4,28},{5,29},{6,30},{7,31},{8,16},{9,... | collective-permute-start | bytes 178184 | tf_op jit(solution)/shard_map/ppermute | solution.py:37
  12.8 5.1 %collective-permute-start.7 = (bf16[8,3712]{1,0:T(8,128)(2,1)S(1)}, bf16[8,3712]{1,0:T(8,128)(2,1)S(1)}, u32[]{:S(2)}, u32[]{:S(2)}) collective-permute-start(bf16[8,3712]{1,0:T(8,128)(2,1)S(1)} %get-tuple-element.28), channel_id=1, source_target_pairs={{0,16},{1,17},{2,18},{3,19},{4,20},{5,21},{6,22},{7,23},{8,24},{9,... | collective-permute-start | bytes 178184 | tf_op jit(solution)/shard_map/ppermute | solution.py:37
  12.8 5.1 %collective-permute-start.6 = (bf16[8,3712]{1,0:T(8,128)(2,1)S(1)}, bf16[8,3712]{1,0:T(8,128)(2,1)S(1)}, u32[]{:S(2)}, u32[]{:S(2)}) collective-permute-start(bf16[8,3712]{1,0:T(8,128)(2,1)S(1)} %get-tuple-element.28), channel_id=1, source_target_pairs={{0,8},{1,9},{2,10},{3,11},{4,12},{5,13},{6,14},{7,15},{8,0},{9,1},... | collective-permute-start | bytes 178184 | tf_op jit(solution)/shard_map/ppermute | solution.py:37
  13.5 6.1 %collective-permute-start.3 = (bf16[32,3584]{1,0:T(8,128)(2,1)S(1)}, bf16[32,3584]{1,0:T(8,128)(2,1)S(1)}, u32[]{:S(2)}, u32[]{:S(2)}) collective-permute-start(bf16[32,3584]{1,0:T(8,128)(2,1)S(1)} %pad_maximum_fusion.1), channel_id=1, source_target_pairs={{0,2},{1,5},{2,0},{3,7},{4,6},{5,1},{6,4},{7,3},{8,10},{9,13},{10,... | collective-permute-start | bytes 688136 | tf_op jit(solution)/shard_map/ppermute | solution.py:37
  17.9 8.7 %collective-permute-start.9 = (bf16[32,3712]{1,0:T(8,128)(2,1)S(1)}, bf16[32,3712]{1,0:T(8,128)(2,1)S(1)}, u32[]{:S(2)}, u32[]{:S(2)}) collective-permute-start(bf16[32,3712]{1,0:T(8,128)(2,1)S(1)} %pad_maximum_fusion), channel_id=1, source_target_pairs={{0,2},{1,5},{2,0},{3,7},{4,6},{5,1},{6,4},{7,3},{8,10},{9,13},{10,... | collective-permute-start | bytes 712712 | tf_op jit(solution)/shard_map/ppermute | solution.py:37
  20.5 8.5 %collective-permute-start.4 = (bf16[64,3584]{1,0:T(8,128)(2,1)S(1)}, bf16[64,3584]{1,0:T(8,128)(2,1)S(1)}, u32[]{:S(2)}, u32[]{:S(2)}) collective-permute-start(bf16[64,3584]{1,0:T(8,128)(2,1)S(1)} %get-tuple-element.24), channel_id=1, source_target_pairs={{0,4},{1,3},{2,6},{3,1},{4,0},{5,7},{6,2},{7,5},{8,12},{9,11},{10,... | collective-permute-start | bytes 1376264 | tf_op jit(solution)/shard_map/ppermute | solution.py:37
  26.7 8.7 %collective-permute-start.10 = (bf16[64,3712]{1,0:T(8,128)(2,1)S(1)}, bf16[64,3712]{1,0:T(8,128)(2,1)S(1)}, u32[]{:S(2)}, u32[]{:S(2)}) collective-permute-start(bf16[64,3712]{1,0:T(8,128)(2,1)S(1)} %get-tuple-element.15), channel_id=1, source_target_pairs={{0,4},{1,3},{2,6},{3,1},{4,0},{5,7},{6,2},{7,5},{8,12},{9,11},{10,... | collective-permute-start | bytes 1425416 | tf_op jit(solution)/shard_map/ppermute | solution.py:37
  29.9 6.9 %collective-permute-start.5 = (bf16[128,3584]{1,0:T(8,128)(2,1)}, bf16[128,3584]{1,0:T(8,128)(2,1)S(1)}, u32[]{:S(2)}, u32[]{:S(2)}) collective-permute-start(bf16[128,3584]{1,0:T(8,128)(2,1)} %get-tuple-element.11), channel_id=1, source_target_pairs={{0,1},{1,0},{2,3},{3,2},{4,5},{5,4},{6,7},{7,6},{8,9},{9,8},{10,11... | collective-permute-start | bytes 2752520 | tf_op jit(solution)/shard_map/ppermute | solution.py:37
  36.9 2.5 %collective-permute-start.11 = (bf16[128,3712]{1,0:T(8,128)(2,1)S(1)}, bf16[128,3712]{1,0:T(8,128)(2,1)S(1)}, u32[]{:S(2)}, u32[]{:S(2)}) collective-permute-start(bf16[128,3712]{1,0:T(8,128)(2,1)S(1)} %get-tuple-element.9), channel_id=1, source_target_pairs={{0,1},{1,0},{2,3},{3,2},{4,5},{5,4},{6,7},{7,6},{8,9},{9,8},{10,11... | collective-permute-start | bytes 2850824 | tf_op jit(solution)/shard_map/ppermute | solution.py:37
  39.4 10.3 %slice-start.2 = ((s8[7340032]{0:T(1024)(128)(4,1)}), s8[4194304]{0:T(1024)(128)(4,1)S(1)}, s32[]{:S(2)}) async-start(s8[7340032]{0:T(1024)(128)(4,1)} %bitcast.30), calls=%async_computation.2 | async-start | bytes 8388608
  41.9 3.9 %copy-start.1 = (bf16[256,3712]{1,0:T(8,128)(2,1)S(1)}, bf16[256,3712]{1,0:T(8,128)(2,1)}, u32[]{:S(2)}) copy-start(bf16[256,3712]{1,0:T(8,128)(2,1)} %constant_dynamic-update-slice_fusion.29) | copy-start | bytes 5701636
  41.9 7.8 %slice-start.3 = ((s8[7340032]{0:T(1024)(128)(4,1)}), s8[3145728]{0:T(1024)(128)(4,1)S(1)}, s32[]{:S(2)}) async-start(s8[7340032]{0:T(1024)(128)(4,1)} %bitcast.30), calls=%async_computation.3 | async-start | bytes 6291456
  42.0 8.9 %slice-start.4 = ((s8[7340032]{0:T(1024)(128)(4,1)}), s8[4194304]{0:T(1024)(128)(4,1)S(1)}, s32[]{:S(2)}) async-start(s8[7340032]{0:T(1024)(128)(4,1)} %bitcast.32), calls=%async_computation.4 | async-start | bytes 8388608
  45.8 3.9 %copy-start.2 = (bf16[256,3584]{1,0:T(8,128)(2,1)S(1)}, bf16[256,3584]{1,0:T(8,128)(2,1)}, u32[]{:S(2)}) copy-start(bf16[256,3584]{1,0:T(8,128)(2,1)} %constant_dynamic-update-slice_fusion.11) | copy-start | bytes 5505028
  45.8 5.1 %slice-start.5 = ((s8[7340032]{0:T(1024)(128)(4,1)}), s8[3145728]{0:T(1024)(128)(4,1)S(1)}, s32[]{:S(2)}) async-start(s8[7340032]{0:T(1024)(128)(4,1)} %bitcast.32), calls=%async_computation.5 | async-start | bytes 6291456
  49.8 2.3 %slice-start = ((s8[7340032]{0:T(1024)(128)(4,1)}), s8[4194304]{0:T(1024)(128)(4,1)S(1)}, s32[]{:S(2)}) async-start(s8[7340032]{0:T(1024)(128)(4,1)} %bitcast.28), calls=%async_computation | async-start | bytes 8388608
  50.9 2.2 %slice-start.1 = ((s8[7340032]{0:T(1024)(128)(4,1)}), s8[3145728]{0:T(1024)(128)(4,1)S(1)}, s32[]{:S(2)}) async-start(s8[7340032]{0:T(1024)(128)(4,1)} %bitcast.28), calls=%async_computation.1 | async-start | bytes 6291456
  54.4 2.5 %collective-permute-start.18 = (bf16[128,3584]{1,0:T(8,128)(2,1)S(1)}, bf16[128,3584]{1,0:T(8,128)(2,1)S(1)}, u32[]{:S(2)}, u32[]{:S(2)}) collective-permute-start(bf16[128,3584]{1,0:T(8,128)(2,1)S(1)} %slice.220), channel_id=1, source_target_pairs={{0,1},{1,0},{2,3},{3,2},{4,5},{5,4},{6,7},{7,6},{8,9},{9,8},{10,11... | collective-permute-start | bytes 2752520 | tf_op jit(solution)/shard_map/ppermute | solution.py:44
  55.8 2.9 %collective-permute-start.12 = (bf16[128,3584]{1,0:T(8,128)(2,1)S(1)}, bf16[128,3584]{1,0:T(8,128)(2,1)S(1)}, u32[]{:S(2)}, u32[]{:S(2)}) collective-permute-start(bf16[128,3584]{1,0:T(8,128)(2,1)S(1)} %slice.221), channel_id=1, source_target_pairs={{0,1},{1,0},{2,3},{3,2},{4,5},{5,4},{6,7},{7,6},{8,9},{9,8},{10,11... | collective-permute-start | bytes 2752520 | tf_op jit(solution)/shard_map/ppermute | solution.py:44
  57.1 8.5 %collective-permute-start.19 = (bf16[64,3584]{1,0:T(8,128)(2,1)S(1)}, bf16[64,3584]{1,0:T(8,128)(2,1)S(1)}, u32[]{:S(2)}, u32[]{:S(2)}) collective-permute-start(bf16[64,3584]{1,0:T(8,128)(2,1)S(1)} %slice.222), channel_id=1, source_target_pairs={{0,4},{1,3},{2,6},{3,1},{4,0},{5,7},{6,2},{7,5},{8,12},{9,11},{10,... | collective-permute-start | bytes 1376264 | tf_op jit(solution)/shard_map/ppermute | solution.py:44
  59.0 14.1 %collective-permute-start.13 = (bf16[64,3584]{1,0:T(8,128)(2,1)S(1)}, bf16[64,3584]{1,0:T(8,128)(2,1)S(1)}, u32[]{:S(2)}, u32[]{:S(2)}) collective-permute-start(bf16[64,3584]{1,0:T(8,128)(2,1)S(1)} %slice.223), channel_id=1, source_target_pairs={{0,4},{1,3},{2,6},{3,1},{4,0},{5,7},{6,2},{7,5},{8,12},{9,11},{10,... | collective-permute-start | bytes 1376264 | tf_op jit(solution)/shard_map/ppermute | solution.py:44
  65.8 9.0 %collective-permute-start.20 = (bf16[32,3584]{1,0:T(8,128)(2,1)S(1)}, bf16[32,3584]{1,0:T(8,128)(2,1)S(1)}, u32[]{:S(2)}, u32[]{:S(2)}) collective-permute-start(bf16[32,3584]{1,0:T(8,128)(2,1)S(1)} %slice.224), channel_id=1, source_target_pairs={{0,2},{1,5},{2,0},{3,7},{4,6},{5,1},{6,4},{7,3},{8,10},{9,13},{10,... | collective-permute-start | bytes 688136 | tf_op jit(solution)/shard_map/ppermute | solution.py:44
  73.3 6.1 %collective-permute-start.14 = (bf16[32,3584]{1,0:T(8,128)(2,1)S(1)}, bf16[32,3584]{1,0:T(8,128)(2,1)S(1)}, u32[]{:S(2)}, u32[]{:S(2)}) collective-permute-start(bf16[32,3584]{1,0:T(8,128)(2,1)S(1)} %slice.225), channel_id=1, source_target_pairs={{0,2},{1,5},{2,0},{3,7},{4,6},{5,1},{6,4},{7,3},{8,10},{9,13},{10,... | collective-permute-start | bytes 688136 | tf_op jit(solution)/shard_map/ppermute | solution.py:44
  74.9 8.0 %collective-permute-start.21 = (bf16[8,3584]{1,0:T(8,128)(2,1)S(1)}, bf16[8,3584]{1,0:T(8,128)(2,1)S(1)}, u32[]{:S(2)}, u32[]{:S(2)}) collective-permute-start(bf16[8,3584]{1,0:T(8,128)(2,1)S(1)} %get-tuple-element.19), channel_id=1, source_target_pairs={{0,8},{1,9},{2,10},{3,11},{4,12},{5,13},{6,14},{7,15},{8,0},{9,1},... | collective-permute-start | bytes 172040 | tf_op jit(solution)/shard_map/ppermute | solution.py:44
  75.4 7.6 %collective-permute-start.23 = (bf16[8,3584]{1,0:T(8,128)(2,1)S(1)}, bf16[8,3584]{1,0:T(8,128)(2,1)S(1)}, u32[]{:S(2)}, u32[]{:S(2)}) collective-permute-start(bf16[8,3584]{1,0:T(8,128)(2,1)S(1)} %get-tuple-element.20), channel_id=1, source_target_pairs={{0,24},{1,25},{2,26},{3,27},{4,28},{5,29},{6,30},{7,31},{8,16},{9,... | collective-permute-start | bytes 172040 | tf_op jit(solution)/shard_map/ppermute | solution.py:44
  78.4 6.8 %collective-permute-start.22 = (bf16[8,3584]{1,0:T(8,128)(2,1)S(1)}, bf16[8,3584]{1,0:T(8,128)(2,1)S(1)}, u32[]{:S(2)}, u32[]{:S(2)}) collective-permute-start(bf16[8,3584]{1,0:T(8,128)(2,1)S(1)} %get-tuple-element.21), channel_id=1, source_target_pairs={{0,16},{1,17},{2,18},{3,19},{4,20},{5,21},{6,22},{7,23},{8,24},{9,... | collective-permute-start | bytes 172040 | tf_op jit(solution)/shard_map/ppermute | solution.py:44
  79.4 5.8 %collective-permute-start.15 = (bf16[8,3584]{1,0:T(8,128)(2,1)S(1)}, bf16[8,3584]{1,0:T(8,128)(2,1)S(1)}, u32[]{:S(2)}, u32[]{:S(2)}) collective-permute-start(bf16[8,3584]{1,0:T(8,128)(2,1)S(1)} %get-tuple-element.16), channel_id=1, source_target_pairs={{0,8},{1,9},{2,10},{3,11},{4,12},{5,13},{6,14},{7,15},{8,0},{9,1},... | collective-permute-start | bytes 172040 | tf_op jit(solution)/shard_map/ppermute | solution.py:44
  80.0 6.1 %collective-permute-start.17 = (bf16[8,3584]{1,0:T(8,128)(2,1)S(1)}, bf16[8,3584]{1,0:T(8,128)(2,1)S(1)}, u32[]{:S(2)}, u32[]{:S(2)}) collective-permute-start(bf16[8,3584]{1,0:T(8,128)(2,1)S(1)} %get-tuple-element.17), channel_id=1, source_target_pairs={{0,24},{1,25},{2,26},{3,27},{4,28},{5,29},{6,30},{7,31},{8,16},{9,... | collective-permute-start | bytes 172040 | tf_op jit(solution)/shard_map/ppermute | solution.py:44
  82.9 5.6 %collective-permute-start.16 = (bf16[8,3584]{1,0:T(8,128)(2,1)S(1)}, bf16[8,3584]{1,0:T(8,128)(2,1)S(1)}, u32[]{:S(2)}, u32[]{:S(2)}) collective-permute-start(bf16[8,3584]{1,0:T(8,128)(2,1)S(1)} %get-tuple-element.18), channel_id=1, source_target_pairs={{0,16},{1,17},{2,18},{3,19},{4,20},{5,21},{6,22},{7,23},{8,24},{9,... | collective-permute-start | bytes 172040 | tf_op jit(solution)/shard_map/ppermute | solution.py:44
  (1 other events, 1.3 us)

commit v2 on v1

v2 whole, which is shorter than its diff:
```python
import functools

import jax
import jax.numpy as jnp
from jax import lax
from jax.experimental import pallas as pl
from jax.experimental.pallas import tpu as pltpu
from jax.sharding import PartitionSpec as P

FF = 1024
AXES = ("wide", "narrow")
LANES = 128
CUT = 7
DOWN = 7
TIE = 0
F32 = jnp.float32
BF16 = jnp.bfloat16


def exchanges(n_wide):
    n = 2 * n_wide
    steps = []
    stride = 8
    rest = n_wide // 4
    while rest > 1:
        radix = min(4, rest)
        steps.append([[(i, i ^ (k * stride)) for i in range(n)] for k in range(1, radix)])
        stride *= radix
        rest //= radix
    steps.append([[(i, i ^ (2 if i % 2 == 0 else 4)) for i in range(n)]])
    last = [(i, i ^ (4 if i % 2 == 0 else 2)) for i in range(n)]
    core = [(i, i ^ 1) for i in range(n)]
    return steps, last, core


def move(x, perm):
    return lax.ppermute(x, AXES, perm)


def after(x, y):
    return lax.optimization_barrier((x, y))


def gather(block, cut, first_product, plan):
    steps, last, core = plan
    for step in steps[:-2]:
        block = jnp.concatenate([block] + [move(block, p) for p in step], 0)
    blocks = [block] + [move(block, p) for p in steps[-2]]
    one, two = [jnp.concatenate([x[:, at] for x in blocks], 0) for at in (slice(0, cut), slice(cut, None))]
    one, two = [jnp.concatenate([x, move(x, steps[-1][0])], 0) for x in (one, two)]
    other = move(one, last)
    acc = first_product((one, other, move(one, core), move(other, core)))
    other = move(two, last)
    return acc, (two, other, move(two, core), move(other, core))


def scatter_sum(near, near_sent, far, plan):
    steps, last, core = plan
    share = near + move(near_sent, core).astype(F32)
    share = share + move(far, last).astype(F32)
    for step in reversed(steps):
        rows = share.shape[0] // (len(step) + 1)
        got = [move(share[(k + 1) * rows:(k + 2) * rows].astype(BF16), p) for k, p in enumerate(step)]
        share = share[:rows]
        for g in got:
            share = share + g.astype(F32)
    return share


def split3(v):
    high = lax.reduce_precision(v, 8, 7)
    mid = lax.reduce_precision(v - high, 8, 7)
    low = lax.reduce_precision(v - high - mid, 8, 7)
    return [high, mid, low]


def dot(a, b):
    return jnp.dot(a, b, preferred_element_type=F32)


class Stream:
    def __init__(self, groups, ahead):
        self.groups, self.ahead, self.used = groups, ahead, 0
        for group in groups[:ahead]:
            for c in group:
                c.start()

    def wait(self):
        for c in self.groups[self.used]:
            c.wait()
        self.used += 1
        after = self.used + self.ahead - 1
        if after < len(self.groups):
            for c in self.groups[after]:
                c.start()


def up_copies(skip, kb, count, wg, wu, wg_held, wu_held, sems):
    groups = []
    for j in range(count):
        at, to = pl.ds(skip + j * kb, kb), pl.ds(j * kb, kb)
        groups.append([
            pltpu.make_async_copy(wg.at[0, at], wg_held.at[to], sems.at[0, j]),
            pltpu.make_async_copy(wu.at[0, at], wu_held.at[to], sems.at[1, j]),
        ])
    return groups


def down_copies(skip, cb, count, wd, held, sems):
    return [[pltpu.make_async_copy(wd.at[0, :, pl.ds(skip + j * cb, cb)], held.at[j], sems.at[j])] for j in range(count)]


def first_kernel(skip, kb, x0, x1, x2, x3, wg, wu, acc, rows, wg_held, wu_held, sems):
    q, width = x0.shape
    hid = wg.shape[2]
    count = width // kb
    stream = Stream(up_copies(skip, kb, count, wg, wu, wg_held, wu_held, sems), 4)
    for j in range(count):
        for n, x in enumerate((x0, x1, x2, x3)):
            rows[n * q:(n + 1) * q, :] = x[:, j * kb:(j + 1) * kb]
        stream.wait()
        gate = dot(rows[...], wg_held[j * kb:(j + 1) * kb, :])
        up = dot(rows[...], wu_held[j * kb:(j + 1) * kb, :])
        if j == 0:
            acc[:, :hid] = gate
            acc[:, hid:] = up
        else:
            acc[:, :hid] += gate
            acc[:, hid:] += up


def second_kernel(skip, kb, x0, x1, x2, x3, mask, acc, wg, wu, wd, hidden, scale, near, far, near_sent, far_sent,
                  rows, total, wg_held, wu_held, sems, wd_held, wd_sems):
    q = x0.shape[0]
    hid = wg.shape[2]
    width = x0.shape[1] - LANES
    count = width // kb
    stream = Stream(
        up_copies(skip, kb, count, wg, wu, wg_held, wu_held, sems)
        + down_copies(0, kb, near.shape[1] // kb, wd, wd_held, wd_sems),
        5,
    )
    for n, x in enumerate((x0, x1, x2, x3)):
        s = jnp.sum(x[:, width:].astype(F32) * mask[...], 1, keepdims=True)
        scale[n * q:(n + 1) * q, :] = jnp.broadcast_to(s, (q, LANES))
    for j in range(count):
        for n, x in enumerate((x0, x1, x2, x3)):
            rows[n * q:(n + 1) * q, :] = x[:, j * kb:(j + 1) * kb]
        stream.wait()
        held = acc if j == 0 else total
        gate = held[:, :hid] + dot(rows[...], wg_held[j * kb:(j + 1) * kb, :])
        up = held[:, hid:] + dot(rows[...], wu_held[j * kb:(j + 1) * kb, :])
        if j < count - 1:
            total[:, :hid] = gate
            total[:, hid:] = up
        else:
            hidden[...] = (gate / (1 + jnp.exp(-gate)) * up).astype(BF16)
    down_blocks(stream, kb, hidden, scale, wd_held, near, far, near_sent, far_sent)


def down_blocks(stream, cb, hidden, scale, held, near, far, near_sent, far_sent):
    q = near.shape[0]
    for j in range(near.shape[1] // cb):
        at = slice(j * cb, (j + 1) * cb)
        stream.wait()
        share = dot(hidden[...], held[j]) * scale[:, :1]
        near[:, at] = share[:q]
        far[:, at] = share[q:2 * q]
        near_sent[:, at] = share[2 * q:3 * q].astype(BF16)
        far_sent[:, at] = share[3 * q:].astype(BF16)


def down_kernel(skip, cb, hidden, scale, wd, near, far, near_sent, far_sent, held, sems):
    stream = Stream(down_copies(skip, cb, near.shape[1] // cb, wd, held, sems), 99)
    down_blocks(stream, cb, hidden, scale, held, near, far, near_sent, far_sent)


def in_vmem(n):
    return [pl.BlockSpec(memory_space=pltpu.VMEM)] * n


def in_hbm(n):
    return [pl.BlockSpec(memory_space=pltpu.HBM)] * n


def params(mib):
    return pltpu.CompilerParams(vmem_limit_bytes=mib << 20)


def first_part(pieces, w_gate, w_up, width, kb):
    q = pieces[0].shape[0]
    hid = w_gate.shape[2]
    return pl.pallas_call(
        functools.partial(first_kernel, 0, kb),
        in_specs=in_vmem(4) + in_hbm(2),
        out_specs=in_vmem(1)[0],
        out_shape=jax.ShapeDtypeStruct((4 * q, 2 * hid), F32),
        scratch_shapes=[pltpu.VMEM((4 * q, kb), BF16)] + held_up(width, hid, kb),
        compiler_params=params(30),
        cost_estimate=cost(16 * q * width * hid, 4 * width * hid),
    )(*pieces, w_gate, w_up)


def second_part(pieces, mask, acc, w_gate, w_up, w_down, skip, width, first, kb):
    q = pieces[0].shape[0]
    hid = w_gate.shape[2]
    return pl.pallas_call(
        functools.partial(second_kernel, skip, kb),
        in_specs=in_vmem(6) + in_hbm(3),
        out_specs=in_vmem(6),
        out_shape=[jax.ShapeDtypeStruct((4 * q, hid), BF16), jax.ShapeDtypeStruct((4 * q, LANES), F32)] + shares(q, first),
        scratch_shapes=[pltpu.VMEM((4 * q, kb), BF16), pltpu.VMEM((4 * q, 2 * hid), F32)]
        + held_up(width, hid, kb) + held_down(first, hid, kb),
        compiler_params=params(30),
        cost_estimate=cost(16 * q * width * hid + 8 * q * first * hid, 4 * width * hid + 2 * first * hid),
    )(*pieces, mask, acc, w_gate, w_up, w_down)


def down_part(hidden, scale, w_down, skip, width, kb):
    q = hidden.shape[0] // 4
    hid = hidden.shape[1]
    return pl.pallas_call(
        functools.partial(down_kernel, skip, kb),
        in_specs=in_vmem(2) + in_hbm(1),
        out_specs=in_vmem(4),
        out_shape=shares(q, width),
        scratch_shapes=held_down(width, hid, kb),
        compiler_params=params(20),
        cost_estimate=cost(8 * q * width * hid, 2 * width * hid),
    )(hidden, scale, w_down)


def cost(flops, moved):
    return pl.CostEstimate(flops=flops, bytes_accessed=moved, transcendentals=0)


def shares(q, width):
    return [jax.ShapeDtypeStruct((q, width), t) for t in (F32, F32, BF16, BF16)]


def held_up(width, hid, kb):
    return [pltpu.VMEM((width, hid), BF16)] * 2 + [pltpu.SemaphoreType.DMA((2, width // kb))]


def held_down(width, hid, kb):
    return [pltpu.VMEM((width // kb, hid, kb), BF16), pltpu.SemaphoreType.DMA((width // kb,))]


def body(tokens, expert_ids, gate_weights, w_gate, w_up, w_down):
    n_wide = lax.axis_size("wide")
    slices = FF // w_gate.shape[2]
    experts = 2 * n_wide // slices
    expert = lax.axis_index(AXES) // slices
    rows, width = tokens.shape
    plan = exchanges(n_wide)

    named = expert_ids[:, :, None] == jnp.arange(experts, dtype=jnp.int32)[None, None, :]
    table = jnp.sum(jnp.where(named, gate_weights[:, :, None], 0.0), 1)
    extra = jnp.concatenate(split3(table) + [jnp.zeros((rows, LANES - 3 * experts), F32)], 1).astype(BF16)
    lane = jnp.arange(LANES, dtype=jnp.int32)
    mask = ((lane % experts == expert) & (lane < 3 * experts)).astype(F32)[None, :]

    w_gate, w_up, w_down = [pltpu.with_memory_space_constraint(w, pltpu.HBM) for w in (w_gate, w_up, w_down)]
    kb = 512
    cut = CUT * width // kb // 14 * kb
    down = DOWN * width // kb // 14 * kb
    sent = jnp.concatenate([tokens, extra], 1)
    acc, two = gather(sent, cut, lambda one: first_part(one, w_gate, w_up, cut, kb), plan)
    hidden, scale, *pieces = second_part(two, mask, acc, w_gate, w_up, w_down, cut, width - cut, down, kb)
    far = pieces[1] + move(pieces[3], plan[2]).astype(F32)
    far = far.astype(BF16)
    if TIE:
        far, hidden = after(far, hidden)
    out = scatter_sum(pieces[0], pieces[2], far, plan)
    pieces = down_part(hidden, scale, w_down, down, width - down, kb)
    far = pieces[1] + move(pieces[3], plan[2]).astype(F32)
    rest = scatter_sum(pieces[0], pieces[2], far.astype(BF16), plan)
    return jnp.concatenate([out.astype(BF16), rest.astype(BF16)], 1)


def solution(mesh):
    tokens = P(("group", "wide", "narrow"), None)
    weights = P(("wide", "narrow"), None, None)
    return jax.shard_map(body, mesh=mesh, in_specs=(tokens,) * 3 + (weights,) * 3, out_specs=tokens, check_vma=False)
```

time: 89.5 us -> 83.7 us (0.935)
  Pallas kernels: 0 us -> 14.3 us
  matrix products: 12.3 us -> 0 us
  local copies, waits for them, and re-layouts: 11.2 us -> 2.02 us
  waiting for transfers between devices: 31 us -> 38.6 us
  starting transfers between devices: 30.6 us -> 26.1 us
  other arithmetic: 3.77 us -> 2.13 us
    pallas_call x0 -> x3, Pallas kernels: none -> 14.3 us  [the longest x1 6.12 us: second_part(): pl.pallas_call(functools.partial(second_kernel, skip, kb), in_specs=in_vm...]
    dot_general x6 -> x0, matrix products: 12.3 us -> none  [dot(): return jnp.dot(a, b, preferred_element_type=F32)]
    ppermute x24 -> x25, waiting for transfers between devices: 31 us -> 38.6 us  [move(): return lax.ppermute(x, AXES, perm)]
    unnamed x28 -> x0, local copies, waits for them, and re-layouts: 6.78 us -> none
    ppermute x24 -> x25, starting transfers between devices: 30.6 us -> 26.1 us  [move(): return lax.ppermute(x, AXES, perm)]
    concatenate x4 -> x2, local copies, waits for them, and re-layouts: 3.11 us -> 0.04 us  [gather(): jnp.concatenate([x, move(x, steps[-1][0])], 0)]
    reduce_sum x1 -> x0, other arithmetic: 1.53 us -> none  [body(): jnp.sum(jnp.where(mine[None, :], second[:, width - cut:].astype(F32), 0.0...]
    slice x0 -> x8, local copies, waits for them, and re-layouts: none -> 0.91 us  [gather(): x[:, at]]
  transfers between devices with their start and end apart: 24 -> 25, of which waited for: 12 -> 12; matrix products, arithmetic and copies ran while one was open for 10% -> 2% of each run, Pallas kernels for 0% -> 10%
where the time goes in v2:
time: 83.7 us; the launch traced here: 83.5 us
  waiting for transfers between devices  38.6 us (46%)
  starting transfers between devices  26.1 us (31%)
  Pallas kernels  14.3 us (17%)
  other arithmetic  2.13 us (3%)
  local copies, waits for them, and re-layouts  2.02 us (2%)
    ppermute x25, waiting for transfers between devices, move(): return lax.ppermute(x, AXES, perm)  38.6 us
    ppermute x25, starting transfers between devices, move(): return lax.ppermute(x, AXES, perm)  26.1 us
    pallas_call x1, Pallas kernels, second_part(): pl.pallas_call(functools.partial(second_kernel, skip, kb), in_specs=in_vm...  6.12 us
    pallas_call x1, Pallas kernels, first_part(): pl.pallas_call(functools.partial(first_kernel, 0, kb), in_specs=in_vmem(4...  4.96 us
    pallas_call x1, Pallas kernels, down_part(): pl.pallas_call(functools.partial(down_kernel, skip, kb), in_specs=in_vmem...  3.24 us
  transfers between devices with their start and end apart: 25, of which 12 were waited for; matrix products, arithmetic and copies ran while one was open for 2% of the time, Pallas kernels for 10%

profile of v2, /device:TPU:0, one launch (start us, length us, event | category | flops | bytes accessed | tf_op | source)
XLA Modules:
  0.0 83.5 jit_solution(5991611168031092180)
XLA Ops:
  0.0 0.8 select_reduce_fusion
  0.8 1.0 %concatenate.23 = bf16[8,7296]{1,0:T(8,128)(2,1)S(1)} concatenate(bf16[8,7168]{1,0:T(8,128)(2,1)} %param.6, bf16[8,16]{1,0:T(8,128)(2,1)S(1)} %get-tuple-element.53, bf16[8,16]{1,0:T(8,128)(2,1)S(1)} %get-tuple-element.52, bf16[8,16]{1,0:T(8,128)(2,1)S(1)} %get-tuple-element.51, bf16[8,80]{1,0:T(8,128)(2,1)S(1)} %broadcast_in_dim.21), dimensions={1} | concatenate | bytes 233472 | tf_op jit(solution)/shard_map/concatenate | solution.py:267
  1.8 5.0 %collective-permute-start.2 = (bf16[8,7296]{1,0:T(8,128)(2,1)S(1)}, bf16[8,7296]{1,0:T(8,128)(2,1)S(1)}, u32[]{:S(2)}, u32[]{:S(2)}) collective-permute-start(bf16[8,7296]{1,0:T(8,128)(2,1)S(1)} %concatenate.23), channel_id=1, source_target_pairs={{0,24},{1,25},{2,26},{3,27},{4,28},{5,29},{6,30},{7,31},{8,16},{9,... | collective-permute-start | bytes 350216 | tf_op jit(solution)/shard_map/ppermute | solution.py:37
  6.9 0.6 collective-permute-start
  7.5 0.8 fusion.19
  8.3 6.0 %collective-permute-done = bf16[8,7296]{1,0:T(8,128)(2,1)S(1)} collective-permute-done((bf16[8,7296]{1,0:T(8,128)(2,1)S(1)}, bf16[8,7296]{1,0:T(8,128)(2,1)S(1)}, u32[]{:S(2)}, u32[]{:S(2)}) %collective-permute-start) | collective-permute-done | bytes 116768 | tf_op jit(solution)/shard_map/ppermute | solution.py:37
  14.4 2.3 %collective-permute-done.1 = bf16[8,7296]{1,0:T(8,128)(2,1)S(1)} collective-permute-done((bf16[8,7296]{1,0:T(8,128)(2,1)S(1)}, bf16[8,7296]{1,0:T(8,128)(2,1)S(1)}, u32[]{:S(2)}, u32[]{:S(2)}) %collective-permute-start.1) | collective-permute-done | bytes 116768 | tf_op jit(solution)/shard_map/ppermute | solution.py:37
  16.8 1.6 %collective-permute-start.7 = (bf16[32,3584]{1,0:T(8,128)(2,1)S(1)}, bf16[32,3584]{1,0:T(8,128)(2,1)S(1)}, u32[]{:S(2)}, u32[]{:S(2)}) collective-permute-start(bf16[32,3584]{1,0:T(8,128)(2,1)S(1)} %pad_maximum_fusion.1), channel_id=1, source_target_pairs={{0,2},{1,5},{2,0},{3,7},{4,6},{5,1},{6,4},{7,3},{8,10},{9,13},{10,... | collective-permute-start | bytes 688136 | tf_op jit(solution)/shard_map/ppermute | solution.py:37
  18.4 0.6 collective-permute-start.3
  19.0 3.8 %collective-permute-done.7 = bf16[32,3584]{1,0:T(8,128)(2,1)S(1)} collective-permute-done((bf16[32,3584]{1,0:T(8,128)(2,1)S(1)}, bf16[32,3584]{1,0:T(8,128)(2,1)S(1)}, u32[]{:S(2)}, u32[]{:S(2)}) %collective-permute-start.7) | collective-permute-done | bytes 229408 | tf_op jit(solution)/shard_map/ppermute | solution.py:37
  22.9 1.6 %collective-permute-start.8 = (bf16[64,3584]{1,0:T(8,128)(2,1)S(1)}, bf16[64,3584]{1,0:T(8,128)(2,1)S(1)}, u32[]{:S(2)}, u32[]{:S(2)}) collective-permute-start(bf16[64,3584]{1,0:T(8,128)(2,1)S(1)} %constant_dynamic-update-slice_fusion.5.x0), channel_id=1, source_target_pairs={{0,4},{1,3},{2,6},{3,1},{4,0},{5,7},{6,2},{7,5},{8,12},{9,11},{10,... | collective-permute-start | bytes 1376264 | tf_op jit(solution)/shard_map/ppermute | solution.py:37
  24.5 2.4 %collective-permute-done.3 = bf16[32,3712]{1,0:T(8,128)(2,1)S(1)} collective-permute-done((bf16[32,3712]{1,0:T(8,128)(2,1)S(1)}, bf16[32,3712]{1,0:T(8,128)(2,1)S(1)}, u32[]{:S(2)}, u32[]{:S(2)}) %collective-permute-start.3) | collective-permute-done | bytes 237600 | tf_op jit(solution)/shard_map/ppermute | solution.py:37
  26.9 1.6 %collective-permute-start.4 = (bf16[64,3712]{1,0:T(8,128)(2,1)S(1)}, bf16[64,3712]{1,0:T(8,128)(2,1)S(1)}, u32[]{:S(2)}, u32[]{:S(2)}) collective-permute-start(bf16[64,3712]{1,0:T(8,128)(2,1)S(1)} %constant_dynamic-update-slice_fusion.x0), channel_id=1, source_target_pairs={{0,4},{1,3},{2,6},{3,1},{4,0},{5,7},{6,2},{7,5},{8,12},{9,11},{10,... | collective-permute-start | bytes 1425416 | tf_op jit(solution)/shard_map/ppermute | solution.py:37
  28.5 2.9 %collective-permute-done.8.x1 = bf16[64,3584]{1,0:T(8,128)(2,1)S(1)} collective-permute-done((bf16[64,3584]{1,0:T(8,128)(2,1)S(1)}, bf16[64,3584]{1,0:T(8,128)(2,1)S(1)}, u32[]{:S(2)}, u32[]{:S(2)}) %collective-permute-start.8) | collective-permute-done | bytes 458784 | tf_op jit(solution)/shard_map/ppermute | solution.py:37
  31.9 4.6 %collective-permute-done.4.x1 = bf16[64,3712]{1,0:T(8,128)(2,1)S(1)} collective-permute-done((bf16[64,3712]{1,0:T(8,128)(2,1)S(1)}, bf16[64,3712]{1,0:T(8,128)(2,1)S(1)}, u32[]{:S(2)}, u32[]{:S(2)}) %collective-permute-start.4) | collective-permute-done | bytes 475168 | tf_op jit(solution)/shard_map/ppermute | solution.py:37
  36.5 5.0 %shard_map.64.acc = f32[256,1024]{1,0:T(8,128)S(1)} custom-call(bf16[64,3584]{1,0:T(8,128)(2,1)S(1)} %constant_dynamic-update-slice_fusion.5.x0, bf16[64,3584]{1,0:T(8,128)(2,1)S(1)} %collective-permute-done.8.x1, bf16[64,3584]{1,0:T(8,128)(2,1)S(1)} %collective-permute-done.9.x2, bf16[64,3584]{1,0:T(8,128)(2,1)} %collective-permute-done.10.x3, ...), custom_call_target="tpu_custom_call" | custom-call | flops 1879048192 | bytes 7340032 | tf_op jit(solution)/shard_map/pallas_call | solution.py:193
  41.5 6.1 %shard_map.65 = (bf16[256,512]{1,0:T(8,128)(2,1)S(1)}, f32[256,128]{1,0:T(8,128)S(1)}, f32[64,3584]{1,0:T(8,128)S(1)}, f32[64,3584]{1,0:T(8,128)S(1)}, bf16[64,3...) custom-call(bf16[64,3712]{1,0:T(8,128)(2,1)S(1)} %constant_dynamic-update-slice_fusion.x0, ...), custom_call_target="tpu_custom_call" | custom-call | flops 2818572288 | bytes 11010048 | tf_op jit(solution)/shard_map/pallas_call | solution.py:207
  48.3 3.2 %shard_map.66 = (f32[64,3584]{1,0:T(8,128)S(1)}, f32[64,3584]{1,0:T(8,128)S(1)}, bf16[64,3584]{1,0:T(8,128)(2,1)S(1)}, bf16[64,3584]{1,0:T(8,128)(2,1)S(1)}) custom-call(bf16[256,512]{1,0:T(8,128)(2,1)S(1)} %get-tuple-element.19.hidden, f32[256,128]{1,0:T(8,128)S(1)} %get-tuple-element.20.scale, bf16[1,512,7168]{2,1,0:T(8,128)(2,1)} %wd.3), custom_call_target="tpu_custom_call" | custom-call | flops 939524096 | bytes 3670016 | tf_op jit(solution)/shard_map/pallas_call | solution.py:222
  52.2 1.6 %collective-permute-start.13 = (bf16[64,3584]{1,0:T(8,128)(2,1)S(1)}, bf16[64,3584]{1,0:T(8,128)(2,1)S(1)}, u32[]{:S(2)}, u32[]{:S(2)}) collective-permute-start(bf16[64,3584]{1,0:T(8,128)(2,1)S(1)} %add_convert_fusion.1), channel_id=1, source_target_pairs={{0,4},{1,3},{2,6},{3,1},{4,0},{5,7},{6,2},{7,5},{8,12},{9,11},{10,... | collective-permute-start | bytes 1376264 | tf_op jit(solution)/shard_map/ppermute | solution.py:37
  54.2 1.6 %collective-permute-start.20 = (bf16[64,3584]{1,0:T(8,128)(2,1)S(1)}, bf16[64,3584]{1,0:T(8,128)(2,1)S(1)}, u32[]{:S(2)}, u32[]{:S(2)}) collective-permute-start(bf16[64,3584]{1,0:T(8,128)(2,1)S(1)} %add_convert_fusion), channel_id=1, source_target_pairs={{0,4},{1,3},{2,6},{3,1},{4,0},{5,7},{6,2},{7,5},{8,12},{9,11},{10,... | collective-permute-start | bytes 1376264 | tf_op jit(solution)/shard_map/ppermute | solution.py:37
  55.8 5.0 %collective-permute-done.13 = bf16[64,3584]{1,0:T(8,128)(2,1)S(1)} collective-permute-done((bf16[64,3584]{1,0:T(8,128)(2,1)S(1)}, bf16[64,3584]{1,0:T(8,128)(2,1)S(1)}, u32[]{:S(2)}, u32[]{:S(2)}) %collective-permute-start.13) | collective-permute-done | bytes 458784 | tf_op jit(solution)/shard_map/ppermute | solution.py:37
  61.0 1.6 %collective-permute-start.14 = (bf16[32,3584]{1,0:T(8,128)(2,1)S(1)}, bf16[32,3584]{1,0:T(8,128)(2,1)S(1)}, u32[]{:S(2)}, u32[]{:S(2)}) collective-permute-start(bf16[32,3584]{1,0:T(8,128)(2,1)S(1)} %slice.134), channel_id=1, source_target_pairs={{0,2},{1,5},{2,0},{3,7},{4,6},{5,1},{6,4},{7,3},{8,10},{9,13},{10,... | collective-permute-start | bytes 688136 | tf_op jit(solution)/shard_map/ppermute | solution.py:37
  62.5 5.6 %collective-permute-done.20 = bf16[64,3584]{1,0:T(8,128)(2,1)S(1)} collective-permute-done((bf16[64,3584]{1,0:T(8,128)(2,1)S(1)}, bf16[64,3584]{1,0:T(8,128)(2,1)S(1)}, u32[]{:S(2)}, u32[]{:S(2)}) %collective-permute-start.20) | collective-permute-done | bytes 458784 | tf_op jit(solution)/shard_map/ppermute | solution.py:37
  68.3 1.6 %collective-permute-start.21 = (bf16[32,3584]{1,0:T(8,128)(2,1)S(1)}, bf16[32,3584]{1,0:T(8,128)(2,1)S(1)}, u32[]{:S(2)}, u32[]{:S(2)}) collective-permute-start(bf16[32,3584]{1,0:T(8,128)(2,1)S(1)} %slice.133), channel_id=1, source_target_pairs={{0,2},{1,5},{2,0},{3,7},{4,6},{5,1},{6,4},{7,3},{8,10},{9,13},{10,... | collective-permute-start | bytes 688136 | tf_op jit(solution)/shard_map/ppermute | solution.py:37
  70.2 2.4 %collective-permute-start.17 = (bf16[8,3584]{1,0:T(8,128)(2,1)S(1)}, bf16[8,3584]{1,0:T(8,128)(2,1)S(1)}, u32[]{:S(2)}, u32[]{:S(2)}) collective-permute-start(bf16[8,3584]{1,0:T(8,128)(2,1)S(1)} %get-tuple-element.30), channel_id=1, source_target_pairs={{0,24},{1,25},{2,26},{3,27},{4,28},{5,29},{6,30},{7,31},{8,16},{9,... | collective-permute-start | bytes 172040 | tf_op jit(solution)/shard_map/ppermute | solution.py:37
  72.6 0.9 %collective-permute-start.16 = (bf16[8,3584]{1,0:T(8,128)(2,1)S(1)}, bf16[8,3584]{1,0:T(8,128)(2,1)S(1)}, u32[]{:S(2)}, u32[]{:S(2)}) collective-permute-start(bf16[8,3584]{1,0:T(8,128)(2,1)S(1)} %get-tuple-element.31), channel_id=1, source_target_pairs={{0,16},{1,17},{2,18},{3,19},{4,20},{5,21},{6,22},{7,23},{8,24},{9,... | collective-permute-start | bytes 172040 | tf_op jit(solution)/shard_map/ppermute | solution.py:37
  73.5 0.9 %collective-permute-done.21 = bf16[32,3584]{1,0:T(8,128)(2,1)S(1)} collective-permute-done((bf16[32,3584]{1,0:T(8,128)(2,1)S(1)}, bf16[32,3584]{1,0:T(8,128)(2,1)S(1)}, u32[]{:S(2)}, u32[]{:S(2)}) %collective-permute-start.21) | collective-permute-done | bytes 229408 | tf_op jit(solution)/shard_map/ppermute | solution.py:37
  74.7 2.4 %collective-permute-start.24 = (bf16[8,3584]{1,0:T(8,128)(2,1)S(1)}, bf16[8,3584]{1,0:T(8,128)(2,1)S(1)}, u32[]{:S(2)}, u32[]{:S(2)}) collective-permute-start(bf16[8,3584]{1,0:T(8,128)(2,1)S(1)} %get-tuple-element.33), channel_id=1, source_target_pairs={{0,24},{1,25},{2,26},{3,27},{4,28},{5,29},{6,30},{7,31},{8,16},{9,... | collective-permute-start | bytes 172040 | tf_op jit(solution)/shard_map/ppermute | solution.py:37
  77.1 0.9 %collective-permute-start.23 = (bf16[8,3584]{1,0:T(8,128)(2,1)S(1)}, bf16[8,3584]{1,0:T(8,128)(2,1)S(1)}, u32[]{:S(2)}, u32[]{:S(2)}) collective-permute-start(bf16[8,3584]{1,0:T(8,128)(2,1)S(1)} %get-tuple-element.34), channel_id=1, source_target_pairs={{0,16},{1,17},{2,18},{3,19},{4,20},{5,21},{6,22},{7,23},{8,24},{9,... | collective-permute-start | bytes 172040 | tf_op jit(solution)/shard_map/ppermute | solution.py:37
  78.0 2.8 %collective-permute-done.16 = bf16[8,3584]{1,0:T(8,128)(2,1)S(1)} collective-permute-done((bf16[8,3584]{1,0:T(8,128)(2,1)S(1)}, bf16[8,3584]{1,0:T(8,128)(2,1)S(1)}, u32[]{:S(2)}, u32[]{:S(2)}) %collective-permute-start.16) | collective-permute-done | bytes 57376 | tf_op jit(solution)/shard_map/ppermute | solution.py:37
  80.9 1.9 %collective-permute-done.23 = bf16[8,3584]{1,0:T(8,128)(2,1)S(1)} collective-permute-done((bf16[8,3584]{1,0:T(8,128)(2,1)S(1)}, bf16[8,3584]{1,0:T(8,128)(2,1)S(1)}, u32[]{:S(2)}, u32[]{:S(2)}) %collective-permute-start.23) | collective-permute-done | bytes 57376 | tf_op jit(solution)/shard_map/ppermute | solution.py:37
  82.8 0.7 pad_maximum_fusion.2
  (51 shorter events, 3.4 us)
Async XLA Ops:
  1.8 14.9 %collective-permute-start.2 = (bf16[8,7296]{1,0:T(8,128)(2,1)S(1)}, bf16[8,7296]{1,0:T(8,128)(2,1)S(1)}, u32[]{:S(2)}, u32[]{:S(2)}) collective-permute-start(bf16[8,7296]{1,0:T(8,128)(2,1)S(1)} %concatenate.23), channel_id=1, source_target_pairs={{0,24},{1,25},{2,26},{3,27},{4,28},{5,29},{6,30},{7,31},{8,16},{9,... | collective-permute-start | bytes 350216 | tf_op jit(solution)/shard_map/ppermute | solution.py:37
  6.9 9.8 %collective-permute-start.1 = (bf16[8,7296]{1,0:T(8,128)(2,1)S(1)}, bf16[8,7296]{1,0:T(8,128)(2,1)S(1)}, u32[]{:S(2)}, u32[]{:S(2)}) collective-permute-start(bf16[8,7296]{1,0:T(8,128)(2,1)S(1)} %concatenate.23), channel_id=1, source_target_pairs={{0,16},{1,17},{2,18},{3,19},{4,20},{5,21},{6,22},{7,23},{8,24},{9,... | collective-permute-start | bytes 350216 | tf_op jit(solution)/shard_map/ppermute | solution.py:37
  6.9 7.5 %collective-permute-start = (bf16[8,7296]{1,0:T(8,128)(2,1)S(1)}, bf16[8,7296]{1,0:T(8,128)(2,1)S(1)}, u32[]{:S(2)}, u32[]{:S(2)}) collective-permute-start(bf16[8,7296]{1,0:T(8,128)(2,1)S(1)} %concatenate.23), channel_id=1, source_target_pairs={{0,8},{1,9},{2,10},{3,11},{4,12},{5,13},{6,14},{7,15},{8,0},{9,1},... | collective-permute-start | bytes 350216 | tf_op jit(solution)/shard_map/ppermute | solution.py:37
  16.8 6.1 %collective-permute-start.7 = (bf16[32,3584]{1,0:T(8,128)(2,1)S(1)}, bf16[32,3584]{1,0:T(8,128)(2,1)S(1)}, u32[]{:S(2)}, u32[]{:S(2)}) collective-permute-start(bf16[32,3584]{1,0:T(8,128)(2,1)S(1)} %pad_maximum_fusion.1), channel_id=1, source_target_pairs={{0,2},{1,5},{2,0},{3,7},{4,6},{5,1},{6,4},{7,3},{8,10},{9,13},{10,... | collective-permute-start | bytes 688136 | tf_op jit(solution)/shard_map/ppermute | solution.py:37
  18.4 8.5 %collective-permute-start.3 = (bf16[32,3712]{1,0:T(8,128)(2,1)S(1)}, bf16[32,3712]{1,0:T(8,128)(2,1)S(1)}, u32[]{:S(2)}, u32[]{:S(2)}) collective-permute-start(bf16[32,3712]{1,0:T(8,128)(2,1)S(1)} %pad_maximum_fusion), channel_id=1, source_target_pairs={{0,2},{1,5},{2,0},{3,7},{4,6},{5,1},{6,4},{7,3},{8,10},{9,13},{10,... | collective-permute-start | bytes 712712 | tf_op jit(solution)/shard_map/ppermute | solution.py:37
  22.9 8.5 %collective-permute-start.8 = (bf16[64,3584]{1,0:T(8,128)(2,1)S(1)}, bf16[64,3584]{1,0:T(8,128)(2,1)S(1)}, u32[]{:S(2)}, u32[]{:S(2)}) collective-permute-start(bf16[64,3584]{1,0:T(8,128)(2,1)S(1)} %constant_dynamic-update-slice_fusion.5.x0), channel_id=1, source_target_pairs={{0,4},{1,3},{2,6},{3,1},{4,0},{5,7},{6,2},{7,5},{8,12},{9,11},{10,... | collective-permute-start | bytes 1376264 | tf_op jit(solution)/shard_map/ppermute | solution.py:37
  26.9 9.6 %collective-permute-start.4 = (bf16[64,3712]{1,0:T(8,128)(2,1)S(1)}, bf16[64,3712]{1,0:T(8,128)(2,1)S(1)}, u32[]{:S(2)}, u32[]{:S(2)}) collective-permute-start(bf16[64,3712]{1,0:T(8,128)(2,1)S(1)} %constant_dynamic-update-slice_fusion.x0), channel_id=1, source_target_pairs={{0,4},{1,3},{2,6},{3,1},{4,0},{5,7},{6,2},{7,5},{8,12},{9,11},{10,... | collective-permute-start | bytes 1425416 | tf_op jit(solution)/shard_map/ppermute | solution.py:37
  28.5 8.0 %collective-permute-start.9 = (bf16[64,3584]{1,0:T(8,128)(2,1)S(1)}, bf16[64,3584]{1,0:T(8,128)(2,1)S(1)}, u32[]{:S(2)}, u32[]{:S(2)}) collective-permute-start(bf16[64,3584]{1,0:T(8,128)(2,1)S(1)} %constant_dynamic-update-slice_fusion.5.x0), channel_id=1, source_target_pairs={{0,1},{1,0},{2,3},{3,2},{4,5},{5,4},{6,7},{7,6},{8,9},{9,8},{10,11... | collective-permute-start | bytes 1376264 | tf_op jit(solution)/shard_map/ppermute | solution.py:37
  31.4 5.1 %collective-permute-start.10 = (bf16[64,3584]{1,0:T(8,128)(2,1)S(1)}, bf16[64,3584]{1,0:T(8,128)(2,1)}, u32[]{:S(2)}, u32[]{:S(2)}) collective-permute-start(bf16[64,3584]{1,0:T(8,128)(2,1)S(1)} %collective-permute-done.8.x1), channel_id=1, source_target_pairs={{0,1},{1,0},{2,3},{3,2},{4,5},{5,4},{6,7},{7,6},{8,9},{9,8},{10,11... | collective-permute-start | bytes 1376264 | tf_op jit(solution)/shard_map/ppermute | solution.py:37
  31.4 10.1 %collective-permute-start.5 = (bf16[64,3712]{1,0:T(8,128)(2,1)S(1)}, bf16[64,3712]{1,0:T(8,128)(2,1)S(1)}, u32[]{:S(2)}, u32[]{:S(2)}) collective-permute-start(bf16[64,3712]{1,0:T(8,128)(2,1)S(1)} %constant_dynamic-update-slice_fusion.x0), channel_id=1, source_target_pairs={{0,1},{1,0},{2,3},{3,2},{4,5},{5,4},{6,7},{7,6},{8,9},{9,8},{10,11... | collective-permute-start | bytes 1425416 | tf_op jit(solution)/shard_map/ppermute | solution.py:37
  36.5 5.0 %collective-permute-start.6 = (bf16[64,3712]{1,0:T(8,128)(2,1)S(1)}, bf16[64,3712]{1,0:T(8,128)(2,1)S(1)}, u32[]{:S(2)}, u32[]{:S(2)}) collective-permute-start(bf16[64,3712]{1,0:T(8,128)(2,1)S(1)} %collective-permute-done.4.x1), channel_id=1, source_target_pairs={{0,1},{1,0},{2,3},{3,2},{4,5},{5,4},{6,7},{7,6},{8,9},{9,8},{10,11... | collective-permute-start | bytes 1425416 | tf_op jit(solution)/shard_map/ppermute | solution.py:37
  47.7 4.5 %collective-permute-start.12 = (bf16[64,3584]{1,0:T(8,128)(2,1)S(1)}, bf16[64,3584]{1,0:T(8,128)(2,1)S(1)}, u32[]{:S(2)}, u32[]{:S(2)}) collective-permute-start(bf16[64,3584]{1,0:T(8,128)(2,1)S(1)} %get-tuple-element.18), channel_id=1, source_target_pairs={{0,1},{1,0},{2,3},{3,2},{4,5},{5,4},{6,7},{7,6},{8,9},{9,8},{10,11... | collective-permute-start | bytes 1376264 | tf_op jit(solution)/shard_map/ppermute | solution.py:37
  48.2 7.6 %collective-permute-start.11 = (bf16[64,3584]{1,0:T(8,128)(2,1)S(1)}, bf16[64,3584]{1,0:T(8,128)(2,1)S(1)}, u32[]{:S(2)}, u32[]{:S(2)}) collective-permute-start(bf16[64,3584]{1,0:T(8,128)(2,1)S(1)} %get-tuple-element.16), channel_id=1, source_target_pairs={{0,1},{1,0},{2,3},{3,2},{4,5},{5,4},{6,7},{7,6},{8,9},{9,8},{10,11... | collective-permute-start | bytes 1376264 | tf_op jit(solution)/shard_map/ppermute | solution.py:37
  51.6 11.0 %collective-permute-start.18 = (bf16[64,3584]{1,0:T(8,128)(2,1)S(1)}, bf16[64,3584]{1,0:T(8,128)(2,1)S(1)}, u32[]{:S(2)}, u32[]{:S(2)}) collective-permute-start(bf16[64,3584]{1,0:T(8,128)(2,1)S(1)} %get-tuple-element.22), channel_id=1, source_target_pairs={{0,1},{1,0},{2,3},{3,2},{4,5},{5,4},{6,7},{7,6},{8,9},{9,8},{10,11... | collective-permute-start | bytes 1376264 | tf_op jit(solution)/shard_map/ppermute | solution.py:37
  52.1 2.1 %collective-permute-start.19 = (bf16[64,3584]{1,0:T(8,128)(2,1)S(1)}, bf16[64,3584]{1,0:T(8,128)(2,1)S(1)}, u32[]{:S(2)}, u32[]{:S(2)}) collective-permute-start(bf16[64,3584]{1,0:T(8,128)(2,1)S(1)} %get-tuple-element.24), channel_id=1, source_target_pairs={{0,1},{1,0},{2,3},{3,2},{4,5},{5,4},{6,7},{7,6},{8,9},{9,8},{10,11... | collective-permute-start | bytes 1376264 | tf_op jit(solution)/shard_map/ppermute | solution.py:37
  52.2 8.5 %collective-permute-start.13 = (bf16[64,3584]{1,0:T(8,128)(2,1)S(1)}, bf16[64,3584]{1,0:T(8,128)(2,1)S(1)}, u32[]{:S(2)}, u32[]{:S(2)}) collective-permute-start(bf16[64,3584]{1,0:T(8,128)(2,1)S(1)} %add_convert_fusion.1), channel_id=1, source_target_pairs={{0,4},{1,3},{2,6},{3,1},{4,0},{5,7},{6,2},{7,5},{8,12},{9,11},{10,... | collective-permute-start | bytes 1376264 | tf_op jit(solution)/shard_map/ppermute | solution.py:37
  54.2 13.9 %collective-permute-start.20 = (bf16[64,3584]{1,0:T(8,128)(2,1)S(1)}, bf16[64,3584]{1,0:T(8,128)(2,1)S(1)}, u32[]{:S(2)}, u32[]{:S(2)}) collective-permute-start(bf16[64,3584]{1,0:T(8,128)(2,1)S(1)} %add_convert_fusion), channel_id=1, source_target_pairs={{0,4},{1,3},{2,6},{3,1},{4,0},{5,7},{6,2},{7,5},{8,12},{9,11},{10,... | collective-permute-start | bytes 1376264 | tf_op jit(solution)/shard_map/ppermute | solution.py:37
  61.0 8.9 %collective-permute-start.14 = (bf16[32,3584]{1,0:T(8,128)(2,1)S(1)}, bf16[32,3584]{1,0:T(8,128)(2,1)S(1)}, u32[]{:S(2)}, u32[]{:S(2)}) collective-permute-start(bf16[32,3584]{1,0:T(8,128)(2,1)S(1)} %slice.134), channel_id=1, source_target_pairs={{0,2},{1,5},{2,0},{3,7},{4,6},{5,1},{6,4},{7,3},{8,10},{9,13},{10,... | collective-permute-start | bytes 688136 | tf_op jit(solution)/shard_map/ppermute | solution.py:37
  68.3 6.1 %collective-permute-start.21 = (bf16[32,3584]{1,0:T(8,128)(2,1)S(1)}, bf16[32,3584]{1,0:T(8,128)(2,1)S(1)}, u32[]{:S(2)}, u32[]{:S(2)}) collective-permute-start(bf16[32,3584]{1,0:T(8,128)(2,1)S(1)} %slice.133), channel_id=1, source_target_pairs={{0,2},{1,5},{2,0},{3,7},{4,6},{5,1},{6,4},{7,3},{8,10},{9,13},{10,... | collective-permute-start | bytes 688136 | tf_op jit(solution)/shard_map/ppermute | solution.py:37
  69.9 7.2 %collective-permute-start.15 = (bf16[8,3584]{1,0:T(8,128)(2,1)S(1)}, bf16[8,3584]{1,0:T(8,128)(2,1)S(1)}, u32[]{:S(2)}, u32[]{:S(2)}) collective-permute-start(bf16[8,3584]{1,0:T(8,128)(2,1)S(1)} %get-tuple-element.29), channel_id=1, source_target_pairs={{0,8},{1,9},{2,10},{3,11},{4,12},{5,13},{6,14},{7,15},{8,0},{9,1},... | collective-permute-start | bytes 172040 | tf_op jit(solution)/shard_map/ppermute | solution.py:37
  70.2 7.9 %collective-permute-start.17 = (bf16[8,3584]{1,0:T(8,128)(2,1)S(1)}, bf16[8,3584]{1,0:T(8,128)(2,1)S(1)}, u32[]{:S(2)}, u32[]{:S(2)}) collective-permute-start(bf16[8,3584]{1,0:T(8,128)(2,1)S(1)} %get-tuple-element.30), channel_id=1, source_target_pairs={{0,24},{1,25},{2,26},{3,27},{4,28},{5,29},{6,30},{7,31},{8,16},{9,... | collective-permute-start | bytes 172040 | tf_op jit(solution)/shard_map/ppermute | solution.py:37
  72.6 8.3 %collective-permute-start.16 = (bf16[8,3584]{1,0:T(8,128)(2,1)S(1)}, bf16[8,3584]{1,0:T(8,128)(2,1)S(1)}, u32[]{:S(2)}, u32[]{:S(2)}) collective-permute-start(bf16[8,3584]{1,0:T(8,128)(2,1)S(1)} %get-tuple-element.31), channel_id=1, source_target_pairs={{0,16},{1,17},{2,18},{3,19},{4,20},{5,21},{6,22},{7,23},{8,24},{9,... | collective-permute-start | bytes 172040 | tf_op jit(solution)/shard_map/ppermute | solution.py:37
  74.5 6.4 %collective-permute-start.22 = (bf16[8,3584]{1,0:T(8,128)(2,1)S(1)}, bf16[8,3584]{1,0:T(8,128)(2,1)S(1)}, u32[]{:S(2)}, u32[]{:S(2)}) collective-permute-start(bf16[8,3584]{1,0:T(8,128)(2,1)S(1)} %get-tuple-element.32), channel_id=1, source_target_pairs={{0,8},{1,9},{2,10},{3,11},{4,12},{5,13},{6,14},{7,15},{8,0},{9,1},... | collective-permute-start | bytes 172040 | tf_op jit(solution)/shard_map/ppermute | solution.py:37
  74.7 6.2 %collective-permute-start.24 = (bf16[8,3584]{1,0:T(8,128)(2,1)S(1)}, bf16[8,3584]{1,0:T(8,128)(2,1)S(1)}, u32[]{:S(2)}, u32[]{:S(2)}) collective-permute-start(bf16[8,3584]{1,0:T(8,128)(2,1)S(1)} %get-tuple-element.33), channel_id=1, source_target_pairs={{0,24},{1,25},{2,26},{3,27},{4,28},{5,29},{6,30},{7,31},{8,16},{9,... | collective-permute-start | bytes 172040 | tf_op jit(solution)/shard_map/ppermute | solution.py:37
  77.1 5.7 %collective-permute-start.23 = (bf16[8,3584]{1,0:T(8,128)(2,1)S(1)}, bf16[8,3584]{1,0:T(8,128)(2,1)S(1)}, u32[]{:S(2)}, u32[]{:S(2)}) collective-permute-start(bf16[8,3584]{1,0:T(8,128)(2,1)S(1)} %get-tuple-element.34), channel_id=1, source_target_pairs={{0,16},{1,17},{2,18},{3,19},{4,20},{5,21},{6,22},{7,23},{8,24},{9,... | collective-permute-start | bytes 172040 | tf_op jit(solution)/shard_map/ppermute | solution.py:37

commit v3 on v2

--- a/solution.py
+++ b/solution.py
@@ -12,7 +12,9 @@
 LANES = 128
 CUT = 7
 DOWN = 7
-TIE = 0
+AHEAD = 3
+FIRST = 2
+SECOND = 30
 F32 = jnp.float32
 BF16 = jnp.bfloat16
 
@@ -41,12 +43,15 @@
     return lax.optimization_barrier((x, y))
 
 
-def gather(block, cut, first_product, plan):
+def gather(block, extra, cut, first_product, plan):
     steps, last, core = plan
     for step in steps[:-2]:
-        block = jnp.concatenate([block] + [move(block, p) for p in step], 0)
+        block, extra = [jnp.concatenate([x] + [move(x, p) for p in step], 0) for x in (block, extra)]
     blocks = [block] + [move(block, p) for p in steps[-2]]
-    one, two = [jnp.concatenate([x[:, at] for x in blocks], 0) for at in (slice(0, cut), slice(cut, None))]
+    extra, blocks[1] = after(extra, blocks[1])
+    extras = [extra] + [move(extra, p) for p in steps[-2]]
+    one = jnp.concatenate([x[:, :cut] for x in blocks], 0)
+    two = jnp.concatenate([jnp.concatenate([x[:, cut:], e], 1) for x, e in zip(blocks, extras)], 0)
     one, two = [jnp.concatenate([x, move(x, steps[-1][0])], 0) for x in (one, two)]
     other = move(one, last)
     acc = first_product((one, other, move(one, core), move(other, core)))
@@ -114,7 +119,7 @@
     q, width = x0.shape
     hid = wg.shape[2]
     count = width // kb
-    stream = Stream(up_copies(skip, kb, count, wg, wu, wg_held, wu_held, sems), 4)
+    stream = Stream(up_copies(skip, kb, count, wg, wu, wg_held, wu_held, sems), FIRST)
     for j in range(count):
         for n, x in enumerate((x0, x1, x2, x3)):
             rows[n * q:(n + 1) * q, :] = x[:, j * kb:(j + 1) * kb]
@@ -129,16 +134,18 @@
             acc[:, hid:] += up
 
 
-def second_kernel(skip, kb, x0, x1, x2, x3, mask, acc, wg, wu, wd, hidden, scale, near, far, near_sent, far_sent,
-                  rows, total, wg_held, wu_held, sems, wd_held, wd_sems):
+def second_kernel(skip, kb, x0, x1, x2, x3, mask, acc, wg, wu, wd, *rest):
+    near, rest = rest[0:4], rest[4:]
+    later, rest = rest[0:4], rest[4:]
+    rows, total, hidden, scale, wg_held, wu_held, sems, wd_held, wd_sems = rest
     q = x0.shape[0]
     hid = wg.shape[2]
     width = x0.shape[1] - LANES
     count = width // kb
     stream = Stream(
         up_copies(skip, kb, count, wg, wu, wg_held, wu_held, sems)
-        + down_copies(0, kb, near.shape[1] // kb, wd, wd_held, wd_sems),
-        5,
+        + down_copies(0, kb, wd_held.shape[0], wd, wd_held, wd_sems),
+        AHEAD,
     )
     for n, x in enumerate((x0, x1, x2, x3)):
         s = jnp.sum(x[:, width:].astype(F32) * mask[...], 1, keepdims=True)
@@ -155,24 +162,21 @@
             total[:, hid:] = up
         else:
             hidden[...] = (gate / (1 + jnp.exp(-gate)) * up).astype(BF16)
-    down_blocks(stream, kb, hidden, scale, wd_held, near, far, near_sent, far_sent)
-
-
-def down_blocks(stream, cb, hidden, scale, held, near, far, near_sent, far_sent):
+    down_blocks(stream, 0, hidden, scale, wd_held, *near)
+    down_blocks(stream, near[0].shape[1] // kb, hidden, scale, wd_held, *later)
+
+
+def down_blocks(stream, base, hidden, scale, held, near, far, near_sent, far_sent):
     q = near.shape[0]
+    cb = held.shape[2]
     for j in range(near.shape[1] // cb):
         at = slice(j * cb, (j + 1) * cb)
         stream.wait()
-        share = dot(hidden[...], held[j]) * scale[:, :1]
+        share = dot(hidden[...], held[base + j]) * scale[:, :1]
         near[:, at] = share[:q]
         far[:, at] = share[q:2 * q]
         near_sent[:, at] = share[2 * q:3 * q].astype(BF16)
         far_sent[:, at] = share[3 * q:].astype(BF16)
-
-
-def down_kernel(skip, cb, hidden, scale, wd, near, far, near_sent, far_sent, held, sems):
-    stream = Stream(down_copies(skip, cb, near.shape[1] // cb, wd, held, sems), 99)
-    down_blocks(stream, cb, hidden, scale, held, near, far, near_sent, far_sent)
 
 
 def in_vmem(n):
@@ -201,33 +205,21 @@
     )(*pieces, w_gate, w_up)
 
 
-def second_part(pieces, mask, acc, w_gate, w_up, w_down, skip, width, first, kb):
+def second_part(pieces, mask, acc, w_gate, w_up, w_down, skip, down, kb):
     q = pieces[0].shape[0]
-    hid = w_gate.shape[2]
+    _, full, hid = w_gate.shape
+    width = full - skip
+    rows = 4 * q
     return pl.pallas_call(
         functools.partial(second_kernel, skip, kb),
         in_specs=in_vmem(6) + in_hbm(3),
-        out_specs=in_vmem(6),
-        out_shape=[jax.ShapeDtypeStruct((4 * q, hid), BF16), jax.ShapeDtypeStruct((4 * q, LANES), F32)] + shares(q, first),
-        scratch_shapes=[pltpu.VMEM((4 * q, kb), BF16), pltpu.VMEM((4 * q, 2 * hid), F32)]
-        + held_up(width, hid, kb) + held_down(first, hid, kb),
-        compiler_params=params(30),
-        cost_estimate=cost(16 * q * width * hid + 8 * q * first * hid, 4 * width * hid + 2 * first * hid),
+        out_specs=in_vmem(8),
+        out_shape=shares(q, down) + shares(q, full - down),
+        scratch_shapes=[pltpu.VMEM((rows, kb), BF16), pltpu.VMEM((rows, 2 * hid), F32), pltpu.VMEM((rows, hid), BF16), pltpu.VMEM((rows, LANES), F32)]
+        + held_up(width, hid, kb) + held_down(full, hid, kb),
+        compiler_params=params(SECOND),
+        cost_estimate=cost(4 * rows * width * hid + 2 * rows * full * hid, 4 * width * hid + 2 * full * hid),
     )(*pieces, mask, acc, w_gate, w_up, w_down)
-
-
-def down_part(hidden, scale, w_down, skip, width, kb):
-    q = hidden.shape[0] // 4
-    hid = hidden.shape[1]
-    return pl.pallas_call(
-        functools.partial(down_kernel, skip, kb),
-        in_specs=in_vmem(2) + in_hbm(1),
-        out_specs=in_vmem(4),
-        out_shape=shares(q, width),
-        scratch_shapes=held_down(width, hid, kb),
-        compiler_params=params(20),
-        cost_estimate=cost(8 * q * width * hid, 2 * width * hid),
-    )(hidden, scale, w_down)
 
 
 def cost(flops, moved):
@@ -261,20 +253,16 @@
     mask = ((lane % experts == expert) & (lane < 3 * experts)).astype(F32)[None, :]
 
     w_gate, w_up, w_down = [pltpu.with_memory_space_constraint(w, pltpu.HBM) for w in (w_gate, w_up, w_down)]
-    kb = 512
-    cut = CUT * width // kb // 14 * kb
-    down = DOWN * width // kb // 14 * kb
-    sent = jnp.concatenate([tokens, extra], 1)
-    acc, two = gather(sent, cut, lambda one: first_part(one, w_gate, w_up, cut, kb), plan)
-    hidden, scale, *pieces = second_part(two, mask, acc, w_gate, w_up, w_down, cut, width - cut, down, kb)
-    far = pieces[1] + move(pieces[3], plan[2]).astype(F32)
-    far = far.astype(BF16)
-    if TIE:
-        far, hidden = after(far, hidden)
+    kb = width // (4 if rows * 2 * n_wide <= 256 else 14)
+    cut = CUT * (width // kb) // 14 * kb
+    down = DOWN * (width // kb) // 14 * kb
+    acc, two = gather(tokens, extra, cut, lambda one: first_part(one, w_gate, w_up, cut, kb), plan)
+    pieces = second_part(two, mask, acc, w_gate, w_up, w_down, cut, down, kb)
+    core = plan[2]
+    far = (pieces[1] + move(pieces[3], core).astype(F32)).astype(BF16)
     out = scatter_sum(pieces[0], pieces[2], far, plan)
-    pieces = down_part(hidden, scale, w_down, down, width - down, kb)
-    far = pieces[1] + move(pieces[3], plan[2]).astype(F32)
-    rest = scatter_sum(pieces[0], pieces[2], far.astype(BF16), plan)
+    far = (pieces[5] + move(pieces[7], core).astype(F32)).astype(BF16)
+    rest = scatter_sum(pieces[4], pieces[6], far, plan)
     return jnp.concatenate([out.astype(BF16), rest.astype(BF16)], 1)
 
 

time: 83.7 us -> 82.6 us (0.987)
  starting transfers between devices: 26.1 us -> 31.4 us
  waiting for transfers between devices: 38.6 us -> 34.8 us
  Pallas kernels: 14.3 us -> 12.5 us
  local copies, waits for them, and re-layouts: 2.02 us -> 1.13 us
    ppermute x25 -> x28, starting transfers between devices: 26.1 us -> 31.4 us  [move(): return lax.ppermute(x, AXES, perm)]
    ppermute x25 -> x28, waiting for transfers between devices: 38.6 us -> 34.8 us  [move(): return lax.ppermute(x, AXES, perm)]
    pallas_call x1 -> x0, Pallas kernels: 3.24 us -> none  [down_part(): pl.pallas_call(functools.partial(down_kernel, skip, kb), in_specs=in_vmem...]
    pallas_call x1, Pallas kernels: 6.12 us -> 7.2 us  [second_part(): pl.pallas_call(functools.partial(second_kernel, skip, kb), in_specs=in_vm...]
    concatenate x1, local copies, waits for them, and re-layouts: 0.99 us -> 0.08 us  [body(): jnp.concatenate(split3(table) + [jnp.zeros((rows, LANES - 3 * experts), F...]
  transfers between devices with their start and end apart: 25 -> 28, of which waited for: 12 -> 13; matrix products, arithmetic and copies ran while one was open for 2% -> 3% of each run, Pallas kernels for 10% -> 6%
where the time goes in v3:
time: 82.6 us; the launch traced here: 82.4 us
  waiting for transfers between devices  34.8 us (42%)
  starting transfers between devices  31.4 us (38%)
  Pallas kernels  12.5 us (15%)
  other arithmetic  2.27 us (3%)
  local copies, waits for them, and re-layouts  1.13 us (1%)
    ppermute x28, waiting for transfers between devices, move(): return lax.ppermute(x, AXES, perm)  34.8 us
    ppermute x28, starting transfers between devices, move(): return lax.ppermute(x, AXES, perm)  31.4 us
    pallas_call x1, Pallas kernels, second_part(): pl.pallas_call(functools.partial(second_kernel, skip, kb), in_specs=in_vm...  7.2 us
    pallas_call x1, Pallas kernels, first_part(): pl.pallas_call(functools.partial(first_kernel, 0, kb), in_specs=in_vmem(4...  5.32 us
  transfers between devices with their start and end apart: 28, of which 13 were waited for; matrix products, arithmetic and copies ran while one was open for 3% of the time, Pallas kernels for 6%

profile of v3, /device:TPU:0, one launch (start us, length us, event | category | flops | bytes accessed | tf_op | source)
XLA Modules:
  0.0 82.4 jit_solution(14726824227091056149)
XLA Ops:
  0.0 3.0 %collective-permute-start = (bf16[8,7168]{1,0:T(8,128)(2,1)}, bf16[8,7168]{1,0:T(8,128)(2,1)S(1)}, u32[]{:S(2)}, u32[]{:S(2)}) collective-permute-start(bf16[8,7168]{1,0:T(8,128)(2,1)} %param.6), channel_id=1, source_target_pairs={{0,8},{1,9},{2,10},{3,11},{4,12},{5,13},{6,14},{7,15},{8,0},{9,1},... | collective-permute-start | bytes 344072 | tf_op jit(solution)/shard_map/ppermute | solution.py:39
  3.0 2.6 %collective-permute-start.2 = (bf16[8,7168]{1,0:T(8,128)(2,1)}, bf16[8,7168]{1,0:T(8,128)(2,1)S(1)}, u32[]{:S(2)}, u32[]{:S(2)}) collective-permute-start(bf16[8,7168]{1,0:T(8,128)(2,1)} %param.6), channel_id=1, source_target_pairs={{0,16},{1,17},{2,18},{3,19},{4,20},{5,21},{6,22},{7,23},{8,24},{9,... | collective-permute-start | bytes 344072 | tf_op jit(solution)/shard_map/ppermute | solution.py:39
  5.6 0.9 %fusion.12 = (bf16[8,3584]{1,0:T(8,128)(2,1)S(1)}, bf16[64,3584]{1,0:T(8,128)(2,1)S(1)}, bf16[8,3584]{1,0:T(8,128)(2,1)S(1)}) fusion(bf16[8,7168]{1,0:T(8,128)(2,1)} %param.6), kind=kLoop, calls=%fused_computation.44 | loop fusion | bytes 286720 | tf_op jit(solution)/shard_map/slice | solution.py:53
  6.5 0.8 select_reduce_fusion
  7.5 4.0 %collective-permute-start.5 = (bf16[8,128]{1,0:T(8,128)(2,1)S(1)}, bf16[8,128]{1,0:T(8,128)(2,1)S(1)}, u32[]{:S(2)}, u32[]{:S(2)}) collective-permute-start(bf16[8,128]{1,0:T(8,128)(2,1)S(1)} %maximum_maximum_fusion.1), channel_id=1, source_target_pairs={{0,24},{1,25},{2,26},{3,27},{4,28},{5,29},{6,30},{7,31},{8,16},{9,... | collective-permute-start | bytes 6152 | tf_op jit(solution)/shard_map/ppermute | solution.py:39
  12.1 2.9 %collective-permute-done.2 = bf16[8,7168]{1,0:T(8,128)(2,1)S(1)} collective-permute-done((bf16[8,7168]{1,0:T(8,128)(2,1)}, bf16[8,7168]{1,0:T(8,128)(2,1)S(1)}, u32[]{:S(2)}, u32[]{:S(2)}) %collective-permute-start.2) | collective-permute-done | bytes 114720 | tf_op jit(solution)/shard_map/ppermute | solution.py:39
  15.1 1.6 %collective-permute-start.10 = (bf16[32,3584]{1,0:T(8,128)(2,1)S(1)}, bf16[32,3584]{1,0:T(8,128)(2,1)S(1)}, u32[]{:S(2)}, u32[]{:S(2)}) collective-permute-start(bf16[32,3584]{1,0:T(8,128)(2,1)S(1)} %pad_maximum_fusion), channel_id=1, source_target_pairs={{0,2},{1,5},{2,0},{3,7},{4,6},{5,1},{6,4},{7,3},{8,10},{9,13},{10,... | collective-permute-start | bytes 688136 | tf_op jit(solution)/shard_map/ppermute | solution.py:39
  16.8 1.2 %collective-permute-start.6 = (bf16[32,3712]{1,0:T(8,128)(2,1)S(1)}, bf16[32,3712]{1,0:T(8,128)(2,1)S(1)}, u32[]{:S(2)}, u32[]{:S(2)}) collective-permute-start(bf16[32,3712]{1,0:T(8,128)(2,1)S(1)} %maximum_maximum_fusion), channel_id=1, source_target_pairs={{0,2},{1,5},{2,0},{3,7},{4,6},{5,1},{6,4},{7,3},{8,10},{9,13},{10,... | collective-permute-start | bytes 712712 | tf_op jit(solution)/shard_map/ppermute | solution.py:39
  18.0 4.3 %collective-permute-done.10 = bf16[32,3584]{1,0:T(8,128)(2,1)S(1)} collective-permute-done((bf16[32,3584]{1,0:T(8,128)(2,1)S(1)}, bf16[32,3584]{1,0:T(8,128)(2,1)S(1)}, u32[]{:S(2)}, u32[]{:S(2)}) %collective-permute-start.10) | collective-permute-done | bytes 229408 | tf_op jit(solution)/shard_map/ppermute | solution.py:39
  22.2 1.6 %collective-permute-start.11 = (bf16[64,3584]{1,0:T(8,128)(2,1)S(1)}, bf16[64,3584]{1,0:T(8,128)(2,1)S(1)}, u32[]{:S(2)}, u32[]{:S(2)}) collective-permute-start(bf16[64,3584]{1,0:T(8,128)(2,1)S(1)} %constant_dynamic-update-slice_fusion.1.x0), channel_id=1, source_target_pairs={{0,4},{1,3},{2,6},{3,1},{4,0},{5,7},{6,2},{7,5},{8,12},{9,11},{10,... | collective-permute-start | bytes 1376264 | tf_op jit(solution)/shard_map/ppermute | solution.py:39
  23.9 3.4 %collective-permute-done.6 = bf16[32,3712]{1,0:T(8,128)(2,1)S(1)} collective-permute-done((bf16[32,3712]{1,0:T(8,128)(2,1)S(1)}, bf16[32,3712]{1,0:T(8,128)(2,1)S(1)}, u32[]{:S(2)}, u32[]{:S(2)}) %collective-permute-start.6) | collective-permute-done | bytes 237600 | tf_op jit(solution)/shard_map/ppermute | solution.py:39
  27.3 1.6 %collective-permute-start.7 = (bf16[64,3712]{1,0:T(8,128)(2,1)S(1)}, bf16[64,3712]{1,0:T(8,128)(2,1)S(1)}, u32[]{:S(2)}, u32[]{:S(2)}) collective-permute-start(bf16[64,3712]{1,0:T(8,128)(2,1)S(1)} %constant_dynamic-update-slice_fusion.x0), channel_id=1, source_target_pairs={{0,4},{1,3},{2,6},{3,1},{4,0},{5,7},{6,2},{7,5},{8,12},{9,11},{10,... | collective-permute-start | bytes 1425416 | tf_op jit(solution)/shard_map/ppermute | solution.py:39
  29.0 1.8 %collective-permute-done.11.x1 = bf16[64,3584]{1,0:T(8,128)(2,1)S(1)} collective-permute-done((bf16[64,3584]{1,0:T(8,128)(2,1)S(1)}, bf16[64,3584]{1,0:T(8,128)(2,1)S(1)}, u32[]{:S(2)}, u32[]{:S(2)}) %collective-permute-start.11) | collective-permute-done | bytes 458784 | tf_op jit(solution)/shard_map/ppermute | solution.py:39
  31.3 4.8 %collective-permute-done.7.x1 = bf16[64,3712]{1,0:T(8,128)(2,1)S(1)} collective-permute-done((bf16[64,3712]{1,0:T(8,128)(2,1)S(1)}, bf16[64,3712]{1,0:T(8,128)(2,1)S(1)}, u32[]{:S(2)}, u32[]{:S(2)}) %collective-permute-start.7) | collective-permute-done | bytes 475168 | tf_op jit(solution)/shard_map/ppermute | solution.py:39
  36.1 5.3 %shard_map.64.acc = f32[256,1024]{1,0:T(8,128)S(1)} custom-call(bf16[64,3584]{1,0:T(8,128)(2,1)S(1)} %constant_dynamic-update-slice_fusion.1.x0, bf16[64,3584]{1,0:T(8,128)(2,1)S(1)} %collective-permute-done.11.x1, bf16[64,3584]{1,0:T(8,128)(2,1)S(1)} %collective-permute-done.12.x2, bf16[64,3584]{1,0:T(8,128)(2,1)} %collective-permute-done.13.x3, ...), custom_call_target="tpu_custom_call" | custom-call | flops 1879048192 | bytes 7340032 | tf_op jit(solution)/shard_map/pallas_call | solution.py:197
  41.4 7.2 %shard_map.65 = (f32[64,3584]{1,0:T(8,128)S(1)}, f32[64,3584]{1,0:T(8,128)S(1)}, bf16[64,3584]{1,0:T(8,128)(2,1)S(1)}, bf16[64,3584]{1,0:T(8,128)(2,1)S(1)}, f32...) custom-call(bf16[64,3712]{1,0:T(8,128)(2,1)S(1)} %constant_dynamic-up, ...), custom_call_target="tpu_custom_call" | custom-call | flops 3758096384 | bytes 14680064 | tf_op jit(solution)/shard_map/pallas_call | solution.py:213
  49.8 0.9 %collective-permute-done.15 = bf16[64,3584]{1,0:T(8,128)(2,1)S(1)} collective-permute-done((bf16[64,3584]{1,0:T(8,128)(2,1)S(1)}, bf16[64,3584]{1,0:T(8,128)(2,1)S(1)}, u32[]{:S(2)}, u32[]{:S(2)}) %collective-permute-start.15) | collective-permute-done | bytes 458784 | tf_op jit(solution)/shard_map/ppermute | solution.py:39
  50.8 1.6 %collective-permute-start.16 = (bf16[64,3584]{1,0:T(8,128)(2,1)S(1)}, bf16[64,3584]{1,0:T(8,128)(2,1)S(1)}, u32[]{:S(2)}, u32[]{:S(2)}) collective-permute-start(bf16[64,3584]{1,0:T(8,128)(2,1)S(1)} %add_convert_fusion.1), channel_id=1, source_target_pairs={{0,4},{1,3},{2,6},{3,1},{4,0},{5,7},{6,2},{7,5},{8,12},{9,11},{10,... | collective-permute-start | bytes 1376264 | tf_op jit(solution)/shard_map/ppermute | solution.py:39
  52.7 1.6 %collective-permute-start.23 = (bf16[64,3584]{1,0:T(8,128)(2,1)S(1)}, bf16[64,3584]{1,0:T(8,128)(2,1)S(1)}, u32[]{:S(2)}, u32[]{:S(2)}) collective-permute-start(bf16[64,3584]{1,0:T(8,128)(2,1)S(1)} %add_convert_fusion), channel_id=1, source_target_pairs={{0,4},{1,3},{2,6},{3,1},{4,0},{5,7},{6,2},{7,5},{8,12},{9,11},{10,... | collective-permute-start | bytes 1376264 | tf_op jit(solution)/shard_map/ppermute | solution.py:39
  54.4 4.9 %collective-permute-done.16 = bf16[64,3584]{1,0:T(8,128)(2,1)S(1)} collective-permute-done((bf16[64,3584]{1,0:T(8,128)(2,1)S(1)}, bf16[64,3584]{1,0:T(8,128)(2,1)S(1)}, u32[]{:S(2)}, u32[]{:S(2)}) %collective-permute-start.16) | collective-permute-done | bytes 458784 | tf_op jit(solution)/shard_map/ppermute | solution.py:39
  59.5 1.6 %collective-permute-start.17 = (bf16[32,3584]{1,0:T(8,128)(2,1)S(1)}, bf16[32,3584]{1,0:T(8,128)(2,1)S(1)}, u32[]{:S(2)}, u32[]{:S(2)}) collective-permute-start(bf16[32,3584]{1,0:T(8,128)(2,1)S(1)} %slice.127), channel_id=1, source_target_pairs={{0,2},{1,5},{2,0},{3,7},{4,6},{5,1},{6,4},{7,3},{8,10},{9,13},{10,... | collective-permute-start | bytes 688136 | tf_op jit(solution)/shard_map/ppermute | solution.py:39
  61.1 5.6 %collective-permute-done.23 = bf16[64,3584]{1,0:T(8,128)(2,1)S(1)} collective-permute-done((bf16[64,3584]{1,0:T(8,128)(2,1)S(1)}, bf16[64,3584]{1,0:T(8,128)(2,1)S(1)}, u32[]{:S(2)}, u32[]{:S(2)}) %collective-permute-start.23) | collective-permute-done | bytes 458784 | tf_op jit(solution)/shard_map/ppermute | solution.py:39
  66.9 1.6 %collective-permute-start.24 = (bf16[32,3584]{1,0:T(8,128)(2,1)S(1)}, bf16[32,3584]{1,0:T(8,128)(2,1)S(1)}, u32[]{:S(2)}, u32[]{:S(2)}) collective-permute-start(bf16[32,3584]{1,0:T(8,128)(2,1)S(1)} %slice.126), channel_id=1, source_target_pairs={{0,2},{1,5},{2,0},{3,7},{4,6},{5,1},{6,4},{7,3},{8,10},{9,13},{10,... | collective-permute-start | bytes 688136 | tf_op jit(solution)/shard_map/ppermute | solution.py:39
  68.5 0.6 collective-permute-start.18
  69.2 2.5 %collective-permute-start.20 = (bf16[8,3584]{1,0:T(8,128)(2,1)S(1)}, bf16[8,3584]{1,0:T(8,128)(2,1)S(1)}, u32[]{:S(2)}, u32[]{:S(2)}) collective-permute-start(bf16[8,3584]{1,0:T(8,128)(2,1)S(1)} %get-tuple-element.30), channel_id=1, source_target_pairs={{0,24},{1,25},{2,26},{3,27},{4,28},{5,29},{6,30},{7,31},{8,16},{9,... | collective-permute-start | bytes 172040 | tf_op jit(solution)/shard_map/ppermute | solution.py:39
  72.1 0.9 %collective-permute-done.24 = bf16[32,3584]{1,0:T(8,128)(2,1)S(1)} collective-permute-done((bf16[32,3584]{1,0:T(8,128)(2,1)S(1)}, bf16[32,3584]{1,0:T(8,128)(2,1)S(1)}, u32[]{:S(2)}, u32[]{:S(2)}) %collective-permute-start.24) | collective-permute-done | bytes 229408 | tf_op jit(solution)/shard_map/ppermute | solution.py:39
  73.0 0.7 collective-permute-start.25
  73.7 2.5 %collective-permute-start.27 = (bf16[8,3584]{1,0:T(8,128)(2,1)S(1)}, bf16[8,3584]{1,0:T(8,128)(2,1)S(1)}, u32[]{:S(2)}, u32[]{:S(2)}) collective-permute-start(bf16[8,3584]{1,0:T(8,128)(2,1)S(1)} %get-tuple-element.33), channel_id=1, source_target_pairs={{0,24},{1,25},{2,26},{3,27},{4,28},{5,29},{6,30},{7,31},{8,16},{9,... | collective-permute-start | bytes 172040 | tf_op jit(solution)/shard_map/ppermute | solution.py:39
  76.6 2.2 %collective-permute-done.19 = bf16[8,3584]{1,0:T(8,128)(2,1)S(1)} collective-permute-done((bf16[8,3584]{1,0:T(8,128)(2,1)S(1)}, bf16[8,3584]{1,0:T(8,128)(2,1)S(1)}, u32[]{:S(2)}, u32[]{:S(2)}) %collective-permute-start.19) | collective-permute-done | bytes 57376 | tf_op jit(solution)/shard_map/ppermute | solution.py:39
  78.8 1.0 %collective-permute-done.27 = bf16[8,3584]{1,0:T(8,128)(2,1)S(1)} collective-permute-done((bf16[8,3584]{1,0:T(8,128)(2,1)S(1)}, bf16[8,3584]{1,0:T(8,128)(2,1)S(1)}, u32[]{:S(2)}, u32[]{:S(2)}) %collective-permute-start.27) | collective-permute-done | bytes 57376 | tf_op jit(solution)/shard_map/ppermute | solution.py:39
  79.8 1.9 %collective-permute-done.26 = bf16[8,3584]{1,0:T(8,128)(2,1)S(1)} collective-permute-done((bf16[8,3584]{1,0:T(8,128)(2,1)S(1)}, bf16[8,3584]{1,0:T(8,128)(2,1)S(1)}, u32[]{:S(2)}, u32[]{:S(2)}) %collective-permute-start.26) | collective-permute-done | bytes 57376 | tf_op jit(solution)/shard_map/ppermute | solution.py:39
  81.7 0.7 pad_maximum_fusion.1
  (57 shorter events, 4.3 us)
Async XLA Ops:
  0.0 7.5 %collective-permute-start = (bf16[8,7168]{1,0:T(8,128)(2,1)}, bf16[8,7168]{1,0:T(8,128)(2,1)S(1)}, u32[]{:S(2)}, u32[]{:S(2)}) collective-permute-start(bf16[8,7168]{1,0:T(8,128)(2,1)} %param.6), channel_id=1, source_target_pairs={{0,8},{1,9},{2,10},{3,11},{4,12},{5,13},{6,14},{7,15},{8,0},{9,1},... | collective-permute-start | bytes 344072 | tf_op jit(solution)/shard_map/ppermute | solution.py:39
  3.0 12.0 %collective-permute-start.2 = (bf16[8,7168]{1,0:T(8,128)(2,1)}, bf16[8,7168]{1,0:T(8,128)(2,1)S(1)}, u32[]{:S(2)}, u32[]{:S(2)}) collective-permute-start(bf16[8,7168]{1,0:T(8,128)(2,1)} %param.6), channel_id=1, source_target_pairs={{0,16},{1,17},{2,18},{3,19},{4,20},{5,21},{6,22},{7,23},{8,24},{9,... | collective-permute-start | bytes 344072 | tf_op jit(solution)/shard_map/ppermute | solution.py:39
  5.6 9.5 %collective-permute-start.4 = (bf16[8,7168]{1,0:T(8,128)(2,1)}, bf16[8,7168]{1,0:T(8,128)(2,1)S(1)}, u32[]{:S(2)}, u32[]{:S(2)}) collective-permute-start(bf16[8,7168]{1,0:T(8,128)(2,1)} %param.6), channel_id=1, source_target_pairs={{0,24},{1,25},{2,26},{3,27},{4,28},{5,29},{6,30},{7,31},{8,16},{9,... | collective-permute-start | bytes 344072 | tf_op jit(solution)/shard_map/ppermute | solution.py:39
  7.5 9.2 %collective-permute-start.5 = (bf16[8,128]{1,0:T(8,128)(2,1)S(1)}, bf16[8,128]{1,0:T(8,128)(2,1)S(1)}, u32[]{:S(2)}, u32[]{:S(2)}) collective-permute-start(bf16[8,128]{1,0:T(8,128)(2,1)S(1)} %maximum_maximum_fusion.1), channel_id=1, source_target_pairs={{0,24},{1,25},{2,26},{3,27},{4,28},{5,29},{6,30},{7,31},{8,16},{9,... | collective-permute-start | bytes 6152 | tf_op jit(solution)/shard_map/ppermute | solution.py:39
  11.5 5.2 %collective-permute-start.3 = (bf16[8,128]{1,0:T(8,128)(2,1)S(1)}, bf16[8,128]{1,0:T(8,128)(2,1)S(1)}, u32[]{:S(2)}, u32[]{:S(2)}) collective-permute-start(bf16[8,128]{1,0:T(8,128)(2,1)S(1)} %maximum_maximum_fusion.1), channel_id=1, source_target_pairs={{0,16},{1,17},{2,18},{3,19},{4,20},{5,21},{6,22},{7,23},{8,24},{9,... | collective-permute-start | bytes 6152 | tf_op jit(solution)/shard_map/ppermute | solution.py:39
  11.5 5.2 %collective-permute-start.1 = (bf16[8,128]{1,0:T(8,128)(2,1)S(1)}, bf16[8,128]{1,0:T(8,128)(2,1)S(1)}, u32[]{:S(2)}, u32[]{:S(2)}) collective-permute-start(bf16[8,128]{1,0:T(8,128)(2,1)S(1)} %maximum_maximum_fusion.1), channel_id=1, source_target_pairs={{0,8},{1,9},{2,10},{3,11},{4,12},{5,13},{6,14},{7,15},{8,0},{9,1},... | collective-permute-start | bytes 6152 | tf_op jit(solution)/shard_map/ppermute | solution.py:39
  15.1 7.1 %collective-permute-start.10 = (bf16[32,3584]{1,0:T(8,128)(2,1)S(1)}, bf16[32,3584]{1,0:T(8,128)(2,1)S(1)}, u32[]{:S(2)}, u32[]{:S(2)}) collective-permute-start(bf16[32,3584]{1,0:T(8,128)(2,1)S(1)} %pad_maximum_fusion), channel_id=1, source_target_pairs={{0,2},{1,5},{2,0},{3,7},{4,6},{5,1},{6,4},{7,3},{8,10},{9,13},{10,... | collective-permute-start | bytes 688136 | tf_op jit(solution)/shard_map/ppermute | solution.py:39
  16.8 10.6 %collective-permute-start.6 = (bf16[32,3712]{1,0:T(8,128)(2,1)S(1)}, bf16[32,3712]{1,0:T(8,128)(2,1)S(1)}, u32[]{:S(2)}, u32[]{:S(2)}) collective-permute-start(bf16[32,3712]{1,0:T(8,128)(2,1)S(1)} %maximum_maximum_fusion), channel_id=1, source_target_pairs={{0,2},{1,5},{2,0},{3,7},{4,6},{5,1},{6,4},{7,3},{8,10},{9,13},{10,... | collective-permute-start | bytes 712712 | tf_op jit(solution)/shard_map/ppermute | solution.py:39
  22.2 8.5 %collective-permute-start.11 = (bf16[64,3584]{1,0:T(8,128)(2,1)S(1)}, bf16[64,3584]{1,0:T(8,128)(2,1)S(1)}, u32[]{:S(2)}, u32[]{:S(2)}) collective-permute-start(bf16[64,3584]{1,0:T(8,128)(2,1)S(1)} %constant_dynamic-update-slice_fusion.1.x0), channel_id=1, source_target_pairs={{0,4},{1,3},{2,6},{3,1},{4,0},{5,7},{6,2},{7,5},{8,12},{9,11},{10,... | collective-permute-start | bytes 1376264 | tf_op jit(solution)/shard_map/ppermute | solution.py:39
  27.3 8.7 %collective-permute-start.7 = (bf16[64,3712]{1,0:T(8,128)(2,1)S(1)}, bf16[64,3712]{1,0:T(8,128)(2,1)S(1)}, u32[]{:S(2)}, u32[]{:S(2)}) collective-permute-start(bf16[64,3712]{1,0:T(8,128)(2,1)S(1)} %constant_dynamic-update-slice_fusion.x0), channel_id=1, source_target_pairs={{0,4},{1,3},{2,6},{3,1},{4,0},{5,7},{6,2},{7,5},{8,12},{9,11},{10,... | collective-permute-start | bytes 1425416 | tf_op jit(solution)/shard_map/ppermute | solution.py:39
  29.0 7.1 %collective-permute-start.12 = (bf16[64,3584]{1,0:T(8,128)(2,1)S(1)}, bf16[64,3584]{1,0:T(8,128)(2,1)S(1)}, u32[]{:S(2)}, u32[]{:S(2)}) collective-permute-start(bf16[64,3584]{1,0:T(8,128)(2,1)S(1)} %constant_dynamic-update-slice_fusion.1.x0), channel_id=1, source_target_pairs={{0,1},{1,0},{2,3},{3,2},{4,5},{5,4},{6,7},{7,6},{8,9},{9,8},{10,11... | collective-permute-start | bytes 1376264 | tf_op jit(solution)/shard_map/ppermute | solution.py:39
  30.8 5.3 %collective-permute-start.13 = (bf16[64,3584]{1,0:T(8,128)(2,1)S(1)}, bf16[64,3584]{1,0:T(8,128)(2,1)}, u32[]{:S(2)}, u32[]{:S(2)}) collective-permute-start(bf16[64,3584]{1,0:T(8,128)(2,1)S(1)} %collective-permute-done.11.x1), channel_id=1, source_target_pairs={{0,1},{1,0},{2,3},{3,2},{4,5},{5,4},{6,7},{7,6},{8,9},{9,8},{10,11... | collective-permute-start | bytes 1376264 | tf_op jit(solution)/shard_map/ppermute | solution.py:39
  30.8 10.6 %collective-permute-start.8 = (bf16[64,3712]{1,0:T(8,128)(2,1)S(1)}, bf16[64,3712]{1,0:T(8,128)(2,1)S(1)}, u32[]{:S(2)}, u32[]{:S(2)}) collective-permute-start(bf16[64,3712]{1,0:T(8,128)(2,1)S(1)} %constant_dynamic-update-slice_fusion.x0), channel_id=1, source_target_pairs={{0,1},{1,0},{2,3},{3,2},{4,5},{5,4},{6,7},{7,6},{8,9},{9,8},{10,11... | collective-permute-start | bytes 1425416 | tf_op jit(solution)/shard_map/ppermute | solution.py:39
  36.1 5.4 %collective-permute-start.9 = (bf16[64,3712]{1,0:T(8,128)(2,1)S(1)}, bf16[64,3712]{1,0:T(8,128)(2,1)S(1)}, u32[]{:S(2)}, u32[]{:S(2)}) collective-permute-start(bf16[64,3712]{1,0:T(8,128)(2,1)S(1)} %collective-permute-done.7.x1), channel_id=1, source_target_pairs={{0,1},{1,0},{2,3},{3,2},{4,5},{5,4},{6,7},{7,6},{8,9},{9,8},{10,11... | collective-permute-start | bytes 1425416 | tf_op jit(solution)/shard_map/ppermute | solution.py:39
  48.7 2.0 %collective-permute-start.15 = (bf16[64,3584]{1,0:T(8,128)(2,1)S(1)}, bf16[64,3584]{1,0:T(8,128)(2,1)S(1)}, u32[]{:S(2)}, u32[]{:S(2)}) collective-permute-start(bf16[64,3584]{1,0:T(8,128)(2,1)S(1)} %get-tuple-element.20), channel_id=1, source_target_pairs={{0,1},{1,0},{2,3},{3,2},{4,5},{5,4},{6,7},{7,6},{8,9},{9,8},{10,11... | collective-permute-start | bytes 1376264 | tf_op jit(solution)/shard_map/ppermute | solution.py:39
  49.2 5.2 %collective-permute-start.14 = (bf16[64,3584]{1,0:T(8,128)(2,1)S(1)}, bf16[64,3584]{1,0:T(8,128)(2,1)S(1)}, u32[]{:S(2)}, u32[]{:S(2)}) collective-permute-start(bf16[64,3584]{1,0:T(8,128)(2,1)S(1)} %get-tuple-element.18), channel_id=1, source_target_pairs={{0,1},{1,0},{2,3},{3,2},{4,5},{5,4},{6,7},{7,6},{8,9},{9,8},{10,11... | collective-permute-start | bytes 1376264 | tf_op jit(solution)/shard_map/ppermute | solution.py:39
  49.3 11.8 %collective-permute-start.21 = (bf16[64,3584]{1,0:T(8,128)(2,1)S(1)}, bf16[64,3584]{1,0:T(8,128)(2,1)S(1)}, u32[]{:S(2)}, u32[]{:S(2)}) collective-permute-start(bf16[64,3584]{1,0:T(8,128)(2,1)S(1)} %get-tuple-element.22), channel_id=1, source_target_pairs={{0,1},{1,0},{2,3},{3,2},{4,5},{5,4},{6,7},{7,6},{8,9},{9,8},{10,11... | collective-permute-start | bytes 1376264 | tf_op jit(solution)/shard_map/ppermute | solution.py:39
  49.7 2.9 %collective-permute-start.22 = (bf16[64,3584]{1,0:T(8,128)(2,1)S(1)}, bf16[64,3584]{1,0:T(8,128)(2,1)S(1)}, u32[]{:S(2)}, u32[]{:S(2)}) collective-permute-start(bf16[64,3584]{1,0:T(8,128)(2,1)S(1)} %get-tuple-element.24), channel_id=1, source_target_pairs={{0,1},{1,0},{2,3},{3,2},{4,5},{5,4},{6,7},{7,6},{8,9},{9,8},{10,11... | collective-permute-start | bytes 1376264 | tf_op jit(solution)/shard_map/ppermute | solution.py:39
  50.8 8.5 %collective-permute-start.16 = (bf16[64,3584]{1,0:T(8,128)(2,1)S(1)}, bf16[64,3584]{1,0:T(8,128)(2,1)S(1)}, u32[]{:S(2)}, u32[]{:S(2)}) collective-permute-start(bf16[64,3584]{1,0:T(8,128)(2,1)S(1)} %add_convert_fusion.1), channel_id=1, source_target_pairs={{0,4},{1,3},{2,6},{3,1},{4,0},{5,7},{6,2},{7,5},{8,12},{9,11},{10,... | collective-permute-start | bytes 1376264 | tf_op jit(solution)/shard_map/ppermute | solution.py:39
  52.7 13.9 %collective-permute-start.23 = (bf16[64,3584]{1,0:T(8,128)(2,1)S(1)}, bf16[64,3584]{1,0:T(8,128)(2,1)S(1)}, u32[]{:S(2)}, u32[]{:S(2)}) collective-permute-start(bf16[64,3584]{1,0:T(8,128)(2,1)S(1)} %add_convert_fusion), channel_id=1, source_target_pairs={{0,4},{1,3},{2,6},{3,1},{4,0},{5,7},{6,2},{7,5},{8,12},{9,11},{10,... | collective-permute-start | bytes 1376264 | tf_op jit(solution)/shard_map/ppermute | solution.py:39
  59.5 9.0 %collective-permute-start.17 = (bf16[32,3584]{1,0:T(8,128)(2,1)S(1)}, bf16[32,3584]{1,0:T(8,128)(2,1)S(1)}, u32[]{:S(2)}, u32[]{:S(2)}) collective-permute-start(bf16[32,3584]{1,0:T(8,128)(2,1)S(1)} %slice.127), channel_id=1, source_target_pairs={{0,2},{1,5},{2,0},{3,7},{4,6},{5,1},{6,4},{7,3},{8,10},{9,13},{10,... | collective-permute-start | bytes 688136 | tf_op jit(solution)/shard_map/ppermute | solution.py:39
  66.9 6.1 %collective-permute-start.24 = (bf16[32,3584]{1,0:T(8,128)(2,1)S(1)}, bf16[32,3584]{1,0:T(8,128)(2,1)S(1)}, u32[]{:S(2)}, u32[]{:S(2)}) collective-permute-start(bf16[32,3584]{1,0:T(8,128)(2,1)S(1)} %slice.126), channel_id=1, source_target_pairs={{0,2},{1,5},{2,0},{3,7},{4,6},{5,1},{6,4},{7,3},{8,10},{9,13},{10,... | collective-permute-start | bytes 688136 | tf_op jit(solution)/shard_map/ppermute | solution.py:39
  68.5 7.7 %collective-permute-start.18 = (bf16[8,3584]{1,0:T(8,128)(2,1)S(1)}, bf16[8,3584]{1,0:T(8,128)(2,1)S(1)}, u32[]{:S(2)}, u32[]{:S(2)}) collective-permute-start(bf16[8,3584]{1,0:T(8,128)(2,1)S(1)} %get-tuple-element.29), channel_id=1, source_target_pairs={{0,8},{1,9},{2,10},{3,11},{4,12},{5,13},{6,14},{7,15},{8,0},{9,1},... | collective-permute-start | bytes 172040 | tf_op jit(solution)/shard_map/ppermute | solution.py:39
  69.2 7.4 %collective-permute-start.20 = (bf16[8,3584]{1,0:T(8,128)(2,1)S(1)}, bf16[8,3584]{1,0:T(8,128)(2,1)S(1)}, u32[]{:S(2)}, u32[]{:S(2)}) collective-permute-start(bf16[8,3584]{1,0:T(8,128)(2,1)S(1)} %get-tuple-element.30), channel_id=1, source_target_pairs={{0,24},{1,25},{2,26},{3,27},{4,28},{5,29},{6,30},{7,31},{8,16},{9,... | collective-permute-start | bytes 172040 | tf_op jit(solution)/shard_map/ppermute | solution.py:39
  71.7 7.1 %collective-permute-start.19 = (bf16[8,3584]{1,0:T(8,128)(2,1)S(1)}, bf16[8,3584]{1,0:T(8,128)(2,1)S(1)}, u32[]{:S(2)}, u32[]{:S(2)}) collective-permute-start(bf16[8,3584]{1,0:T(8,128)(2,1)S(1)} %get-tuple-element.31), channel_id=1, source_target_pairs={{0,16},{1,17},{2,18},{3,19},{4,20},{5,21},{6,22},{7,23},{8,24},{9,... | collective-permute-start | bytes 172040 | tf_op jit(solution)/shard_map/ppermute | solution.py:39
  73.0 5.8 %collective-permute-start.25 = (bf16[8,3584]{1,0:T(8,128)(2,1)S(1)}, bf16[8,3584]{1,0:T(8,128)(2,1)S(1)}, u32[]{:S(2)}, u32[]{:S(2)}) collective-permute-start(bf16[8,3584]{1,0:T(8,128)(2,1)S(1)} %get-tuple-element.32), channel_id=1, source_target_pairs={{0,8},{1,9},{2,10},{3,11},{4,12},{5,13},{6,14},{7,15},{8,0},{9,1},... | collective-permute-start | bytes 172040 | tf_op jit(solution)/shard_map/ppermute | solution.py:39
  73.7 6.1 %collective-permute-start.27 = (bf16[8,3584]{1,0:T(8,128)(2,1)S(1)}, bf16[8,3584]{1,0:T(8,128)(2,1)S(1)}, u32[]{:S(2)}, u32[]{:S(2)}) collective-permute-start(bf16[8,3584]{1,0:T(8,128)(2,1)S(1)} %get-tuple-element.33), channel_id=1, source_target_pairs={{0,24},{1,25},{2,26},{3,27},{4,28},{5,29},{6,30},{7,31},{8,16},{9,... | collective-permute-start | bytes 172040 | tf_op jit(solution)/shard_map/ppermute | solution.py:39
  76.2 5.5 %collective-permute-start.26 = (bf16[8,3584]{1,0:T(8,128)(2,1)S(1)}, bf16[8,3584]{1,0:T(8,128)(2,1)S(1)}, u32[]{:S(2)}, u32[]{:S(2)}) collective-permute-start(bf16[8,3584]{1,0:T(8,128)(2,1)S(1)} %get-tuple-element.34), channel_id=1, source_target_pairs={{0,16},{1,17},{2,18},{3,19},{4,20},{5,21},{6,22},{7,23},{8,24},{9,... | collective-permute-start | bytes 172040 | tf_op jit(solution)/shard_map/ppermute | solution.py:39

commit v4 on v3

--- a/solution.py
+++ b/solution.py
@@ -15,6 +15,7 @@
 AHEAD = 3
 FIRST = 2
 SECOND = 30
+WEIGHT = 20
 F32 = jnp.float32
 BF16 = jnp.bfloat16
 
@@ -201,7 +202,7 @@
         out_shape=jax.ShapeDtypeStruct((4 * q, 2 * hid), F32),
         scratch_shapes=[pltpu.VMEM((4 * q, kb), BF16)] + held_up(width, hid, kb),
         compiler_params=params(30),
-        cost_estimate=cost(16 * q * width * hid, 4 * width * hid),
+        cost_estimate=cost(WEIGHT * 16 * q * width * hid, WEIGHT * 4 * width * hid),
     )(*pieces, w_gate, w_up)
 
 

time: 82.6 us -> 81.6 us (0.988)
  Pallas kernels: 12.5 us -> 11.5 us
    pallas_call x1, Pallas kernels: 5.32 us -> 4.3 us  [first_part(): pl.pallas_call(functools.partial(first_kernel, 0, kb), in_specs=in_vmem(4...]
  transfers between devices with their start and end apart: 28 -> 28, of which waited for: 13 -> 13; matrix products, arithmetic and copies ran while one was open for 3% -> 3% of each run, Pallas kernels for 6% -> 5%
where the time goes in v4:
time: 81.6 us; the launch traced here: 81.4 us
  waiting for transfers between devices  34.8 us (43%)
  starting transfers between devices  31.4 us (38%)
  Pallas kernels  11.5 us (14%)
  other arithmetic  2.27 us (3%)
  local copies, waits for them, and re-layouts  1.13 us (1%)
    ppermute x28, waiting for transfers between devices, move(): return lax.ppermute(x, AXES, perm)  34.8 us
    ppermute x28, starting transfers between devices, move(): return lax.ppermute(x, AXES, perm)  31.4 us
    pallas_call x1, Pallas kernels, second_part(): pl.pallas_call(functools.partial(second_kernel, skip, kb), in_specs=in_vm...  7.2 us
    pallas_call x1, Pallas kernels, first_part(): pl.pallas_call(functools.partial(first_kernel, 0, kb), in_specs=in_vmem(4...  4.3 us
  transfers between devices with their start and end apart: 28, of which 13 were waited for; matrix products, arithmetic and copies ran while one was open for 3% of the time, Pallas kernels for 5%

profile of v4, /device:TPU:0, one launch (start us, length us, event | category | flops | bytes accessed | tf_op | source)
XLA Modules:
  0.0 81.4 jit_solution(10951763437409223333)
XLA Ops:
  0.0 3.0 %collective-permute-start = (bf16[8,7168]{1,0:T(8,128)(2,1)}, bf16[8,7168]{1,0:T(8,128)(2,1)S(1)}, u32[]{:S(2)}, u32[]{:S(2)}) collective-permute-start(bf16[8,7168]{1,0:T(8,128)(2,1)} %param.6), channel_id=1, source_target_pairs={{0,8},{1,9},{2,10},{3,11},{4,12},{5,13},{6,14},{7,15},{8,0},{9,1},... | collective-permute-start | bytes 344072 | tf_op jit(solution)/shard_map/ppermute | solution.py:40
  3.0 2.6 %collective-permute-start.2 = (bf16[8,7168]{1,0:T(8,128)(2,1)}, bf16[8,7168]{1,0:T(8,128)(2,1)S(1)}, u32[]{:S(2)}, u32[]{:S(2)}) collective-permute-start(bf16[8,7168]{1,0:T(8,128)(2,1)} %param.6), channel_id=1, source_target_pairs={{0,16},{1,17},{2,18},{3,19},{4,20},{5,21},{6,22},{7,23},{8,24},{9,... | collective-permute-start | bytes 344072 | tf_op jit(solution)/shard_map/ppermute | solution.py:40
  5.6 0.9 %fusion.12 = (bf16[8,3584]{1,0:T(8,128)(2,1)S(1)}, bf16[64,3584]{1,0:T(8,128)(2,1)S(1)}, bf16[8,3584]{1,0:T(8,128)(2,1)S(1)}) fusion(bf16[8,7168]{1,0:T(8,128)(2,1)} %param.6), kind=kLoop, calls=%fused_computation.44 | loop fusion | bytes 286720 | tf_op jit(solution)/shard_map/slice | solution.py:54
  6.5 0.8 select_reduce_fusion
  7.5 4.0 %collective-permute-start.5 = (bf16[8,128]{1,0:T(8,128)(2,1)S(1)}, bf16[8,128]{1,0:T(8,128)(2,1)S(1)}, u32[]{:S(2)}, u32[]{:S(2)}) collective-permute-start(bf16[8,128]{1,0:T(8,128)(2,1)S(1)} %maximum_maximum_fusion.1), channel_id=1, source_target_pairs={{0,24},{1,25},{2,26},{3,27},{4,28},{5,29},{6,30},{7,31},{8,16},{9,... | collective-permute-start | bytes 6152 | tf_op jit(solution)/shard_map/ppermute | solution.py:40
  12.1 2.9 %collective-permute-done.2 = bf16[8,7168]{1,0:T(8,128)(2,1)S(1)} collective-permute-done((bf16[8,7168]{1,0:T(8,128)(2,1)}, bf16[8,7168]{1,0:T(8,128)(2,1)S(1)}, u32[]{:S(2)}, u32[]{:S(2)}) %collective-permute-start.2) | collective-permute-done | bytes 114720 | tf_op jit(solution)/shard_map/ppermute | solution.py:40
  15.1 1.6 %collective-permute-start.10 = (bf16[32,3584]{1,0:T(8,128)(2,1)S(1)}, bf16[32,3584]{1,0:T(8,128)(2,1)S(1)}, u32[]{:S(2)}, u32[]{:S(2)}) collective-permute-start(bf16[32,3584]{1,0:T(8,128)(2,1)S(1)} %pad_maximum_fusion), channel_id=1, source_target_pairs={{0,2},{1,5},{2,0},{3,7},{4,6},{5,1},{6,4},{7,3},{8,10},{9,13},{10,... | collective-permute-start | bytes 688136 | tf_op jit(solution)/shard_map/ppermute | solution.py:40
  16.8 1.2 %collective-permute-start.6 = (bf16[32,3712]{1,0:T(8,128)(2,1)S(1)}, bf16[32,3712]{1,0:T(8,128)(2,1)S(1)}, u32[]{:S(2)}, u32[]{:S(2)}) collective-permute-start(bf16[32,3712]{1,0:T(8,128)(2,1)S(1)} %maximum_maximum_fusion), channel_id=1, source_target_pairs={{0,2},{1,5},{2,0},{3,7},{4,6},{5,1},{6,4},{7,3},{8,10},{9,13},{10,... | collective-permute-start | bytes 712712 | tf_op jit(solution)/shard_map/ppermute | solution.py:40
  18.0 4.3 %collective-permute-done.10 = bf16[32,3584]{1,0:T(8,128)(2,1)S(1)} collective-permute-done((bf16[32,3584]{1,0:T(8,128)(2,1)S(1)}, bf16[32,3584]{1,0:T(8,128)(2,1)S(1)}, u32[]{:S(2)}, u32[]{:S(2)}) %collective-permute-start.10) | collective-permute-done | bytes 229408 | tf_op jit(solution)/shard_map/ppermute | solution.py:40
  22.2 1.6 %collective-permute-start.11 = (bf16[64,3584]{1,0:T(8,128)(2,1)S(1)}, bf16[64,3584]{1,0:T(8,128)(2,1)S(1)}, u32[]{:S(2)}, u32[]{:S(2)}) collective-permute-start(bf16[64,3584]{1,0:T(8,128)(2,1)S(1)} %constant_dynamic-update-slice_fusion.1.x0), channel_id=1, source_target_pairs={{0,4},{1,3},{2,6},{3,1},{4,0},{5,7},{6,2},{7,5},{8,12},{9,11},{10,... | collective-permute-start | bytes 1376264 | tf_op jit(solution)/shard_map/ppermute | solution.py:40
  23.9 3.4 %collective-permute-done.6 = bf16[32,3712]{1,0:T(8,128)(2,1)S(1)} collective-permute-done((bf16[32,3712]{1,0:T(8,128)(2,1)S(1)}, bf16[32,3712]{1,0:T(8,128)(2,1)S(1)}, u32[]{:S(2)}, u32[]{:S(2)}) %collective-permute-start.6) | collective-permute-done | bytes 237600 | tf_op jit(solution)/shard_map/ppermute | solution.py:40
  27.3 1.6 %collective-permute-start.7 = (bf16[64,3712]{1,0:T(8,128)(2,1)S(1)}, bf16[64,3712]{1,0:T(8,128)(2,1)S(1)}, u32[]{:S(2)}, u32[]{:S(2)}) collective-permute-start(bf16[64,3712]{1,0:T(8,128)(2,1)S(1)} %constant_dynamic-update-slice_fusion.x0), channel_id=1, source_target_pairs={{0,4},{1,3},{2,6},{3,1},{4,0},{5,7},{6,2},{7,5},{8,12},{9,11},{10,... | collective-permute-start | bytes 1425416 | tf_op jit(solution)/shard_map/ppermute | solution.py:40
  29.0 1.8 %collective-permute-done.11.x1 = bf16[64,3584]{1,0:T(8,128)(2,1)S(1)} collective-permute-done((bf16[64,3584]{1,0:T(8,128)(2,1)S(1)}, bf16[64,3584]{1,0:T(8,128)(2,1)S(1)}, u32[]{:S(2)}, u32[]{:S(2)}) %collective-permute-start.11) | collective-permute-done | bytes 458784 | tf_op jit(solution)/shard_map/ppermute | solution.py:40
  31.3 4.8 %collective-permute-done.7.x1 = bf16[64,3712]{1,0:T(8,128)(2,1)S(1)} collective-permute-done((bf16[64,3712]{1,0:T(8,128)(2,1)S(1)}, bf16[64,3712]{1,0:T(8,128)(2,1)S(1)}, u32[]{:S(2)}, u32[]{:S(2)}) %collective-permute-start.7) | collective-permute-done | bytes 475168 | tf_op jit(solution)/shard_map/ppermute | solution.py:40
  36.1 4.3 %shard_map.64.acc = f32[256,1024]{1,0:T(8,128)S(1)} custom-call(bf16[64,3584]{1,0:T(8,128)(2,1)S(1)} %constant_dynamic-update-slice_fusion.1.x0, bf16[64,3584]{1,0:T(8,128)(2,1)S(1)} %collective-permute-done.11.x1, bf16[64,3584]{1,0:T(8,128)(2,1)S(1)} %collective-permute-done.12.x2, bf16[64,3584]{1,0:T(8,128)(2,1)S(1)} %collective-permute-done.13.x3, ...), custom_call_target="tpu_custom_call" | custom-call | flops 37580963840 | bytes 146800640 | tf_op jit(solution)/shard_map/pallas_call | solution.py:198
  40.4 7.2 %shard_map.65 = (f32[64,3584]{1,0:T(8,128)S(1)}, f32[64,3584]{1,0:T(8,128)S(1)}, bf16[64,3584]{1,0:T(8,128)(2,1)S(1)}, bf16[64,3584]{1,0:T(8,128)(2,1)S(1)}, f32...) custom-call(bf16[64,3712]{1,0:T(8,128)(2,1)S(1)} %constant_dynamic-up, ...), custom_call_target="tpu_custom_call" | custom-call | flops 3758096384 | bytes 14680064 | tf_op jit(solution)/shard_map/pallas_call | solution.py:214
  48.8 0.9 %collective-permute-done.15 = bf16[64,3584]{1,0:T(8,128)(2,1)S(1)} collective-permute-done((bf16[64,3584]{1,0:T(8,128)(2,1)S(1)}, bf16[64,3584]{1,0:T(8,128)(2,1)S(1)}, u32[]{:S(2)}, u32[]{:S(2)}) %collective-permute-start.15) | collective-permute-done | bytes 458784 | tf_op jit(solution)/shard_map/ppermute | solution.py:40
  49.7 1.6 %collective-permute-start.16 = (bf16[64,3584]{1,0:T(8,128)(2,1)S(1)}, bf16[64,3584]{1,0:T(8,128)(2,1)S(1)}, u32[]{:S(2)}, u32[]{:S(2)}) collective-permute-start(bf16[64,3584]{1,0:T(8,128)(2,1)S(1)} %add_convert_fusion.1), channel_id=1, source_target_pairs={{0,4},{1,3},{2,6},{3,1},{4,0},{5,7},{6,2},{7,5},{8,12},{9,11},{10,... | collective-permute-start | bytes 1376264 | tf_op jit(solution)/shard_map/ppermute | solution.py:40
  51.7 1.6 %collective-permute-start.23 = (bf16[64,3584]{1,0:T(8,128)(2,1)S(1)}, bf16[64,3584]{1,0:T(8,128)(2,1)S(1)}, u32[]{:S(2)}, u32[]{:S(2)}) collective-permute-start(bf16[64,3584]{1,0:T(8,128)(2,1)S(1)} %add_convert_fusion), channel_id=1, source_target_pairs={{0,4},{1,3},{2,6},{3,1},{4,0},{5,7},{6,2},{7,5},{8,12},{9,11},{10,... | collective-permute-start | bytes 1376264 | tf_op jit(solution)/shard_map/ppermute | solution.py:40
  53.3 4.9 %collective-permute-done.16 = bf16[64,3584]{1,0:T(8,128)(2,1)S(1)} collective-permute-done((bf16[64,3584]{1,0:T(8,128)(2,1)S(1)}, bf16[64,3584]{1,0:T(8,128)(2,1)S(1)}, u32[]{:S(2)}, u32[]{:S(2)}) %collective-permute-start.16) | collective-permute-done | bytes 458784 | tf_op jit(solution)/shard_map/ppermute | solution.py:40
  58.5 1.6 %collective-permute-start.17 = (bf16[32,3584]{1,0:T(8,128)(2,1)S(1)}, bf16[32,3584]{1,0:T(8,128)(2,1)S(1)}, u32[]{:S(2)}, u32[]{:S(2)}) collective-permute-start(bf16[32,3584]{1,0:T(8,128)(2,1)S(1)} %slice.127), channel_id=1, source_target_pairs={{0,2},{1,5},{2,0},{3,7},{4,6},{5,1},{6,4},{7,3},{8,10},{9,13},{10,... | collective-permute-start | bytes 688136 | tf_op jit(solution)/shard_map/ppermute | solution.py:40
  60.1 5.6 %collective-permute-done.23 = bf16[64,3584]{1,0:T(8,128)(2,1)S(1)} collective-permute-done((bf16[64,3584]{1,0:T(8,128)(2,1)S(1)}, bf16[64,3584]{1,0:T(8,128)(2,1)S(1)}, u32[]{:S(2)}, u32[]{:S(2)}) %collective-permute-start.23) | collective-permute-done | bytes 458784 | tf_op jit(solution)/shard_map/ppermute | solution.py:40
  65.8 1.6 %collective-permute-start.24 = (bf16[32,3584]{1,0:T(8,128)(2,1)S(1)}, bf16[32,3584]{1,0:T(8,128)(2,1)S(1)}, u32[]{:S(2)}, u32[]{:S(2)}) collective-permute-start(bf16[32,3584]{1,0:T(8,128)(2,1)S(1)} %slice.126), channel_id=1, source_target_pairs={{0,2},{1,5},{2,0},{3,7},{4,6},{5,1},{6,4},{7,3},{8,10},{9,13},{10,... | collective-permute-start | bytes 688136 | tf_op jit(solution)/shard_map/ppermute | solution.py:40
  67.5 0.6 collective-permute-start.18
  68.1 2.5 %collective-permute-start.20 = (bf16[8,3584]{1,0:T(8,128)(2,1)S(1)}, bf16[8,3584]{1,0:T(8,128)(2,1)S(1)}, u32[]{:S(2)}, u32[]{:S(2)}) collective-permute-start(bf16[8,3584]{1,0:T(8,128)(2,1)S(1)} %get-tuple-element.30), channel_id=1, source_target_pairs={{0,24},{1,25},{2,26},{3,27},{4,28},{5,29},{6,30},{7,31},{8,16},{9,... | collective-permute-start | bytes 172040 | tf_op jit(solution)/shard_map/ppermute | solution.py:40
  71.1 0.9 %collective-permute-done.24 = bf16[32,3584]{1,0:T(8,128)(2,1)S(1)} collective-permute-done((bf16[32,3584]{1,0:T(8,128)(2,1)S(1)}, bf16[32,3584]{1,0:T(8,128)(2,1)S(1)}, u32[]{:S(2)}, u32[]{:S(2)}) %collective-permute-start.24) | collective-permute-done | bytes 229408 | tf_op jit(solution)/shard_map/ppermute | solution.py:40
  72.0 0.7 collective-permute-start.25
  72.7 2.5 %collective-permute-start.27 = (bf16[8,3584]{1,0:T(8,128)(2,1)S(1)}, bf16[8,3584]{1,0:T(8,128)(2,1)S(1)}, u32[]{:S(2)}, u32[]{:S(2)}) collective-permute-start(bf16[8,3584]{1,0:T(8,128)(2,1)S(1)} %get-tuple-element.33), channel_id=1, source_target_pairs={{0,24},{1,25},{2,26},{3,27},{4,28},{5,29},{6,30},{7,31},{8,16},{9,... | collective-permute-start | bytes 172040 | tf_op jit(solution)/shard_map/ppermute | solution.py:40
  75.6 2.2 %collective-permute-done.19 = bf16[8,3584]{1,0:T(8,128)(2,1)S(1)} collective-permute-done((bf16[8,3584]{1,0:T(8,128)(2,1)S(1)}, bf16[8,3584]{1,0:T(8,128)(2,1)S(1)}, u32[]{:S(2)}, u32[]{:S(2)}) %collective-permute-start.19) | collective-permute-done | bytes 57376 | tf_op jit(solution)/shard_map/ppermute | solution.py:40
  77.8 1.0 %collective-permute-done.27 = bf16[8,3584]{1,0:T(8,128)(2,1)S(1)} collective-permute-done((bf16[8,3584]{1,0:T(8,128)(2,1)S(1)}, bf16[8,3584]{1,0:T(8,128)(2,1)S(1)}, u32[]{:S(2)}, u32[]{:S(2)}) %collective-permute-start.27) | collective-permute-done | bytes 57376 | tf_op jit(solution)/shard_map/ppermute | solution.py:40
  78.7 1.9 %collective-permute-done.26 = bf16[8,3584]{1,0:T(8,128)(2,1)S(1)} collective-permute-done((bf16[8,3584]{1,0:T(8,128)(2,1)S(1)}, bf16[8,3584]{1,0:T(8,128)(2,1)S(1)}, u32[]{:S(2)}, u32[]{:S(2)}) %collective-permute-start.26) | collective-permute-done | bytes 57376 | tf_op jit(solution)/shard_map/ppermute | solution.py:40
  80.7 0.7 pad_maximum_fusion.1
  (57 shorter events, 4.3 us)
Async XLA Ops:
  0.0 7.5 %collective-permute-start = (bf16[8,7168]{1,0:T(8,128)(2,1)}, bf16[8,7168]{1,0:T(8,128)(2,1)S(1)}, u32[]{:S(2)}, u32[]{:S(2)}) collective-permute-start(bf16[8,7168]{1,0:T(8,128)(2,1)} %param.6), channel_id=1, source_target_pairs={{0,8},{1,9},{2,10},{3,11},{4,12},{5,13},{6,14},{7,15},{8,0},{9,1},... | collective-permute-start | bytes 344072 | tf_op jit(solution)/shard_map/ppermute | solution.py:40
  3.0 12.0 %collective-permute-start.2 = (bf16[8,7168]{1,0:T(8,128)(2,1)}, bf16[8,7168]{1,0:T(8,128)(2,1)S(1)}, u32[]{:S(2)}, u32[]{:S(2)}) collective-permute-start(bf16[8,7168]{1,0:T(8,128)(2,1)} %param.6), channel_id=1, source_target_pairs={{0,16},{1,17},{2,18},{3,19},{4,20},{5,21},{6,22},{7,23},{8,24},{9,... | collective-permute-start | bytes 344072 | tf_op jit(solution)/shard_map/ppermute | solution.py:40
  5.6 9.5 %collective-permute-start.4 = (bf16[8,7168]{1,0:T(8,128)(2,1)}, bf16[8,7168]{1,0:T(8,128)(2,1)S(1)}, u32[]{:S(2)}, u32[]{:S(2)}) collective-permute-start(bf16[8,7168]{1,0:T(8,128)(2,1)} %param.6), channel_id=1, source_target_pairs={{0,24},{1,25},{2,26},{3,27},{4,28},{5,29},{6,30},{7,31},{8,16},{9,... | collective-permute-start | bytes 344072 | tf_op jit(solution)/shard_map/ppermute | solution.py:40
  7.5 9.2 %collective-permute-start.5 = (bf16[8,128]{1,0:T(8,128)(2,1)S(1)}, bf16[8,128]{1,0:T(8,128)(2,1)S(1)}, u32[]{:S(2)}, u32[]{:S(2)}) collective-permute-start(bf16[8,128]{1,0:T(8,128)(2,1)S(1)} %maximum_maximum_fusion.1), channel_id=1, source_target_pairs={{0,24},{1,25},{2,26},{3,27},{4,28},{5,29},{6,30},{7,31},{8,16},{9,... | collective-permute-start | bytes 6152 | tf_op jit(solution)/shard_map/ppermute | solution.py:40
  11.5 5.2 %collective-permute-start.3 = (bf16[8,128]{1,0:T(8,128)(2,1)S(1)}, bf16[8,128]{1,0:T(8,128)(2,1)S(1)}, u32[]{:S(2)}, u32[]{:S(2)}) collective-permute-start(bf16[8,128]{1,0:T(8,128)(2,1)S(1)} %maximum_maximum_fusion.1), channel_id=1, source_target_pairs={{0,16},{1,17},{2,18},{3,19},{4,20},{5,21},{6,22},{7,23},{8,24},{9,... | collective-permute-start | bytes 6152 | tf_op jit(solution)/shard_map/ppermute | solution.py:40
  11.5 5.2 %collective-permute-start.1 = (bf16[8,128]{1,0:T(8,128)(2,1)S(1)}, bf16[8,128]{1,0:T(8,128)(2,1)S(1)}, u32[]{:S(2)}, u32[]{:S(2)}) collective-permute-start(bf16[8,128]{1,0:T(8,128)(2,1)S(1)} %maximum_maximum_fusion.1), channel_id=1, source_target_pairs={{0,8},{1,9},{2,10},{3,11},{4,12},{5,13},{6,14},{7,15},{8,0},{9,1},... | collective-permute-start | bytes 6152 | tf_op jit(solution)/shard_map/ppermute | solution.py:40
  15.1 7.1 %collective-permute-start.10 = (bf16[32,3584]{1,0:T(8,128)(2,1)S(1)}, bf16[32,3584]{1,0:T(8,128)(2,1)S(1)}, u32[]{:S(2)}, u32[]{:S(2)}) collective-permute-start(bf16[32,3584]{1,0:T(8,128)(2,1)S(1)} %pad_maximum_fusion), channel_id=1, source_target_pairs={{0,2},{1,5},{2,0},{3,7},{4,6},{5,1},{6,4},{7,3},{8,10},{9,13},{10,... | collective-permute-start | bytes 688136 | tf_op jit(solution)/shard_map/ppermute | solution.py:40
  16.8 10.6 %collective-permute-start.6 = (bf16[32,3712]{1,0:T(8,128)(2,1)S(1)}, bf16[32,3712]{1,0:T(8,128)(2,1)S(1)}, u32[]{:S(2)}, u32[]{:S(2)}) collective-permute-start(bf16[32,3712]{1,0:T(8,128)(2,1)S(1)} %maximum_maximum_fusion), channel_id=1, source_target_pairs={{0,2},{1,5},{2,0},{3,7},{4,6},{5,1},{6,4},{7,3},{8,10},{9,13},{10,... | collective-permute-start | bytes 712712 | tf_op jit(solution)/shard_map/ppermute | solution.py:40
  22.2 8.5 %collective-permute-start.11 = (bf16[64,3584]{1,0:T(8,128)(2,1)S(1)}, bf16[64,3584]{1,0:T(8,128)(2,1)S(1)}, u32[]{:S(2)}, u32[]{:S(2)}) collective-permute-start(bf16[64,3584]{1,0:T(8,128)(2,1)S(1)} %constant_dynamic-update-slice_fusion.1.x0), channel_id=1, source_target_pairs={{0,4},{1,3},{2,6},{3,1},{4,0},{5,7},{6,2},{7,5},{8,12},{9,11},{10,... | collective-permute-start | bytes 1376264 | tf_op jit(solution)/shard_map/ppermute | solution.py:40
  27.3 8.7 %collective-permute-start.7 = (bf16[64,3712]{1,0:T(8,128)(2,1)S(1)}, bf16[64,3712]{1,0:T(8,128)(2,1)S(1)}, u32[]{:S(2)}, u32[]{:S(2)}) collective-permute-start(bf16[64,3712]{1,0:T(8,128)(2,1)S(1)} %constant_dynamic-update-slice_fusion.x0), channel_id=1, source_target_pairs={{0,4},{1,3},{2,6},{3,1},{4,0},{5,7},{6,2},{7,5},{8,12},{9,11},{10,... | collective-permute-start | bytes 1425416 | tf_op jit(solution)/shard_map/ppermute | solution.py:40
  29.0 7.1 %collective-permute-start.12 = (bf16[64,3584]{1,0:T(8,128)(2,1)S(1)}, bf16[64,3584]{1,0:T(8,128)(2,1)S(1)}, u32[]{:S(2)}, u32[]{:S(2)}) collective-permute-start(bf16[64,3584]{1,0:T(8,128)(2,1)S(1)} %constant_dynamic-update-slice_fusion.1.x0), channel_id=1, source_target_pairs={{0,1},{1,0},{2,3},{3,2},{4,5},{5,4},{6,7},{7,6},{8,9},{9,8},{10,11... | collective-permute-start | bytes 1376264 | tf_op jit(solution)/shard_map/ppermute | solution.py:40
  30.8 5.3 %collective-permute-start.13 = (bf16[64,3584]{1,0:T(8,128)(2,1)S(1)}, bf16[64,3584]{1,0:T(8,128)(2,1)S(1)}, u32[]{:S(2)}, u32[]{:S(2)}) collective-permute-start(bf16[64,3584]{1,0:T(8,128)(2,1)S(1)} %collective-permute-done.11.x1), channel_id=1, source_target_pairs={{0,1},{1,0},{2,3},{3,2},{4,5},{5,4},{6,7},{7,6},{8,9},{9,8},{10,11... | collective-permute-start | bytes 1376264 | tf_op jit(solution)/shard_map/ppermute | solution.py:40
  30.8 9.6 %collective-permute-start.8 = (bf16[64,3712]{1,0:T(8,128)(2,1)S(1)}, bf16[64,3712]{1,0:T(8,128)(2,1)S(1)}, u32[]{:S(2)}, u32[]{:S(2)}) collective-permute-start(bf16[64,3712]{1,0:T(8,128)(2,1)S(1)} %constant_dynamic-update-slice_fusion.x0), channel_id=1, source_target_pairs={{0,1},{1,0},{2,3},{3,2},{4,5},{5,4},{6,7},{7,6},{8,9},{9,8},{10,11... | collective-permute-start | bytes 1425416 | tf_op jit(solution)/shard_map/ppermute | solution.py:40
  36.1 4.3 %collective-permute-start.9 = (bf16[64,3712]{1,0:T(8,128)(2,1)S(1)}, bf16[64,3712]{1,0:T(8,128)(2,1)S(1)}, u32[]{:S(2)}, u32[]{:S(2)}) collective-permute-start(bf16[64,3712]{1,0:T(8,128)(2,1)S(1)} %collective-permute-done.7.x1), channel_id=1, source_target_pairs={{0,1},{1,0},{2,3},{3,2},{4,5},{5,4},{6,7},{7,6},{8,9},{9,8},{10,11... | collective-permute-start | bytes 1425416 | tf_op jit(solution)/shard_map/ppermute | solution.py:40
  47.6 2.0 %collective-permute-start.15 = (bf16[64,3584]{1,0:T(8,128)(2,1)S(1)}, bf16[64,3584]{1,0:T(8,128)(2,1)S(1)}, u32[]{:S(2)}, u32[]{:S(2)}) collective-permute-start(bf16[64,3584]{1,0:T(8,128)(2,1)S(1)} %get-tuple-element.20), channel_id=1, source_target_pairs={{0,1},{1,0},{2,3},{3,2},{4,5},{5,4},{6,7},{7,6},{8,9},{9,8},{10,11... | collective-permute-start | bytes 1376264 | tf_op jit(solution)/shard_map/ppermute | solution.py:40
  48.2 5.1 %collective-permute-start.14 = (bf16[64,3584]{1,0:T(8,128)(2,1)S(1)}, bf16[64,3584]{1,0:T(8,128)(2,1)S(1)}, u32[]{:S(2)}, u32[]{:S(2)}) collective-permute-start(bf16[64,3584]{1,0:T(8,128)(2,1)S(1)} %get-tuple-element.18), channel_id=1, source_target_pairs={{0,1},{1,0},{2,3},{3,2},{4,5},{5,4},{6,7},{7,6},{8,9},{9,8},{10,11... | collective-permute-start | bytes 1376264 | tf_op jit(solution)/shard_map/ppermute | solution.py:40
  48.3 11.8 %collective-permute-start.21 = (bf16[64,3584]{1,0:T(8,128)(2,1)S(1)}, bf16[64,3584]{1,0:T(8,128)(2,1)S(1)}, u32[]{:S(2)}, u32[]{:S(2)}) collective-permute-start(bf16[64,3584]{1,0:T(8,128)(2,1)S(1)} %get-tuple-element.22), channel_id=1, source_target_pairs={{0,1},{1,0},{2,3},{3,2},{4,5},{5,4},{6,7},{7,6},{8,9},{9,8},{10,11... | collective-permute-start | bytes 1376264 | tf_op jit(solution)/shard_map/ppermute | solution.py:40
  48.7 2.9 %collective-permute-start.22 = (bf16[64,3584]{1,0:T(8,128)(2,1)S(1)}, bf16[64,3584]{1,0:T(8,128)(2,1)S(1)}, u32[]{:S(2)}, u32[]{:S(2)}) collective-permute-start(bf16[64,3584]{1,0:T(8,128)(2,1)S(1)} %get-tuple-element.24), channel_id=1, source_target_pairs={{0,1},{1,0},{2,3},{3,2},{4,5},{5,4},{6,7},{7,6},{8,9},{9,8},{10,11... | collective-permute-start | bytes 1376264 | tf_op jit(solution)/shard_map/ppermute | solution.py:40
  49.7 8.5 %collective-permute-start.16 = (bf16[64,3584]{1,0:T(8,128)(2,1)S(1)}, bf16[64,3584]{1,0:T(8,128)(2,1)S(1)}, u32[]{:S(2)}, u32[]{:S(2)}) collective-permute-start(bf16[64,3584]{1,0:T(8,128)(2,1)S(1)} %add_convert_fusion.1), channel_id=1, source_target_pairs={{0,4},{1,3},{2,6},{3,1},{4,0},{5,7},{6,2},{7,5},{8,12},{9,11},{10,... | collective-permute-start | bytes 1376264 | tf_op jit(solution)/shard_map/ppermute | solution.py:40
  51.7 13.9 %collective-permute-start.23 = (bf16[64,3584]{1,0:T(8,128)(2,1)S(1)}, bf16[64,3584]{1,0:T(8,128)(2,1)S(1)}, u32[]{:S(2)}, u32[]{:S(2)}) collective-permute-start(bf16[64,3584]{1,0:T(8,128)(2,1)S(1)} %add_convert_fusion), channel_id=1, source_target_pairs={{0,4},{1,3},{2,6},{3,1},{4,0},{5,7},{6,2},{7,5},{8,12},{9,11},{10,... | collective-permute-start | bytes 1376264 | tf_op jit(solution)/shard_map/ppermute | solution.py:40
  58.5 9.0 %collective-permute-start.17 = (bf16[32,3584]{1,0:T(8,128)(2,1)S(1)}, bf16[32,3584]{1,0:T(8,128)(2,1)S(1)}, u32[]{:S(2)}, u32[]{:S(2)}) collective-permute-start(bf16[32,3584]{1,0:T(8,128)(2,1)S(1)} %slice.127), channel_id=1, source_target_pairs={{0,2},{1,5},{2,0},{3,7},{4,6},{5,1},{6,4},{7,3},{8,10},{9,13},{10,... | collective-permute-start | bytes 688136 | tf_op jit(solution)/shard_map/ppermute | solution.py:40
  65.8 6.1 %collective-permute-start.24 = (bf16[32,3584]{1,0:T(8,128)(2,1)S(1)}, bf16[32,3584]{1,0:T(8,128)(2,1)S(1)}, u32[]{:S(2)}, u32[]{:S(2)}) collective-permute-start(bf16[32,3584]{1,0:T(8,128)(2,1)S(1)} %slice.126), channel_id=1, source_target_pairs={{0,2},{1,5},{2,0},{3,7},{4,6},{5,1},{6,4},{7,3},{8,10},{9,13},{10,... | collective-permute-start | bytes 688136 | tf_op jit(solution)/shard_map/ppermute | solution.py:40
  67.5 7.7 %collective-permute-start.18 = (bf16[8,3584]{1,0:T(8,128)(2,1)S(1)}, bf16[8,3584]{1,0:T(8,128)(2,1)S(1)}, u32[]{:S(2)}, u32[]{:S(2)}) collective-permute-start(bf16[8,3584]{1,0:T(8,128)(2,1)S(1)} %get-tuple-element.29), channel_id=1, source_target_pairs={{0,8},{1,9},{2,10},{3,11},{4,12},{5,13},{6,14},{7,15},{8,0},{9,1},... | collective-permute-start | bytes 172040 | tf_op jit(solution)/shard_map/ppermute | solution.py:40
  68.1 7.4 %collective-permute-start.20 = (bf16[8,3584]{1,0:T(8,128)(2,1)S(1)}, bf16[8,3584]{1,0:T(8,128)(2,1)S(1)}, u32[]{:S(2)}, u32[]{:S(2)}) collective-permute-start(bf16[8,3584]{1,0:T(8,128)(2,1)S(1)} %get-tuple-element.30), channel_id=1, source_target_pairs={{0,24},{1,25},{2,26},{3,27},{4,28},{5,29},{6,30},{7,31},{8,16},{9,... | collective-permute-start | bytes 172040 | tf_op jit(solution)/shard_map/ppermute | solution.py:40
  70.7 7.1 %collective-permute-start.19 = (bf16[8,3584]{1,0:T(8,128)(2,1)S(1)}, bf16[8,3584]{1,0:T(8,128)(2,1)S(1)}, u32[]{:S(2)}, u32[]{:S(2)}) collective-permute-start(bf16[8,3584]{1,0:T(8,128)(2,1)S(1)} %get-tuple-element.31), channel_id=1, source_target_pairs={{0,16},{1,17},{2,18},{3,19},{4,20},{5,21},{6,22},{7,23},{8,24},{9,... | collective-permute-start | bytes 172040 | tf_op jit(solution)/shard_map/ppermute | solution.py:40
  72.0 5.8 %collective-permute-start.25 = (bf16[8,3584]{1,0:T(8,128)(2,1)S(1)}, bf16[8,3584]{1,0:T(8,128)(2,1)S(1)}, u32[]{:S(2)}, u32[]{:S(2)}) collective-permute-start(bf16[8,3584]{1,0:T(8,128)(2,1)S(1)} %get-tuple-element.32), channel_id=1, source_target_pairs={{0,8},{1,9},{2,10},{3,11},{4,12},{5,13},{6,14},{7,15},{8,0},{9,1},... | collective-permute-start | bytes 172040 | tf_op jit(solution)/shard_map/ppermute | solution.py:40
  72.7 6.1 %collective-permute-start.27 = (bf16[8,3584]{1,0:T(8,128)(2,1)S(1)}, bf16[8,3584]{1,0:T(8,128)(2,1)S(1)}, u32[]{:S(2)}, u32[]{:S(2)}) collective-permute-start(bf16[8,3584]{1,0:T(8,128)(2,1)S(1)} %get-tuple-element.33), channel_id=1, source_target_pairs={{0,24},{1,25},{2,26},{3,27},{4,28},{5,29},{6,30},{7,31},{8,16},{9,... | collective-permute-start | bytes 172040 | tf_op jit(solution)/shard_map/ppermute | solution.py:40
  75.2 5.5 %collective-permute-start.26 = (bf16[8,3584]{1,0:T(8,128)(2,1)S(1)}, bf16[8,3584]{1,0:T(8,128)(2,1)S(1)}, u32[]{:S(2)}, u32[]{:S(2)}) collective-permute-start(bf16[8,3584]{1,0:T(8,128)(2,1)S(1)} %get-tuple-element.34), channel_id=1, source_target_pairs={{0,16},{1,17},{2,18},{3,19},{4,20},{5,21},{6,22},{7,23},{8,24},{9,... | collective-permute-start | bytes 172040 | tf_op jit(solution)/shard_map/ppermute | solution.py:40

commit v5 on v4

--- a/solution.py
+++ b/solution.py
@@ -13,7 +13,7 @@
 CUT = 7
 DOWN = 7
 AHEAD = 3
-FIRST = 2
+FIRST = 5
 SECOND = 30
 WEIGHT = 20
 F32 = jnp.float32
@@ -257,7 +257,7 @@
     kb = width // (4 if rows * 2 * n_wide <= 256 else 14)
     cut = CUT * (width // kb) // 14 * kb
     down = DOWN * (width // kb) // 14 * kb
-    acc, two = gather(tokens, extra, cut, lambda one: first_part(one, w_gate, w_up, cut, kb), plan)
+    acc, two = gather(tokens, extra, cut, lambda one: first_part(one, w_gate, w_up, cut, cut // 7), plan)
     pieces = second_part(two, mask, acc, w_gate, w_up, w_down, cut, down, kb)
     core = plan[2]
     far = (pieces[1] + move(pieces[3], core).astype(F32)).astype(BF16)

time: 81.6 us -> 81.2 us (level)
  no operation moved by 1% of the time
where the time goes in v5:
time: 81.2 us; the launch traced here: 81 us
  waiting for transfers between devices  34.8 us (43%)
  starting transfers between devices  31.4 us (39%)
  Pallas kernels  11.1 us (14%)
  other arithmetic  2.27 us (3%)
  local copies, waits for them, and re-layouts  1.13 us (1%)
    ppermute x28, waiting for transfers between devices, move(): return lax.ppermute(x, AXES, perm)  34.8 us
    ppermute x28, starting transfers between devices, move(): return lax.ppermute(x, AXES, perm)  31.4 us
    pallas_call x1, Pallas kernels, second_part(): pl.pallas_call(functools.partial(second_kernel, skip, kb), in_specs=in_vm...  7.2 us
    pallas_call x1, Pallas kernels, first_part(): pl.pallas_call(functools.partial(first_kernel, 0, kb), in_specs=in_vmem(4...  3.9 us
  transfers between devices with their start and end apart: 28, of which 13 were waited for; matrix products, arithmetic and copies ran while one was open for 3% of the time, Pallas kernels for 5%

profile of v5, /device:TPU:0, one launch (start us, length us, event | category | flops | bytes accessed | tf_op | source)
XLA Modules:
  0.0 81.0 jit_solution(808358730596211996)
XLA Ops:
  0.0 3.0 %collective-permute-start = (bf16[8,7168]{1,0:T(8,128)(2,1)}, bf16[8,7168]{1,0:T(8,128)(2,1)S(1)}, u32[]{:S(2)}, u32[]{:S(2)}) collective-permute-start(bf16[8,7168]{1,0:T(8,128)(2,1)} %param.6), channel_id=1, source_target_pairs={{0,8},{1,9},{2,10},{3,11},{4,12},{5,13},{6,14},{7,15},{8,0},{9,1},... | collective-permute-start | bytes 344072 | tf_op jit(solution)/shard_map/ppermute | solution.py:40
  3.0 2.6 %collective-permute-start.2 = (bf16[8,7168]{1,0:T(8,128)(2,1)}, bf16[8,7168]{1,0:T(8,128)(2,1)S(1)}, u32[]{:S(2)}, u32[]{:S(2)}) collective-permute-start(bf16[8,7168]{1,0:T(8,128)(2,1)} %param.6), channel_id=1, source_target_pairs={{0,16},{1,17},{2,18},{3,19},{4,20},{5,21},{6,22},{7,23},{8,24},{9,... | collective-permute-start | bytes 344072 | tf_op jit(solution)/shard_map/ppermute | solution.py:40
  5.6 0.9 %fusion.12 = (bf16[8,3584]{1,0:T(8,128)(2,1)S(1)}, bf16[64,3584]{1,0:T(8,128)(2,1)S(1)}, bf16[8,3584]{1,0:T(8,128)(2,1)S(1)}) fusion(bf16[8,7168]{1,0:T(8,128)(2,1)} %param.6), kind=kLoop, calls=%fused_computation.44 | loop fusion | bytes 286720 | tf_op jit(solution)/shard_map/slice | solution.py:54
  6.5 0.8 select_reduce_fusion
  7.5 4.0 %collective-permute-start.5 = (bf16[8,128]{1,0:T(8,128)(2,1)S(1)}, bf16[8,128]{1,0:T(8,128)(2,1)S(1)}, u32[]{:S(2)}, u32[]{:S(2)}) collective-permute-start(bf16[8,128]{1,0:T(8,128)(2,1)S(1)} %maximum_maximum_fusion.1), channel_id=1, source_target_pairs={{0,24},{1,25},{2,26},{3,27},{4,28},{5,29},{6,30},{7,31},{8,16},{9,... | collective-permute-start | bytes 6152 | tf_op jit(solution)/shard_map/ppermute | solution.py:40
  12.1 2.9 %collective-permute-done.2 = bf16[8,7168]{1,0:T(8,128)(2,1)S(1)} collective-permute-done((bf16[8,7168]{1,0:T(8,128)(2,1)}, bf16[8,7168]{1,0:T(8,128)(2,1)S(1)}, u32[]{:S(2)}, u32[]{:S(2)}) %collective-permute-start.2) | collective-permute-done | bytes 114720 | tf_op jit(solution)/shard_map/ppermute | solution.py:40
  15.1 1.6 %collective-permute-start.10 = (bf16[32,3584]{1,0:T(8,128)(2,1)S(1)}, bf16[32,3584]{1,0:T(8,128)(2,1)S(1)}, u32[]{:S(2)}, u32[]{:S(2)}) collective-permute-start(bf16[32,3584]{1,0:T(8,128)(2,1)S(1)} %pad_maximum_fusion), channel_id=1, source_target_pairs={{0,2},{1,5},{2,0},{3,7},{4,6},{5,1},{6,4},{7,3},{8,10},{9,13},{10,... | collective-permute-start | bytes 688136 | tf_op jit(solution)/shard_map/ppermute | solution.py:40
  16.8 1.2 %collective-permute-start.6 = (bf16[32,3712]{1,0:T(8,128)(2,1)S(1)}, bf16[32,3712]{1,0:T(8,128)(2,1)S(1)}, u32[]{:S(2)}, u32[]{:S(2)}) collective-permute-start(bf16[32,3712]{1,0:T(8,128)(2,1)S(1)} %maximum_maximum_fusion), channel_id=1, source_target_pairs={{0,2},{1,5},{2,0},{3,7},{4,6},{5,1},{6,4},{7,3},{8,10},{9,13},{10,... | collective-permute-start | bytes 712712 | tf_op jit(solution)/shard_map/ppermute | solution.py:40
  18.0 4.3 %collective-permute-done.10 = bf16[32,3584]{1,0:T(8,128)(2,1)S(1)} collective-permute-done((bf16[32,3584]{1,0:T(8,128)(2,1)S(1)}, bf16[32,3584]{1,0:T(8,128)(2,1)S(1)}, u32[]{:S(2)}, u32[]{:S(2)}) %collective-permute-start.10) | collective-permute-done | bytes 229408 | tf_op jit(solution)/shard_map/ppermute | solution.py:40
  22.2 1.6 %collective-permute-start.11 = (bf16[64,3584]{1,0:T(8,128)(2,1)S(1)}, bf16[64,3584]{1,0:T(8,128)(2,1)S(1)}, u32[]{:S(2)}, u32[]{:S(2)}) collective-permute-start(bf16[64,3584]{1,0:T(8,128)(2,1)S(1)} %constant_dynamic-update-slice_fusion.1.x0), channel_id=1, source_target_pairs={{0,4},{1,3},{2,6},{3,1},{4,0},{5,7},{6,2},{7,5},{8,12},{9,11},{10,... | collective-permute-start | bytes 1376264 | tf_op jit(solution)/shard_map/ppermute | solution.py:40
  23.9 3.4 %collective-permute-done.6 = bf16[32,3712]{1,0:T(8,128)(2,1)S(1)} collective-permute-done((bf16[32,3712]{1,0:T(8,128)(2,1)S(1)}, bf16[32,3712]{1,0:T(8,128)(2,1)S(1)}, u32[]{:S(2)}, u32[]{:S(2)}) %collective-permute-start.6) | collective-permute-done | bytes 237600 | tf_op jit(solution)/shard_map/ppermute | solution.py:40
  27.3 1.6 %collective-permute-start.7 = (bf16[64,3712]{1,0:T(8,128)(2,1)S(1)}, bf16[64,3712]{1,0:T(8,128)(2,1)S(1)}, u32[]{:S(2)}, u32[]{:S(2)}) collective-permute-start(bf16[64,3712]{1,0:T(8,128)(2,1)S(1)} %constant_dynamic-update-slice_fusion.x0), channel_id=1, source_target_pairs={{0,4},{1,3},{2,6},{3,1},{4,0},{5,7},{6,2},{7,5},{8,12},{9,11},{10,... | collective-permute-start | bytes 1425416 | tf_op jit(solution)/shard_map/ppermute | solution.py:40
  29.0 1.8 %collective-permute-done.11.x1 = bf16[64,3584]{1,0:T(8,128)(2,1)S(1)} collective-permute-done((bf16[64,3584]{1,0:T(8,128)(2,1)S(1)}, bf16[64,3584]{1,0:T(8,128)(2,1)S(1)}, u32[]{:S(2)}, u32[]{:S(2)}) %collective-permute-start.11) | collective-permute-done | bytes 458784 | tf_op jit(solution)/shard_map/ppermute | solution.py:40
  31.3 4.8 %collective-permute-done.7.x1 = bf16[64,3712]{1,0:T(8,128)(2,1)S(1)} collective-permute-done((bf16[64,3712]{1,0:T(8,128)(2,1)S(1)}, bf16[64,3712]{1,0:T(8,128)(2,1)S(1)}, u32[]{:S(2)}, u32[]{:S(2)}) %collective-permute-start.7) | collective-permute-done | bytes 475168 | tf_op jit(solution)/shard_map/ppermute | solution.py:40
  36.1 3.9 %shard_map.64.acc = f32[256,1024]{1,0:T(8,128)S(1)} custom-call(bf16[64,3584]{1,0:T(8,128)(2,1)S(1)} %constant_dynamic-update-slice_fusion.1.x0, bf16[64,3584]{1,0:T(8,128)(2,1)S(1)} %collective-permute-done.11.x1, bf16[64,3584]{1,0:T(8,128)(2,1)S(1)} %collective-permute-done.12.x2, bf16[64,3584]{1,0:T(8,128)(2,1)S(1)} %collective-permute-done.13.x3, ...), custom_call_target="tpu_custom_call" | custom-call | flops 37580963840 | bytes 146800640 | tf_op jit(solution)/shard_map/pallas_call | solution.py:198
  40.0 7.2 %shard_map.65 = (f32[64,3584]{1,0:T(8,128)S(1)}, f32[64,3584]{1,0:T(8,128)S(1)}, bf16[64,3584]{1,0:T(8,128)(2,1)S(1)}, bf16[64,3584]{1,0:T(8,128)(2,1)S(1)}, f32...) custom-call(bf16[64,3712]{1,0:T(8,128)(2,1)S(1)} %constant_dynamic-up, ...), custom_call_target="tpu_custom_call" | custom-call | flops 3758096384 | bytes 14680064 | tf_op jit(solution)/shard_map/pallas_call | solution.py:214
  48.4 0.9 %collective-permute-done.15 = bf16[64,3584]{1,0:T(8,128)(2,1)S(1)} collective-permute-done((bf16[64,3584]{1,0:T(8,128)(2,1)S(1)}, bf16[64,3584]{1,0:T(8,128)(2,1)S(1)}, u32[]{:S(2)}, u32[]{:S(2)}) %collective-permute-start.15) | collective-permute-done | bytes 458784 | tf_op jit(solution)/shard_map/ppermute | solution.py:40
  49.3 1.6 %collective-permute-start.16 = (bf16[64,3584]{1,0:T(8,128)(2,1)S(1)}, bf16[64,3584]{1,0:T(8,128)(2,1)S(1)}, u32[]{:S(2)}, u32[]{:S(2)}) collective-permute-start(bf16[64,3584]{1,0:T(8,128)(2,1)S(1)} %add_convert_fusion.1), channel_id=1, source_target_pairs={{0,4},{1,3},{2,6},{3,1},{4,0},{5,7},{6,2},{7,5},{8,12},{9,11},{10,... | collective-permute-start | bytes 1376264 | tf_op jit(solution)/shard_map/ppermute | solution.py:40
  51.3 1.6 %collective-permute-start.23 = (bf16[64,3584]{1,0:T(8,128)(2,1)S(1)}, bf16[64,3584]{1,0:T(8,128)(2,1)S(1)}, u32[]{:S(2)}, u32[]{:S(2)}) collective-permute-start(bf16[64,3584]{1,0:T(8,128)(2,1)S(1)} %add_convert_fusion), channel_id=1, source_target_pairs={{0,4},{1,3},{2,6},{3,1},{4,0},{5,7},{6,2},{7,5},{8,12},{9,11},{10,... | collective-permute-start | bytes 1376264 | tf_op jit(solution)/shard_map/ppermute | solution.py:40
  52.9 4.9 %collective-permute-done.16 = bf16[64,3584]{1,0:T(8,128)(2,1)S(1)} collective-permute-done((bf16[64,3584]{1,0:T(8,128)(2,1)S(1)}, bf16[64,3584]{1,0:T(8,128)(2,1)S(1)}, u32[]{:S(2)}, u32[]{:S(2)}) %collective-permute-start.16) | collective-permute-done | bytes 458784 | tf_op jit(solution)/shard_map/ppermute | solution.py:40
  58.1 1.6 %collective-permute-start.17 = (bf16[32,3584]{1,0:T(8,128)(2,1)S(1)}, bf16[32,3584]{1,0:T(8,128)(2,1)S(1)}, u32[]{:S(2)}, u32[]{:S(2)}) collective-permute-start(bf16[32,3584]{1,0:T(8,128)(2,1)S(1)} %slice.127), channel_id=1, source_target_pairs={{0,2},{1,5},{2,0},{3,7},{4,6},{5,1},{6,4},{7,3},{8,10},{9,13},{10,... | collective-permute-start | bytes 688136 | tf_op jit(solution)/shard_map/ppermute | solution.py:40
  59.7 5.6 %collective-permute-done.23 = bf16[64,3584]{1,0:T(8,128)(2,1)S(1)} collective-permute-done((bf16[64,3584]{1,0:T(8,128)(2,1)S(1)}, bf16[64,3584]{1,0:T(8,128)(2,1)S(1)}, u32[]{:S(2)}, u32[]{:S(2)}) %collective-permute-start.23) | collective-permute-done | bytes 458784 | tf_op jit(solution)/shard_map/ppermute | solution.py:40
  65.4 1.6 %collective-permute-start.24 = (bf16[32,3584]{1,0:T(8,128)(2,1)S(1)}, bf16[32,3584]{1,0:T(8,128)(2,1)S(1)}, u32[]{:S(2)}, u32[]{:S(2)}) collective-permute-start(bf16[32,3584]{1,0:T(8,128)(2,1)S(1)} %slice.126), channel_id=1, source_target_pairs={{0,2},{1,5},{2,0},{3,7},{4,6},{5,1},{6,4},{7,3},{8,10},{9,13},{10,... | collective-permute-start | bytes 688136 | tf_op jit(solution)/shard_map/ppermute | solution.py:40
  67.1 0.6 collective-permute-start.18
  67.7 2.5 %collective-permute-start.20 = (bf16[8,3584]{1,0:T(8,128)(2,1)S(1)}, bf16[8,3584]{1,0:T(8,128)(2,1)S(1)}, u32[]{:S(2)}, u32[]{:S(2)}) collective-permute-start(bf16[8,3584]{1,0:T(8,128)(2,1)S(1)} %get-tuple-element.30), channel_id=1, source_target_pairs={{0,24},{1,25},{2,26},{3,27},{4,28},{5,29},{6,30},{7,31},{8,16},{9,... | collective-permute-start | bytes 172040 | tf_op jit(solution)/shard_map/ppermute | solution.py:40
  70.7 0.9 %collective-permute-done.24 = bf16[32,3584]{1,0:T(8,128)(2,1)S(1)} collective-permute-done((bf16[32,3584]{1,0:T(8,128)(2,1)S(1)}, bf16[32,3584]{1,0:T(8,128)(2,1)S(1)}, u32[]{:S(2)}, u32[]{:S(2)}) %collective-permute-start.24) | collective-permute-done | bytes 229408 | tf_op jit(solution)/shard_map/ppermute | solution.py:40
  71.6 0.7 collective-permute-start.25
  72.3 2.5 %collective-permute-start.27 = (bf16[8,3584]{1,0:T(8,128)(2,1)S(1)}, bf16[8,3584]{1,0:T(8,128)(2,1)S(1)}, u32[]{:S(2)}, u32[]{:S(2)}) collective-permute-start(bf16[8,3584]{1,0:T(8,128)(2,1)S(1)} %get-tuple-element.33), channel_id=1, source_target_pairs={{0,24},{1,25},{2,26},{3,27},{4,28},{5,29},{6,30},{7,31},{8,16},{9,... | collective-permute-start | bytes 172040 | tf_op jit(solution)/shard_map/ppermute | solution.py:40
  75.2 2.2 %collective-permute-done.19 = bf16[8,3584]{1,0:T(8,128)(2,1)S(1)} collective-permute-done((bf16[8,3584]{1,0:T(8,128)(2,1)S(1)}, bf16[8,3584]{1,0:T(8,128)(2,1)S(1)}, u32[]{:S(2)}, u32[]{:S(2)}) %collective-permute-start.19) | collective-permute-done | bytes 57376 | tf_op jit(solution)/shard_map/ppermute | solution.py:40
  77.4 1.0 %collective-permute-done.27 = bf16[8,3584]{1,0:T(8,128)(2,1)S(1)} collective-permute-done((bf16[8,3584]{1,0:T(8,128)(2,1)S(1)}, bf16[8,3584]{1,0:T(8,128)(2,1)S(1)}, u32[]{:S(2)}, u32[]{:S(2)}) %collective-permute-start.27) | collective-permute-done | bytes 57376 | tf_op jit(solution)/shard_map/ppermute | solution.py:40
  78.3 1.9 %collective-permute-done.26 = bf16[8,3584]{1,0:T(8,128)(2,1)S(1)} collective-permute-done((bf16[8,3584]{1,0:T(8,128)(2,1)S(1)}, bf16[8,3584]{1,0:T(8,128)(2,1)S(1)}, u32[]{:S(2)}, u32[]{:S(2)}) %collective-permute-start.26) | collective-permute-done | bytes 57376 | tf_op jit(solution)/shard_map/ppermute | solution.py:40
  80.3 0.7 pad_maximum_fusion.1
  (57 shorter events, 4.3 us)
Async XLA Ops:
  0.0 7.5 %collective-permute-start = (bf16[8,7168]{1,0:T(8,128)(2,1)}, bf16[8,7168]{1,0:T(8,128)(2,1)S(1)}, u32[]{:S(2)}, u32[]{:S(2)}) collective-permute-start(bf16[8,7168]{1,0:T(8,128)(2,1)} %param.6), channel_id=1, source_target_pairs={{0,8},{1,9},{2,10},{3,11},{4,12},{5,13},{6,14},{7,15},{8,0},{9,1},... | collective-permute-start | bytes 344072 | tf_op jit(solution)/shard_map/ppermute | solution.py:40
  3.0 12.0 %collective-permute-start.2 = (bf16[8,7168]{1,0:T(8,128)(2,1)}, bf16[8,7168]{1,0:T(8,128)(2,1)S(1)}, u32[]{:S(2)}, u32[]{:S(2)}) collective-permute-start(bf16[8,7168]{1,0:T(8,128)(2,1)} %param.6), channel_id=1, source_target_pairs={{0,16},{1,17},{2,18},{3,19},{4,20},{5,21},{6,22},{7,23},{8,24},{9,... | collective-permute-start | bytes 344072 | tf_op jit(solution)/shard_map/ppermute | solution.py:40
  5.6 9.5 %collective-permute-start.4 = (bf16[8,7168]{1,0:T(8,128)(2,1)}, bf16[8,7168]{1,0:T(8,128)(2,1)S(1)}, u32[]{:S(2)}, u32[]{:S(2)}) collective-permute-start(bf16[8,7168]{1,0:T(8,128)(2,1)} %param.6), channel_id=1, source_target_pairs={{0,24},{1,25},{2,26},{3,27},{4,28},{5,29},{6,30},{7,31},{8,16},{9,... | collective-permute-start | bytes 344072 | tf_op jit(solution)/shard_map/ppermute | solution.py:40
  7.5 9.2 %collective-permute-start.5 = (bf16[8,128]{1,0:T(8,128)(2,1)S(1)}, bf16[8,128]{1,0:T(8,128)(2,1)S(1)}, u32[]{:S(2)}, u32[]{:S(2)}) collective-permute-start(bf16[8,128]{1,0:T(8,128)(2,1)S(1)} %maximum_maximum_fusion.1), channel_id=1, source_target_pairs={{0,24},{1,25},{2,26},{3,27},{4,28},{5,29},{6,30},{7,31},{8,16},{9,... | collective-permute-start | bytes 6152 | tf_op jit(solution)/shard_map/ppermute | solution.py:40
  11.5 5.2 %collective-permute-start.3 = (bf16[8,128]{1,0:T(8,128)(2,1)S(1)}, bf16[8,128]{1,0:T(8,128)(2,1)S(1)}, u32[]{:S(2)}, u32[]{:S(2)}) collective-permute-start(bf16[8,128]{1,0:T(8,128)(2,1)S(1)} %maximum_maximum_fusion.1), channel_id=1, source_target_pairs={{0,16},{1,17},{2,18},{3,19},{4,20},{5,21},{6,22},{7,23},{8,24},{9,... | collective-permute-start | bytes 6152 | tf_op jit(solution)/shard_map/ppermute | solution.py:40
  11.5 5.2 %collective-permute-start.1 = (bf16[8,128]{1,0:T(8,128)(2,1)S(1)}, bf16[8,128]{1,0:T(8,128)(2,1)S(1)}, u32[]{:S(2)}, u32[]{:S(2)}) collective-permute-start(bf16[8,128]{1,0:T(8,128)(2,1)S(1)} %maximum_maximum_fusion.1), channel_id=1, source_target_pairs={{0,8},{1,9},{2,10},{3,11},{4,12},{5,13},{6,14},{7,15},{8,0},{9,1},... | collective-permute-start | bytes 6152 | tf_op jit(solution)/shard_map/ppermute | solution.py:40
  15.1 7.1 %collective-permute-start.10 = (bf16[32,3584]{1,0:T(8,128)(2,1)S(1)}, bf16[32,3584]{1,0:T(8,128)(2,1)S(1)}, u32[]{:S(2)}, u32[]{:S(2)}) collective-permute-start(bf16[32,3584]{1,0:T(8,128)(2,1)S(1)} %pad_maximum_fusion), channel_id=1, source_target_pairs={{0,2},{1,5},{2,0},{3,7},{4,6},{5,1},{6,4},{7,3},{8,10},{9,13},{10,... | collective-permute-start | bytes 688136 | tf_op jit(solution)/shard_map/ppermute | solution.py:40
  16.8 10.6 %collective-permute-start.6 = (bf16[32,3712]{1,0:T(8,128)(2,1)S(1)}, bf16[32,3712]{1,0:T(8,128)(2,1)S(1)}, u32[]{:S(2)}, u32[]{:S(2)}) collective-permute-start(bf16[32,3712]{1,0:T(8,128)(2,1)S(1)} %maximum_maximum_fusion), channel_id=1, source_target_pairs={{0,2},{1,5},{2,0},{3,7},{4,6},{5,1},{6,4},{7,3},{8,10},{9,13},{10,... | collective-permute-start | bytes 712712 | tf_op jit(solution)/shard_map/ppermute | solution.py:40
  22.2 8.5 %collective-permute-start.11 = (bf16[64,3584]{1,0:T(8,128)(2,1)S(1)}, bf16[64,3584]{1,0:T(8,128)(2,1)S(1)}, u32[]{:S(2)}, u32[]{:S(2)}) collective-permute-start(bf16[64,3584]{1,0:T(8,128)(2,1)S(1)} %constant_dynamic-update-slice_fusion.1.x0), channel_id=1, source_target_pairs={{0,4},{1,3},{2,6},{3,1},{4,0},{5,7},{6,2},{7,5},{8,12},{9,11},{10,... | collective-permute-start | bytes 1376264 | tf_op jit(solution)/shard_map/ppermute | solution.py:40
  27.3 8.7 %collective-permute-start.7 = (bf16[64,3712]{1,0:T(8,128)(2,1)S(1)}, bf16[64,3712]{1,0:T(8,128)(2,1)S(1)}, u32[]{:S(2)}, u32[]{:S(2)}) collective-permute-start(bf16[64,3712]{1,0:T(8,128)(2,1)S(1)} %constant_dynamic-update-slice_fusion.x0), channel_id=1, source_target_pairs={{0,4},{1,3},{2,6},{3,1},{4,0},{5,7},{6,2},{7,5},{8,12},{9,11},{10,... | collective-permute-start | bytes 1425416 | tf_op jit(solution)/shard_map/ppermute | solution.py:40
  29.0 7.1 %collective-permute-start.12 = (bf16[64,3584]{1,0:T(8,128)(2,1)S(1)}, bf16[64,3584]{1,0:T(8,128)(2,1)S(1)}, u32[]{:S(2)}, u32[]{:S(2)}) collective-permute-start(bf16[64,3584]{1,0:T(8,128)(2,1)S(1)} %constant_dynamic-update-slice_fusion.1.x0), channel_id=1, source_target_pairs={{0,1},{1,0},{2,3},{3,2},{4,5},{5,4},{6,7},{7,6},{8,9},{9,8},{10,11... | collective-permute-start | bytes 1376264 | tf_op jit(solution)/shard_map/ppermute | solution.py:40
  30.8 5.3 %collective-permute-start.13 = (bf16[64,3584]{1,0:T(8,128)(2,1)S(1)}, bf16[64,3584]{1,0:T(8,128)(2,1)S(1)}, u32[]{:S(2)}, u32[]{:S(2)}) collective-permute-start(bf16[64,3584]{1,0:T(8,128)(2,1)S(1)} %collective-permute-done.11.x1), channel_id=1, source_target_pairs={{0,1},{1,0},{2,3},{3,2},{4,5},{5,4},{6,7},{7,6},{8,9},{9,8},{10,11... | collective-permute-start | bytes 1376264 | tf_op jit(solution)/shard_map/ppermute | solution.py:40
  30.8 9.2 %collective-permute-start.8 = (bf16[64,3712]{1,0:T(8,128)(2,1)S(1)}, bf16[64,3712]{1,0:T(8,128)(2,1)S(1)}, u32[]{:S(2)}, u32[]{:S(2)}) collective-permute-start(bf16[64,3712]{1,0:T(8,128)(2,1)S(1)} %constant_dynamic-update-slice_fusion.x0), channel_id=1, source_target_pairs={{0,1},{1,0},{2,3},{3,2},{4,5},{5,4},{6,7},{7,6},{8,9},{9,8},{10,11... | collective-permute-start | bytes 1425416 | tf_op jit(solution)/shard_map/ppermute | solution.py:40
  36.1 3.9 %collective-permute-start.9 = (bf16[64,3712]{1,0:T(8,128)(2,1)S(1)}, bf16[64,3712]{1,0:T(8,128)(2,1)S(1)}, u32[]{:S(2)}, u32[]{:S(2)}) collective-permute-start(bf16[64,3712]{1,0:T(8,128)(2,1)S(1)} %collective-permute-done.7.x1), channel_id=1, source_target_pairs={{0,1},{1,0},{2,3},{3,2},{4,5},{5,4},{6,7},{7,6},{8,9},{9,8},{10,11... | collective-permute-start | bytes 1425416 | tf_op jit(solution)/shard_map/ppermute | solution.py:40
  47.2 2.0 %collective-permute-start.15 = (bf16[64,3584]{1,0:T(8,128)(2,1)S(1)}, bf16[64,3584]{1,0:T(8,128)(2,1)S(1)}, u32[]{:S(2)}, u32[]{:S(2)}) collective-permute-start(bf16[64,3584]{1,0:T(8,128)(2,1)S(1)} %get-tuple-element.20), channel_id=1, source_target_pairs={{0,1},{1,0},{2,3},{3,2},{4,5},{5,4},{6,7},{7,6},{8,9},{9,8},{10,11... | collective-permute-start | bytes 1376264 | tf_op jit(solution)/shard_map/ppermute | solution.py:40
  47.8 5.1 %collective-permute-start.14 = (bf16[64,3584]{1,0:T(8,128)(2,1)S(1)}, bf16[64,3584]{1,0:T(8,128)(2,1)S(1)}, u32[]{:S(2)}, u32[]{:S(2)}) collective-permute-start(bf16[64,3584]{1,0:T(8,128)(2,1)S(1)} %get-tuple-element.18), channel_id=1, source_target_pairs={{0,1},{1,0},{2,3},{3,2},{4,5},{5,4},{6,7},{7,6},{8,9},{9,8},{10,11... | collective-permute-start | bytes 1376264 | tf_op jit(solution)/shard_map/ppermute | solution.py:40
  47.9 11.8 %collective-permute-start.21 = (bf16[64,3584]{1,0:T(8,128)(2,1)S(1)}, bf16[64,3584]{1,0:T(8,128)(2,1)S(1)}, u32[]{:S(2)}, u32[]{:S(2)}) collective-permute-start(bf16[64,3584]{1,0:T(8,128)(2,1)S(1)} %get-tuple-element.22), channel_id=1, source_target_pairs={{0,1},{1,0},{2,3},{3,2},{4,5},{5,4},{6,7},{7,6},{8,9},{9,8},{10,11... | collective-permute-start | bytes 1376264 | tf_op jit(solution)/shard_map/ppermute | solution.py:40
  48.3 2.9 %collective-permute-start.22 = (bf16[64,3584]{1,0:T(8,128)(2,1)S(1)}, bf16[64,3584]{1,0:T(8,128)(2,1)S(1)}, u32[]{:S(2)}, u32[]{:S(2)}) collective-permute-start(bf16[64,3584]{1,0:T(8,128)(2,1)S(1)} %get-tuple-element.24), channel_id=1, source_target_pairs={{0,1},{1,0},{2,3},{3,2},{4,5},{5,4},{6,7},{7,6},{8,9},{9,8},{10,11... | collective-permute-start | bytes 1376264 | tf_op jit(solution)/shard_map/ppermute | solution.py:40
  49.3 8.5 %collective-permute-start.16 = (bf16[64,3584]{1,0:T(8,128)(2,1)S(1)}, bf16[64,3584]{1,0:T(8,128)(2,1)S(1)}, u32[]{:S(2)}, u32[]{:S(2)}) collective-permute-start(bf16[64,3584]{1,0:T(8,128)(2,1)S(1)} %add_convert_fusion.1), channel_id=1, source_target_pairs={{0,4},{1,3},{2,6},{3,1},{4,0},{5,7},{6,2},{7,5},{8,12},{9,11},{10,... | collective-permute-start | bytes 1376264 | tf_op jit(solution)/shard_map/ppermute | solution.py:40
  51.3 13.9 %collective-permute-start.23 = (bf16[64,3584]{1,0:T(8,128)(2,1)S(1)}, bf16[64,3584]{1,0:T(8,128)(2,1)S(1)}, u32[]{:S(2)}, u32[]{:S(2)}) collective-permute-start(bf16[64,3584]{1,0:T(8,128)(2,1)S(1)} %add_convert_fusion), channel_id=1, source_target_pairs={{0,4},{1,3},{2,6},{3,1},{4,0},{5,7},{6,2},{7,5},{8,12},{9,11},{10,... | collective-permute-start | bytes 1376264 | tf_op jit(solution)/shard_map/ppermute | solution.py:40
  58.1 9.0 %collective-permute-start.17 = (bf16[32,3584]{1,0:T(8,128)(2,1)S(1)}, bf16[32,3584]{1,0:T(8,128)(2,1)S(1)}, u32[]{:S(2)}, u32[]{:S(2)}) collective-permute-start(bf16[32,3584]{1,0:T(8,128)(2,1)S(1)} %slice.127), channel_id=1, source_target_pairs={{0,2},{1,5},{2,0},{3,7},{4,6},{5,1},{6,4},{7,3},{8,10},{9,13},{10,... | collective-permute-start | bytes 688136 | tf_op jit(solution)/shard_map/ppermute | solution.py:40
  65.4 6.1 %collective-permute-start.24 = (bf16[32,3584]{1,0:T(8,128)(2,1)S(1)}, bf16[32,3584]{1,0:T(8,128)(2,1)S(1)}, u32[]{:S(2)}, u32[]{:S(2)}) collective-permute-start(bf16[32,3584]{1,0:T(8,128)(2,1)S(1)} %slice.126), channel_id=1, source_target_pairs={{0,2},{1,5},{2,0},{3,7},{4,6},{5,1},{6,4},{7,3},{8,10},{9,13},{10,... | collective-permute-start | bytes 688136 | tf_op jit(solution)/shard_map/ppermute | solution.py:40
  67.1 7.7 %collective-permute-start.18 = (bf16[8,3584]{1,0:T(8,128)(2,1)S(1)}, bf16[8,3584]{1,0:T(8,128)(2,1)S(1)}, u32[]{:S(2)}, u32[]{:S(2)}) collective-permute-start(bf16[8,3584]{1,0:T(8,128)(2,1)S(1)} %get-tuple-element.29), channel_id=1, source_target_pairs={{0,8},{1,9},{2,10},{3,11},{4,12},{5,13},{6,14},{7,15},{8,0},{9,1},... | collective-permute-start | bytes 172040 | tf_op jit(solution)/shard_map/ppermute | solution.py:40
  67.7 7.4 %collective-permute-start.20 = (bf16[8,3584]{1,0:T(8,128)(2,1)S(1)}, bf16[8,3584]{1,0:T(8,128)(2,1)S(1)}, u32[]{:S(2)}, u32[]{:S(2)}) collective-permute-start(bf16[8,3584]{1,0:T(8,128)(2,1)S(1)} %get-tuple-element.30), channel_id=1, source_target_pairs={{0,24},{1,25},{2,26},{3,27},{4,28},{5,29},{6,30},{7,31},{8,16},{9,... | collective-permute-start | bytes 172040 | tf_op jit(solution)/shard_map/ppermute | solution.py:40
  70.3 7.1 %collective-permute-start.19 = (bf16[8,3584]{1,0:T(8,128)(2,1)S(1)}, bf16[8,3584]{1,0:T(8,128)(2,1)S(1)}, u32[]{:S(2)}, u32[]{:S(2)}) collective-permute-start(bf16[8,3584]{1,0:T(8,128)(2,1)S(1)} %get-tuple-element.31), channel_id=1, source_target_pairs={{0,16},{1,17},{2,18},{3,19},{4,20},{5,21},{6,22},{7,23},{8,24},{9,... | collective-permute-start | bytes 172040 | tf_op jit(solution)/shard_map/ppermute | solution.py:40
  71.6 5.8 %collective-permute-start.25 = (bf16[8,3584]{1,0:T(8,128)(2,1)S(1)}, bf16[8,3584]{1,0:T(8,128)(2,1)S(1)}, u32[]{:S(2)}, u32[]{:S(2)}) collective-permute-start(bf16[8,3584]{1,0:T(8,128)(2,1)S(1)} %get-tuple-element.32), channel_id=1, source_target_pairs={{0,8},{1,9},{2,10},{3,11},{4,12},{5,13},{6,14},{7,15},{8,0},{9,1},... | collective-permute-start | bytes 172040 | tf_op jit(solution)/shard_map/ppermute | solution.py:40
  72.3 6.1 %collective-permute-start.27 = (bf16[8,3584]{1,0:T(8,128)(2,1)S(1)}, bf16[8,3584]{1,0:T(8,128)(2,1)S(1)}, u32[]{:S(2)}, u32[]{:S(2)}) collective-permute-start(bf16[8,3584]{1,0:T(8,128)(2,1)S(1)} %get-tuple-element.33), channel_id=1, source_target_pairs={{0,24},{1,25},{2,26},{3,27},{4,28},{5,29},{6,30},{7,31},{8,16},{9,... | collective-permute-start | bytes 172040 | tf_op jit(solution)/shard_map/ppermute | solution.py:40
  74.8 5.5 %collective-permute-start.26 = (bf16[8,3584]{1,0:T(8,128)(2,1)S(1)}, bf16[8,3584]{1,0:T(8,128)(2,1)S(1)}, u32[]{:S(2)}, u32[]{:S(2)}) collective-permute-start(bf16[8,3584]{1,0:T(8,128)(2,1)S(1)} %get-tuple-element.34), channel_id=1, source_target_pairs={{0,16},{1,17},{2,18},{3,19},{4,20},{5,21},{6,22},{7,23},{8,24},{9,... | collective-permute-start | bytes 172040 | tf_op jit(solution)/shard_map/ppermute | solution.py:40

commit v6 on v5

--- a/solution.py
+++ b/solution.py
@@ -12,7 +12,7 @@
 LANES = 128
 CUT = 7
 DOWN = 7
-AHEAD = 3
+AHEAD = 4
 FIRST = 5
 SECOND = 30
 WEIGHT = 20

time: 81.2 us -> 81.2 us (level)
  no operation moved by 1% of the time
where the time goes in v6:
time: 81.2 us; the launch traced here: 81 us
  waiting for transfers between devices  34.8 us (43%)
  starting transfers between devices  31.4 us (39%)
  Pallas kernels  11.1 us (14%)
  other arithmetic  2.27 us (3%)
  local copies, waits for them, and re-layouts  1.13 us (1%)
    ppermute x28, waiting for transfers between devices, move(): return lax.ppermute(x, AXES, perm)  34.8 us
    ppermute x28, starting transfers between devices, move(): return lax.ppermute(x, AXES, perm)  31.4 us
    pallas_call x1, Pallas kernels, second_part(): pl.pallas_call(functools.partial(second_kernel, skip, kb), in_specs=in_vm...  7.2 us
    pallas_call x1, Pallas kernels, first_part(): pl.pallas_call(functools.partial(first_kernel, 0, kb), in_specs=in_vmem(4...  3.9 us
  transfers between devices with their start and end apart: 28, of which 13 were waited for; matrix products, arithmetic and copies ran while one was open for 3% of the time, Pallas kernels for 5%

profile of v6, /device:TPU:0, one launch (start us, length us, event | category | flops | bytes accessed | tf_op | source)
XLA Modules:
  0.0 81.0 jit_solution(4761047869342842534)
XLA Ops:
  0.0 3.0 %collective-permute-start = (bf16[8,7168]{1,0:T(8,128)(2,1)}, bf16[8,7168]{1,0:T(8,128)(2,1)S(1)}, u32[]{:S(2)}, u32[]{:S(2)}) collective-permute-start(bf16[8,7168]{1,0:T(8,128)(2,1)} %param.6), channel_id=1, source_target_pairs={{0,8},{1,9},{2,10},{3,11},{4,12},{5,13},{6,14},{7,15},{8,0},{9,1},... | collective-permute-start | bytes 344072 | tf_op jit(solution)/shard_map/ppermute | solution.py:40
  3.0 2.6 %collective-permute-start.2 = (bf16[8,7168]{1,0:T(8,128)(2,1)}, bf16[8,7168]{1,0:T(8,128)(2,1)S(1)}, u32[]{:S(2)}, u32[]{:S(2)}) collective-permute-start(bf16[8,7168]{1,0:T(8,128)(2,1)} %param.6), channel_id=1, source_target_pairs={{0,16},{1,17},{2,18},{3,19},{4,20},{5,21},{6,22},{7,23},{8,24},{9,... | collective-permute-start | bytes 344072 | tf_op jit(solution)/shard_map/ppermute | solution.py:40
  5.6 0.9 %fusion.12 = (bf16[8,3584]{1,0:T(8,128)(2,1)S(1)}, bf16[64,3584]{1,0:T(8,128)(2,1)S(1)}, bf16[8,3584]{1,0:T(8,128)(2,1)S(1)}) fusion(bf16[8,7168]{1,0:T(8,128)(2,1)} %param.6), kind=kLoop, calls=%fused_computation.44 | loop fusion | bytes 286720 | tf_op jit(solution)/shard_map/slice | solution.py:54
  6.5 0.8 select_reduce_fusion
  7.5 4.0 %collective-permute-start.5 = (bf16[8,128]{1,0:T(8,128)(2,1)S(1)}, bf16[8,128]{1,0:T(8,128)(2,1)S(1)}, u32[]{:S(2)}, u32[]{:S(2)}) collective-permute-start(bf16[8,128]{1,0:T(8,128)(2,1)S(1)} %maximum_maximum_fusion.1), channel_id=1, source_target_pairs={{0,24},{1,25},{2,26},{3,27},{4,28},{5,29},{6,30},{7,31},{8,16},{9,... | collective-permute-start | bytes 6152 | tf_op jit(solution)/shard_map/ppermute | solution.py:40
  12.1 2.9 %collective-permute-done.2 = bf16[8,7168]{1,0:T(8,128)(2,1)S(1)} collective-permute-done((bf16[8,7168]{1,0:T(8,128)(2,1)}, bf16[8,7168]{1,0:T(8,128)(2,1)S(1)}, u32[]{:S(2)}, u32[]{:S(2)}) %collective-permute-start.2) | collective-permute-done | bytes 114720 | tf_op jit(solution)/shard_map/ppermute | solution.py:40
  15.1 1.6 %collective-permute-start.10 = (bf16[32,3584]{1,0:T(8,128)(2,1)S(1)}, bf16[32,3584]{1,0:T(8,128)(2,1)S(1)}, u32[]{:S(2)}, u32[]{:S(2)}) collective-permute-start(bf16[32,3584]{1,0:T(8,128)(2,1)S(1)} %pad_maximum_fusion), channel_id=1, source_target_pairs={{0,2},{1,5},{2,0},{3,7},{4,6},{5,1},{6,4},{7,3},{8,10},{9,13},{10,... | collective-permute-start | bytes 688136 | tf_op jit(solution)/shard_map/ppermute | solution.py:40
  16.8 1.2 %collective-permute-start.6 = (bf16[32,3712]{1,0:T(8,128)(2,1)S(1)}, bf16[32,3712]{1,0:T(8,128)(2,1)S(1)}, u32[]{:S(2)}, u32[]{:S(2)}) collective-permute-start(bf16[32,3712]{1,0:T(8,128)(2,1)S(1)} %maximum_maximum_fusion), channel_id=1, source_target_pairs={{0,2},{1,5},{2,0},{3,7},{4,6},{5,1},{6,4},{7,3},{8,10},{9,13},{10,... | collective-permute-start | bytes 712712 | tf_op jit(solution)/shard_map/ppermute | solution.py:40
  18.0 4.3 %collective-permute-done.10 = bf16[32,3584]{1,0:T(8,128)(2,1)S(1)} collective-permute-done((bf16[32,3584]{1,0:T(8,128)(2,1)S(1)}, bf16[32,3584]{1,0:T(8,128)(2,1)S(1)}, u32[]{:S(2)}, u32[]{:S(2)}) %collective-permute-start.10) | collective-permute-done | bytes 229408 | tf_op jit(solution)/shard_map/ppermute | solution.py:40
  22.2 1.6 %collective-permute-start.11 = (bf16[64,3584]{1,0:T(8,128)(2,1)S(1)}, bf16[64,3584]{1,0:T(8,128)(2,1)S(1)}, u32[]{:S(2)}, u32[]{:S(2)}) collective-permute-start(bf16[64,3584]{1,0:T(8,128)(2,1)S(1)} %constant_dynamic-update-slice_fusion.1.x0), channel_id=1, source_target_pairs={{0,4},{1,3},{2,6},{3,1},{4,0},{5,7},{6,2},{7,5},{8,12},{9,11},{10,... | collective-permute-start | bytes 1376264 | tf_op jit(solution)/shard_map/ppermute | solution.py:40
  23.9 3.4 %collective-permute-done.6 = bf16[32,3712]{1,0:T(8,128)(2,1)S(1)} collective-permute-done((bf16[32,3712]{1,0:T(8,128)(2,1)S(1)}, bf16[32,3712]{1,0:T(8,128)(2,1)S(1)}, u32[]{:S(2)}, u32[]{:S(2)}) %collective-permute-start.6) | collective-permute-done | bytes 237600 | tf_op jit(solution)/shard_map/ppermute | solution.py:40
  27.3 1.6 %collective-permute-start.7 = (bf16[64,3712]{1,0:T(8,128)(2,1)S(1)}, bf16[64,3712]{1,0:T(8,128)(2,1)S(1)}, u32[]{:S(2)}, u32[]{:S(2)}) collective-permute-start(bf16[64,3712]{1,0:T(8,128)(2,1)S(1)} %constant_dynamic-update-slice_fusion.x0), channel_id=1, source_target_pairs={{0,4},{1,3},{2,6},{3,1},{4,0},{5,7},{6,2},{7,5},{8,12},{9,11},{10,... | collective-permute-start | bytes 1425416 | tf_op jit(solution)/shard_map/ppermute | solution.py:40
  29.0 1.8 %collective-permute-done.11.x1 = bf16[64,3584]{1,0:T(8,128)(2,1)S(1)} collective-permute-done((bf16[64,3584]{1,0:T(8,128)(2,1)S(1)}, bf16[64,3584]{1,0:T(8,128)(2,1)S(1)}, u32[]{:S(2)}, u32[]{:S(2)}) %collective-permute-start.11) | collective-permute-done | bytes 458784 | tf_op jit(solution)/shard_map/ppermute | solution.py:40
  31.3 4.8 %collective-permute-done.7.x1 = bf16[64,3712]{1,0:T(8,128)(2,1)S(1)} collective-permute-done((bf16[64,3712]{1,0:T(8,128)(2,1)S(1)}, bf16[64,3712]{1,0:T(8,128)(2,1)S(1)}, u32[]{:S(2)}, u32[]{:S(2)}) %collective-permute-start.7) | collective-permute-done | bytes 475168 | tf_op jit(solution)/shard_map/ppermute | solution.py:40
  36.1 3.9 %shard_map.64.acc = f32[256,1024]{1,0:T(8,128)S(1)} custom-call(bf16[64,3584]{1,0:T(8,128)(2,1)S(1)} %constant_dynamic-update-slice_fusion.1.x0, bf16[64,3584]{1,0:T(8,128)(2,1)S(1)} %collective-permute-done.11.x1, bf16[64,3584]{1,0:T(8,128)(2,1)S(1)} %collective-permute-done.12.x2, bf16[64,3584]{1,0:T(8,128)(2,1)S(1)} %collective-permute-done.13.x3, ...), custom_call_target="tpu_custom_call" | custom-call | flops 37580963840 | bytes 146800640 | tf_op jit(solution)/shard_map/pallas_call | solution.py:198
  40.0 7.2 %shard_map.65 = (f32[64,3584]{1,0:T(8,128)S(1)}, f32[64,3584]{1,0:T(8,128)S(1)}, bf16[64,3584]{1,0:T(8,128)(2,1)S(1)}, bf16[64,3584]{1,0:T(8,128)(2,1)S(1)}, f32...) custom-call(bf16[64,3712]{1,0:T(8,128)(2,1)S(1)} %constant_dynamic-up, ...), custom_call_target="tpu_custom_call" | custom-call | flops 3758096384 | bytes 14680064 | tf_op jit(solution)/shard_map/pallas_call | solution.py:214
  48.4 0.9 %collective-permute-done.15 = bf16[64,3584]{1,0:T(8,128)(2,1)S(1)} collective-permute-done((bf16[64,3584]{1,0:T(8,128)(2,1)S(1)}, bf16[64,3584]{1,0:T(8,128)(2,1)S(1)}, u32[]{:S(2)}, u32[]{:S(2)}) %collective-permute-start.15) | collective-permute-done | bytes 458784 | tf_op jit(solution)/shard_map/ppermute | solution.py:40
  49.3 1.6 %collective-permute-start.16 = (bf16[64,3584]{1,0:T(8,128)(2,1)S(1)}, bf16[64,3584]{1,0:T(8,128)(2,1)S(1)}, u32[]{:S(2)}, u32[]{:S(2)}) collective-permute-start(bf16[64,3584]{1,0:T(8,128)(2,1)S(1)} %add_convert_fusion.1), channel_id=1, source_target_pairs={{0,4},{1,3},{2,6},{3,1},{4,0},{5,7},{6,2},{7,5},{8,12},{9,11},{10,... | collective-permute-start | bytes 1376264 | tf_op jit(solution)/shard_map/ppermute | solution.py:40
  51.3 1.6 %collective-permute-start.23 = (bf16[64,3584]{1,0:T(8,128)(2,1)S(1)}, bf16[64,3584]{1,0:T(8,128)(2,1)S(1)}, u32[]{:S(2)}, u32[]{:S(2)}) collective-permute-start(bf16[64,3584]{1,0:T(8,128)(2,1)S(1)} %add_convert_fusion), channel_id=1, source_target_pairs={{0,4},{1,3},{2,6},{3,1},{4,0},{5,7},{6,2},{7,5},{8,12},{9,11},{10,... | collective-permute-start | bytes 1376264 | tf_op jit(solution)/shard_map/ppermute | solution.py:40
  52.9 4.9 %collective-permute-done.16 = bf16[64,3584]{1,0:T(8,128)(2,1)S(1)} collective-permute-done((bf16[64,3584]{1,0:T(8,128)(2,1)S(1)}, bf16[64,3584]{1,0:T(8,128)(2,1)S(1)}, u32[]{:S(2)}, u32[]{:S(2)}) %collective-permute-start.16) | collective-permute-done | bytes 458784 | tf_op jit(solution)/shard_map/ppermute | solution.py:40
  58.1 1.6 %collective-permute-start.17 = (bf16[32,3584]{1,0:T(8,128)(2,1)S(1)}, bf16[32,3584]{1,0:T(8,128)(2,1)S(1)}, u32[]{:S(2)}, u32[]{:S(2)}) collective-permute-start(bf16[32,3584]{1,0:T(8,128)(2,1)S(1)} %slice.127), channel_id=1, source_target_pairs={{0,2},{1,5},{2,0},{3,7},{4,6},{5,1},{6,4},{7,3},{8,10},{9,13},{10,... | collective-permute-start | bytes 688136 | tf_op jit(solution)/shard_map/ppermute | solution.py:40
  59.7 5.6 %collective-permute-done.23 = bf16[64,3584]{1,0:T(8,128)(2,1)S(1)} collective-permute-done((bf16[64,3584]{1,0:T(8,128)(2,1)S(1)}, bf16[64,3584]{1,0:T(8,128)(2,1)S(1)}, u32[]{:S(2)}, u32[]{:S(2)}) %collective-permute-start.23) | collective-permute-done | bytes 458784 | tf_op jit(solution)/shard_map/ppermute | solution.py:40
  65.4 1.6 %collective-permute-start.24 = (bf16[32,3584]{1,0:T(8,128)(2,1)S(1)}, bf16[32,3584]{1,0:T(8,128)(2,1)S(1)}, u32[]{:S(2)}, u32[]{:S(2)}) collective-permute-start(bf16[32,3584]{1,0:T(8,128)(2,1)S(1)} %slice.126), channel_id=1, source_target_pairs={{0,2},{1,5},{2,0},{3,7},{4,6},{5,1},{6,4},{7,3},{8,10},{9,13},{10,... | collective-permute-start | bytes 688136 | tf_op jit(solution)/shard_map/ppermute | solution.py:40
  67.1 0.6 collective-permute-start.18
  67.7 2.5 %collective-permute-start.20 = (bf16[8,3584]{1,0:T(8,128)(2,1)S(1)}, bf16[8,3584]{1,0:T(8,128)(2,1)S(1)}, u32[]{:S(2)}, u32[]{:S(2)}) collective-permute-start(bf16[8,3584]{1,0:T(8,128)(2,1)S(1)} %get-tuple-element.30), channel_id=1, source_target_pairs={{0,24},{1,25},{2,26},{3,27},{4,28},{5,29},{6,30},{7,31},{8,16},{9,... | collective-permute-start | bytes 172040 | tf_op jit(solution)/shard_map/ppermute | solution.py:40
  70.7 0.9 %collective-permute-done.24 = bf16[32,3584]{1,0:T(8,128)(2,1)S(1)} collective-permute-done((bf16[32,3584]{1,0:T(8,128)(2,1)S(1)}, bf16[32,3584]{1,0:T(8,128)(2,1)S(1)}, u32[]{:S(2)}, u32[]{:S(2)}) %collective-permute-start.24) | collective-permute-done | bytes 229408 | tf_op jit(solution)/shard_map/ppermute | solution.py:40
  71.6 0.7 collective-permute-start.25
  72.3 2.5 %collective-permute-start.27 = (bf16[8,3584]{1,0:T(8,128)(2,1)S(1)}, bf16[8,3584]{1,0:T(8,128)(2,1)S(1)}, u32[]{:S(2)}, u32[]{:S(2)}) collective-permute-start(bf16[8,3584]{1,0:T(8,128)(2,1)S(1)} %get-tuple-element.33), channel_id=1, source_target_pairs={{0,24},{1,25},{2,26},{3,27},{4,28},{5,29},{6,30},{7,31},{8,16},{9,... | collective-permute-start | bytes 172040 | tf_op jit(solution)/shard_map/ppermute | solution.py:40
  75.2 2.2 %collective-permute-done.19 = bf16[8,3584]{1,0:T(8,128)(2,1)S(1)} collective-permute-done((bf16[8,3584]{1,0:T(8,128)(2,1)S(1)}, bf16[8,3584]{1,0:T(8,128)(2,1)S(1)}, u32[]{:S(2)}, u32[]{:S(2)}) %collective-permute-start.19) | collective-permute-done | bytes 57376 | tf_op jit(solution)/shard_map/ppermute | solution.py:40
  77.4 1.0 %collective-permute-done.27 = bf16[8,3584]{1,0:T(8,128)(2,1)S(1)} collective-permute-done((bf16[8,3584]{1,0:T(8,128)(2,1)S(1)}, bf16[8,3584]{1,0:T(8,128)(2,1)S(1)}, u32[]{:S(2)}, u32[]{:S(2)}) %collective-permute-start.27) | collective-permute-done | bytes 57376 | tf_op jit(solution)/shard_map/ppermute | solution.py:40
  78.3 1.9 %collective-permute-done.26 = bf16[8,3584]{1,0:T(8,128)(2,1)S(1)} collective-permute-done((bf16[8,3584]{1,0:T(8,128)(2,1)S(1)}, bf16[8,3584]{1,0:T(8,128)(2,1)S(1)}, u32[]{:S(2)}, u32[]{:S(2)}) %collective-permute-start.26) | collective-permute-done | bytes 57376 | tf_op jit(solution)/shard_map/ppermute | solution.py:40
  80.3 0.7 pad_maximum_fusion.1
  (57 shorter events, 4.3 us)
Async XLA Ops:
  0.0 7.5 %collective-permute-start = (bf16[8,7168]{1,0:T(8,128)(2,1)}, bf16[8,7168]{1,0:T(8,128)(2,1)S(1)}, u32[]{:S(2)}, u32[]{:S(2)}) collective-permute-start(bf16[8,7168]{1,0:T(8,128)(2,1)} %param.6), channel_id=1, source_target_pairs={{0,8},{1,9},{2,10},{3,11},{4,12},{5,13},{6,14},{7,15},{8,0},{9,1},... | collective-permute-start | bytes 344072 | tf_op jit(solution)/shard_map/ppermute | solution.py:40
  3.0 12.0 %collective-permute-start.2 = (bf16[8,7168]{1,0:T(8,128)(2,1)}, bf16[8,7168]{1,0:T(8,128)(2,1)S(1)}, u32[]{:S(2)}, u32[]{:S(2)}) collective-permute-start(bf16[8,7168]{1,0:T(8,128)(2,1)} %param.6), channel_id=1, source_target_pairs={{0,16},{1,17},{2,18},{3,19},{4,20},{5,21},{6,22},{7,23},{8,24},{9,... | collective-permute-start | bytes 344072 | tf_op jit(solution)/shard_map/ppermute | solution.py:40
  5.6 9.5 %collective-permute-start.4 = (bf16[8,7168]{1,0:T(8,128)(2,1)}, bf16[8,7168]{1,0:T(8,128)(2,1)S(1)}, u32[]{:S(2)}, u32[]{:S(2)}) collective-permute-start(bf16[8,7168]{1,0:T(8,128)(2,1)} %param.6), channel_id=1, source_target_pairs={{0,24},{1,25},{2,26},{3,27},{4,28},{5,29},{6,30},{7,31},{8,16},{9,... | collective-permute-start | bytes 344072 | tf_op jit(solution)/shard_map/ppermute | solution.py:40
  7.5 9.2 %collective-permute-start.5 = (bf16[8,128]{1,0:T(8,128)(2,1)S(1)}, bf16[8,128]{1,0:T(8,128)(2,1)S(1)}, u32[]{:S(2)}, u32[]{:S(2)}) collective-permute-start(bf16[8,128]{1,0:T(8,128)(2,1)S(1)} %maximum_maximum_fusion.1), channel_id=1, source_target_pairs={{0,24},{1,25},{2,26},{3,27},{4,28},{5,29},{6,30},{7,31},{8,16},{9,... | collective-permute-start | bytes 6152 | tf_op jit(solution)/shard_map/ppermute | solution.py:40
  11.5 5.2 %collective-permute-start.3 = (bf16[8,128]{1,0:T(8,128)(2,1)S(1)}, bf16[8,128]{1,0:T(8,128)(2,1)S(1)}, u32[]{:S(2)}, u32[]{:S(2)}) collective-permute-start(bf16[8,128]{1,0:T(8,128)(2,1)S(1)} %maximum_maximum_fusion.1), channel_id=1, source_target_pairs={{0,16},{1,17},{2,18},{3,19},{4,20},{5,21},{6,22},{7,23},{8,24},{9,... | collective-permute-start | bytes 6152 | tf_op jit(solution)/shard_map/ppermute | solution.py:40
  11.5 5.2 %collective-permute-start.1 = (bf16[8,128]{1,0:T(8,128)(2,1)S(1)}, bf16[8,128]{1,0:T(8,128)(2,1)S(1)}, u32[]{:S(2)}, u32[]{:S(2)}) collective-permute-start(bf16[8,128]{1,0:T(8,128)(2,1)S(1)} %maximum_maximum_fusion.1), channel_id=1, source_target_pairs={{0,8},{1,9},{2,10},{3,11},{4,12},{5,13},{6,14},{7,15},{8,0},{9,1},... | collective-permute-start | bytes 6152 | tf_op jit(solution)/shard_map/ppermute | solution.py:40
  15.1 7.1 %collective-permute-start.10 = (bf16[32,3584]{1,0:T(8,128)(2,1)S(1)}, bf16[32,3584]{1,0:T(8,128)(2,1)S(1)}, u32[]{:S(2)}, u32[]{:S(2)}) collective-permute-start(bf16[32,3584]{1,0:T(8,128)(2,1)S(1)} %pad_maximum_fusion), channel_id=1, source_target_pairs={{0,2},{1,5},{2,0},{3,7},{4,6},{5,1},{6,4},{7,3},{8,10},{9,13},{10,... | collective-permute-start | bytes 688136 | tf_op jit(solution)/shard_map/ppermute | solution.py:40
  16.8 10.6 %collective-permute-start.6 = (bf16[32,3712]{1,0:T(8,128)(2,1)S(1)}, bf16[32,3712]{1,0:T(8,128)(2,1)S(1)}, u32[]{:S(2)}, u32[]{:S(2)}) collective-permute-start(bf16[32,3712]{1,0:T(8,128)(2,1)S(1)} %maximum_maximum_fusion), channel_id=1, source_target_pairs={{0,2},{1,5},{2,0},{3,7},{4,6},{5,1},{6,4},{7,3},{8,10},{9,13},{10,... | collective-permute-start | bytes 712712 | tf_op jit(solution)/shard_map/ppermute | solution.py:40
  22.2 8.5 %collective-permute-start.11 = (bf16[64,3584]{1,0:T(8,128)(2,1)S(1)}, bf16[64,3584]{1,0:T(8,128)(2,1)S(1)}, u32[]{:S(2)}, u32[]{:S(2)}) collective-permute-start(bf16[64,3584]{1,0:T(8,128)(2,1)S(1)} %constant_dynamic-update-slice_fusion.1.x0), channel_id=1, source_target_pairs={{0,4},{1,3},{2,6},{3,1},{4,0},{5,7},{6,2},{7,5},{8,12},{9,11},{10,... | collective-permute-start | bytes 1376264 | tf_op jit(solution)/shard_map/ppermute | solution.py:40
  27.3 8.7 %collective-permute-start.7 = (bf16[64,3712]{1,0:T(8,128)(2,1)S(1)}, bf16[64,3712]{1,0:T(8,128)(2,1)S(1)}, u32[]{:S(2)}, u32[]{:S(2)}) collective-permute-start(bf16[64,3712]{1,0:T(8,128)(2,1)S(1)} %constant_dynamic-update-slice_fusion.x0), channel_id=1, source_target_pairs={{0,4},{1,3},{2,6},{3,1},{4,0},{5,7},{6,2},{7,5},{8,12},{9,11},{10,... | collective-permute-start | bytes 1425416 | tf_op jit(solution)/shard_map/ppermute | solution.py:40
  29.0 7.1 %collective-permute-start.12 = (bf16[64,3584]{1,0:T(8,128)(2,1)S(1)}, bf16[64,3584]{1,0:T(8,128)(2,1)S(1)}, u32[]{:S(2)}, u32[]{:S(2)}) collective-permute-start(bf16[64,3584]{1,0:T(8,128)(2,1)S(1)} %constant_dynamic-update-slice_fusion.1.x0), channel_id=1, source_target_pairs={{0,1},{1,0},{2,3},{3,2},{4,5},{5,4},{6,7},{7,6},{8,9},{9,8},{10,11... | collective-permute-start | bytes 1376264 | tf_op jit(solution)/shard_map/ppermute | solution.py:40
  30.8 5.3 %collective-permute-start.13 = (bf16[64,3584]{1,0:T(8,128)(2,1)S(1)}, bf16[64,3584]{1,0:T(8,128)(2,1)S(1)}, u32[]{:S(2)}, u32[]{:S(2)}) collective-permute-start(bf16[64,3584]{1,0:T(8,128)(2,1)S(1)} %collective-permute-done.11.x1), channel_id=1, source_target_pairs={{0,1},{1,0},{2,3},{3,2},{4,5},{5,4},{6,7},{7,6},{8,9},{9,8},{10,11... | collective-permute-start | bytes 1376264 | tf_op jit(solution)/shard_map/ppermute | solution.py:40
  30.8 9.2 %collective-permute-start.8 = (bf16[64,3712]{1,0:T(8,128)(2,1)S(1)}, bf16[64,3712]{1,0:T(8,128)(2,1)S(1)}, u32[]{:S(2)}, u32[]{:S(2)}) collective-permute-start(bf16[64,3712]{1,0:T(8,128)(2,1)S(1)} %constant_dynamic-update-slice_fusion.x0), channel_id=1, source_target_pairs={{0,1},{1,0},{2,3},{3,2},{4,5},{5,4},{6,7},{7,6},{8,9},{9,8},{10,11... | collective-permute-start | bytes 1425416 | tf_op jit(solution)/shard_map/ppermute | solution.py:40
  36.1 3.9 %collective-permute-start.9 = (bf16[64,3712]{1,0:T(8,128)(2,1)S(1)}, bf16[64,3712]{1,0:T(8,128)(2,1)S(1)}, u32[]{:S(2)}, u32[]{:S(2)}) collective-permute-start(bf16[64,3712]{1,0:T(8,128)(2,1)S(1)} %collective-permute-done.7.x1), channel_id=1, source_target_pairs={{0,1},{1,0},{2,3},{3,2},{4,5},{5,4},{6,7},{7,6},{8,9},{9,8},{10,11... | collective-permute-start | bytes 1425416 | tf_op jit(solution)/shard_map/ppermute | solution.py:40
  47.2 2.0 %collective-permute-start.15 = (bf16[64,3584]{1,0:T(8,128)(2,1)S(1)}, bf16[64,3584]{1,0:T(8,128)(2,1)S(1)}, u32[]{:S(2)}, u32[]{:S(2)}) collective-permute-start(bf16[64,3584]{1,0:T(8,128)(2,1)S(1)} %get-tuple-element.20), channel_id=1, source_target_pairs={{0,1},{1,0},{2,3},{3,2},{4,5},{5,4},{6,7},{7,6},{8,9},{9,8},{10,11... | collective-permute-start | bytes 1376264 | tf_op jit(solution)/shard_map/ppermute | solution.py:40
  47.8 5.2 %collective-permute-start.14 = (bf16[64,3584]{1,0:T(8,128)(2,1)S(1)}, bf16[64,3584]{1,0:T(8,128)(2,1)S(1)}, u32[]{:S(2)}, u32[]{:S(2)}) collective-permute-start(bf16[64,3584]{1,0:T(8,128)(2,1)S(1)} %get-tuple-element.18), channel_id=1, source_target_pairs={{0,1},{1,0},{2,3},{3,2},{4,5},{5,4},{6,7},{7,6},{8,9},{9,8},{10,11... | collective-permute-start | bytes 1376264 | tf_op jit(solution)/shard_map/ppermute | solution.py:40
  47.9 11.8 %collective-permute-start.21 = (bf16[64,3584]{1,0:T(8,128)(2,1)S(1)}, bf16[64,3584]{1,0:T(8,128)(2,1)S(1)}, u32[]{:S(2)}, u32[]{:S(2)}) collective-permute-start(bf16[64,3584]{1,0:T(8,128)(2,1)S(1)} %get-tuple-element.22), channel_id=1, source_target_pairs={{0,1},{1,0},{2,3},{3,2},{4,5},{5,4},{6,7},{7,6},{8,9},{9,8},{10,11... | collective-permute-start | bytes 1376264 | tf_op jit(solution)/shard_map/ppermute | solution.py:40
  48.3 2.9 %collective-permute-start.22 = (bf16[64,3584]{1,0:T(8,128)(2,1)S(1)}, bf16[64,3584]{1,0:T(8,128)(2,1)S(1)}, u32[]{:S(2)}, u32[]{:S(2)}) collective-permute-start(bf16[64,3584]{1,0:T(8,128)(2,1)S(1)} %get-tuple-element.24), channel_id=1, source_target_pairs={{0,1},{1,0},{2,3},{3,2},{4,5},{5,4},{6,7},{7,6},{8,9},{9,8},{10,11... | collective-permute-start | bytes 1376264 | tf_op jit(solution)/shard_map/ppermute | solution.py:40
  49.3 8.5 %collective-permute-start.16 = (bf16[64,3584]{1,0:T(8,128)(2,1)S(1)}, bf16[64,3584]{1,0:T(8,128)(2,1)S(1)}, u32[]{:S(2)}, u32[]{:S(2)}) collective-permute-start(bf16[64,3584]{1,0:T(8,128)(2,1)S(1)} %add_convert_fusion.1), channel_id=1, source_target_pairs={{0,4},{1,3},{2,6},{3,1},{4,0},{5,7},{6,2},{7,5},{8,12},{9,11},{10,... | collective-permute-start | bytes 1376264 | tf_op jit(solution)/shard_map/ppermute | solution.py:40
  51.3 13.9 %collective-permute-start.23 = (bf16[64,3584]{1,0:T(8,128)(2,1)S(1)}, bf16[64,3584]{1,0:T(8,128)(2,1)S(1)}, u32[]{:S(2)}, u32[]{:S(2)}) collective-permute-start(bf16[64,3584]{1,0:T(8,128)(2,1)S(1)} %add_convert_fusion), channel_id=1, source_target_pairs={{0,4},{1,3},{2,6},{3,1},{4,0},{5,7},{6,2},{7,5},{8,12},{9,11},{10,... | collective-permute-start | bytes 1376264 | tf_op jit(solution)/shard_map/ppermute | solution.py:40
  58.1 9.0 %collective-permute-start.17 = (bf16[32,3584]{1,0:T(8,128)(2,1)S(1)}, bf16[32,3584]{1,0:T(8,128)(2,1)S(1)}, u32[]{:S(2)}, u32[]{:S(2)}) collective-permute-start(bf16[32,3584]{1,0:T(8,128)(2,1)S(1)} %slice.127), channel_id=1, source_target_pairs={{0,2},{1,5},{2,0},{3,7},{4,6},{5,1},{6,4},{7,3},{8,10},{9,13},{10,... | collective-permute-start | bytes 688136 | tf_op jit(solution)/shard_map/ppermute | solution.py:40
  65.4 6.1 %collective-permute-start.24 = (bf16[32,3584]{1,0:T(8,128)(2,1)S(1)}, bf16[32,3584]{1,0:T(8,128)(2,1)S(1)}, u32[]{:S(2)}, u32[]{:S(2)}) collective-permute-start(bf16[32,3584]{1,0:T(8,128)(2,1)S(1)} %slice.126), channel_id=1, source_target_pairs={{0,2},{1,5},{2,0},{3,7},{4,6},{5,1},{6,4},{7,3},{8,10},{9,13},{10,... | collective-permute-start | bytes 688136 | tf_op jit(solution)/shard_map/ppermute | solution.py:40
  67.1 7.7 %collective-permute-start.18 = (bf16[8,3584]{1,0:T(8,128)(2,1)S(1)}, bf16[8,3584]{1,0:T(8,128)(2,1)S(1)}, u32[]{:S(2)}, u32[]{:S(2)}) collective-permute-start(bf16[8,3584]{1,0:T(8,128)(2,1)S(1)} %get-tuple-element.29), channel_id=1, source_target_pairs={{0,8},{1,9},{2,10},{3,11},{4,12},{5,13},{6,14},{7,15},{8,0},{9,1},... | collective-permute-start | bytes 172040 | tf_op jit(solution)/shard_map/ppermute | solution.py:40
  67.7 7.4 %collective-permute-start.20 = (bf16[8,3584]{1,0:T(8,128)(2,1)S(1)}, bf16[8,3584]{1,0:T(8,128)(2,1)S(1)}, u32[]{:S(2)}, u32[]{:S(2)}) collective-permute-start(bf16[8,3584]{1,0:T(8,128)(2,1)S(1)} %get-tuple-element.30), channel_id=1, source_target_pairs={{0,24},{1,25},{2,26},{3,27},{4,28},{5,29},{6,30},{7,31},{8,16},{9,... | collective-permute-start | bytes 172040 | tf_op jit(solution)/shard_map/ppermute | solution.py:40
  70.3 7.1 %collective-permute-start.19 = (bf16[8,3584]{1,0:T(8,128)(2,1)S(1)}, bf16[8,3584]{1,0:T(8,128)(2,1)S(1)}, u32[]{:S(2)}, u32[]{:S(2)}) collective-permute-start(bf16[8,3584]{1,0:T(8,128)(2,1)S(1)} %get-tuple-element.31), channel_id=1, source_target_pairs={{0,16},{1,17},{2,18},{3,19},{4,20},{5,21},{6,22},{7,23},{8,24},{9,... | collective-permute-start | bytes 172040 | tf_op jit(solution)/shard_map/ppermute | solution.py:40
  71.6 5.8 %collective-permute-start.25 = (bf16[8,3584]{1,0:T(8,128)(2,1)S(1)}, bf16[8,3584]{1,0:T(8,128)(2,1)S(1)}, u32[]{:S(2)}, u32[]{:S(2)}) collective-permute-start(bf16[8,3584]{1,0:T(8,128)(2,1)S(1)} %get-tuple-element.32), channel_id=1, source_target_pairs={{0,8},{1,9},{2,10},{3,11},{4,12},{5,13},{6,14},{7,15},{8,0},{9,1},... | collective-permute-start | bytes 172040 | tf_op jit(solution)/shard_map/ppermute | solution.py:40
  72.3 6.1 %collective-permute-start.27 = (bf16[8,3584]{1,0:T(8,128)(2,1)S(1)}, bf16[8,3584]{1,0:T(8,128)(2,1)S(1)}, u32[]{:S(2)}, u32[]{:S(2)}) collective-permute-start(bf16[8,3584]{1,0:T(8,128)(2,1)S(1)} %get-tuple-element.33), channel_id=1, source_target_pairs={{0,24},{1,25},{2,26},{3,27},{4,28},{5,29},{6,30},{7,31},{8,16},{9,... | collective-permute-start | bytes 172040 | tf_op jit(solution)/shard_map/ppermute | solution.py:40
  74.8 5.5 %collective-permute-start.26 = (bf16[8,3584]{1,0:T(8,128)(2,1)S(1)}, bf16[8,3584]{1,0:T(8,128)(2,1)S(1)}, u32[]{:S(2)}, u32[]{:S(2)}) collective-permute-start(bf16[8,3584]{1,0:T(8,128)(2,1)S(1)} %get-tuple-element.34), channel_id=1, source_target_pairs={{0,16},{1,17},{2,18},{3,19},{4,20},{5,21},{6,22},{7,23},{8,24},{9,... | collective-permute-start | bytes 172040 | tf_op jit(solution)/shard_map/ppermute | solution.py:40
